TPU v7x, 256 devices: a whole 4x4x8 slice. The times are simulated.
256 devices in a mesh: dp: 8 (over z_lo, y), tensor: 32 (over x, z_hi, core).
Axes of the slice: x: 4, y: 4, z: 8 (z_hi: 4, z_lo: 2; z = z_hi * 2 + z_lo), core: 2. Of those that a mesh axis runs over, the one named last changes fastest.
Arguments:
- tokens: bfloat16 [2048, 10240], P(('dp', 'tensor')), may hold values from -24 to 24
- cotangent: bfloat16 [2048, 10240], P('dp', 'tensor'), may hold values from -0.59765625 to 0.59765625
- old_weight: bfloat16 [5120, 5120], P('tensor'), may hold values from -0.078125 to 0.078125
- old_first: float32 [5120, 5120], P('tensor'), may hold values from -6 to 6
- old_second: float32 [5120, 5120], P('tensor'), may hold values from 0.25 to 4
- row_source: int32 [5120], replicated, may hold values from 0 to 5119
- col_source: int32 [5120], replicated, may hold values from 0 to 5119
- row_level: int32 [5120], replicated, may hold values from 0 to 4
- col_level: int32 [5120], replicated, may hold values from 0 to 4
Outputs:
- activation: bfloat16 [2048, 10240], P('dp', 'tensor')
- new_weight: bfloat16 [10240, 10240], P('dp', 'tensor')
- new_first: float32 [10240, 10240], P('dp', 'tensor')
- new_second: float32 [10240, 10240], P('dp', 'tensor')
All inputs are finite; a program needn't handle non-finite values.
Results may differ from a plain program's by a relative error of at most 0.014.
Values may be sent and summed in bfloat16 or wider, within the bound.
No kernel may reach another device: no remote copies, remote signals or barrier semaphores. Data moves between devices by JAX's collectives and lax.ppermute only.
A program may use at most 128 MiB of HBM per device.

v0:
```python
import jax
import jax.numpy as jnp
from jax import lax
from jax.sharding import PartitionSpec as P

beta_one = 0.9
beta_two = 0.95
adam_eps = 1e-08
learn_rate = 0.01
weight_decay = 0.1
adam_step = 1000.0


def growth_maps(row_source, col_source, row_level, col_level, old_width):
    identity = jnp.arange(old_width, dtype=jnp.int32)
    row_map = jnp.concatenate([identity, row_source])
    col_map = jnp.concatenate([identity, col_source])
    unit_scale = jnp.ones((old_width,), jnp.float32)
    row_scale = jnp.concatenate([unit_scale, (row_level.astype(jnp.float32) + 1.0) / 5.0])
    col_scale = jnp.concatenate([unit_scale, (col_level.astype(jnp.float32) + 1.0) / 5.0])
    return (row_map, col_map, row_scale, col_scale)


def activate(values):
    return jax.nn.gelu(values, approximate=True)


def adam_update(weight_rows, first_moment, second_moment, gradient):
    weight_float = weight_rows.astype(jnp.float32)
    new_first = beta_one * first_moment + (1.0 - beta_one) * gradient
    new_second = beta_two * second_moment + (1.0 - beta_two) * gradient * gradient
    first_corr = 1.0 - beta_one**adam_step
    second_corr = 1.0 - beta_two**adam_step
    update = (
        new_first / first_corr / (jnp.sqrt(new_second / second_corr) + adam_eps)
        + weight_decay * weight_float
    )
    new_weight = (weight_float - learn_rate * update).astype(jnp.bfloat16)
    return (new_weight, new_first, new_second)


def shards(
    tokens,
    cotangent,
    old_weight,
    old_first,
    old_second,
    row_source,
    col_source,
    row_level,
    col_level,
):
    tensor_count = lax.axis_size("tensor")
    group_count = lax.axis_size("dp")
    local_rows, old_width = old_weight.shape
    new_width = old_width + row_source.shape[0]
    slab_width = new_width // tensor_count
    block_rows = new_width // group_count
    row_map, col_map, row_scale, col_scale = growth_maps(
        row_source, col_source, row_level, col_level, old_width
    )
    slab_start = lax.axis_index("tensor") * slab_width
    block_start = lax.axis_index("dp") * block_rows
    slab_scale = lax.dynamic_slice_in_dim(col_scale, slab_start, slab_width)
    wide_weight = jnp.take(old_weight, col_map, axis=1)
    rows_weight = lax.all_to_all(wide_weight, "tensor", split_axis=1, concat_axis=0, tiled=True)
    wide_first = jnp.take(old_first, col_map, axis=1)
    wide_second = jnp.take(old_second, col_map, axis=1)
    rows_first, rows_second = (
        lax.all_to_all(
            wide_first.astype(jnp.bfloat16), "tensor", split_axis=1, concat_axis=0, tiled=True
        ).astype(wide_first.dtype),
        lax.all_to_all(
            wide_second.astype(jnp.bfloat16), "tensor", split_axis=1, concat_axis=0, tiled=True
        ).astype(wide_second.dtype),
    )
    copied = jnp.take(rows_weight, row_map, axis=0)
    grown_weight = (copied.astype(jnp.float32) * row_scale[:, None] * slab_scale[None, :]).astype(
        jnp.bfloat16
    )
    block_position = lax.dynamic_slice_in_dim(row_map, block_start, block_rows)
    grown_first = jnp.take(rows_first, block_position, axis=0)
    grown_second = jnp.take(rows_second, block_position, axis=0)
    all_tokens = lax.all_gather(tokens, "tensor", axis=0, tiled=True)
    hidden = jnp.dot(all_tokens, grown_weight, preferred_element_type=jnp.float32)
    activation = activate(hidden).astype(jnp.bfloat16)
    _, pullback = jax.vjp(activate, hidden)
    hidden_grad = pullback(cotangent.astype(jnp.float32))[0].astype(jnp.bfloat16)
    gradient = lax.psum_scatter(
        lax.dot_general(
            all_tokens, hidden_grad, (((0,), (0,)), ((), ())), preferred_element_type=jnp.float32
        ).astype(jnp.bfloat16),
        "dp",
        scatter_dimension=0,
        tiled=True,
    ).astype(jnp.float32)
    weight_block = lax.dynamic_slice_in_dim(grown_weight, block_start, block_rows, 0)
    new_weight, new_first, new_second = adam_update(
        weight_block, grown_first, grown_second, gradient
    )
    return (activation, new_weight, new_first, new_second)


def solution(mesh):
    placed = (
        P(("dp", "tensor"), None),
        P("dp", "tensor"),
        P("tensor", None),
        P("tensor", None),
        P("tensor", None),
        P(),
        P(),
        P(),
        P(),
    )
    return jax.shard_map(
        shards,
        mesh=mesh,
        in_specs=placed,
        out_specs=(P("dp", "tensor"), P("dp", "tensor"), P("dp", "tensor"), P("dp", "tensor")),
        check_vma=False,
    )
```

profile of v0, /device:TPU:1, one launch (start us, length us, event | category | flops | bytes accessed | tf_op | source)
XLA Modules:
  0.0 525.7 jit_solution(3105196090899026551)
XLA Ops:
  7.2 0.7 all-gather.2.cloned.1.call-update
  7.9 0.8 compare_select_fusion
  8.7 0.8 concatenate.77
  9.5 3.0 copy.31
  12.6 41.1 %gather_fusion = bf16[10240,160]{1,0:T(8,128)(2,1)} fusion(bf16[160,5120]{0,1:T(8,128)(2,1)S(1)} %copy.31, s32[10240]{0:T(1024)S(1)} %broadcast_clamp_fusion.1), kind=kCustom, calls=%fused_computation.4 | custom fusion | bytes 6594560 | tf_op jit(solution)/shard_map/jit(_take)/gather | solution.py:65
  53.7 7.6 %copy.32 = bf16[160,32,320]{2,0,1:T(8,128)(2,1)} copy(bf16[160,32,320]{0,2,1:T(8,128)(2,1)} %bitcast.33) | data formatting | bytes 6553600 | tf_op jit(solution)/shard_map/jit(_take)/gather | solution.py:65
  61.3 4.5 broadcast_select_fusion
  65.9 12.7 %all-to-all-start = ((bf16[160,32,320]{2,0,1:T(8,128)(2,1)}), bf16[160,32,320]{2,0,1:T(8,128)(2,1)}, u32[]{:S(2)}, u32[]{:S(2)}) async-start(bf16[160,32,320]{2,0,1:T(8,128)(2,1)} %broadcast_select_fusion), calls=%async_computation | async-start | bytes 7864320 | tf_op jit(solution)/shard_map/all_to_all | solution.py:66
  78.8 2.7 copy.34
  81.5 3.4 copy.37
  85.0 40.7 %gather_fusion.2 = bf16[10240,160]{1,0:T(8,128)(2,1)} fusion(bf16[160,5120]{0,1:T(8,128)(2,1)} %copy.34, s32[10240]{0:T(1024)S(1)} %fusion.23), kind=kCustom, calls=%fused_computation.clone | custom fusion | bytes 6594560 | tf_op jit(solution)/shard_map/jit(_take)/gather | solution.py:67
  125.7 41.1 %gather_fusion.4 = bf16[10240,160]{1,0:T(8,128)(2,1)} fusion(bf16[160,5120]{0,1:T(8,128)(2,1)S(1)} %copy.37, s32[10240]{0:T(1024)S(1)} %fusion.23), kind=kCustom, calls=%fused_computation.2.clone | custom fusion | bytes 6594560 | tf_op jit(solution)/shard_map/jit(_take)/gather | solution.py:68
  167.0 0.8 all-to-all-done
  167.8 43.1 %gather_fusion.1 = bf16[10240,320]{1,0:T(8,128)(2,1)} fusion(bf16[5120,320]{1,0:T(8,128)(2,1)} %bitcast.5, s32[10240]{0:T(1024)S(1)} %broadcast_clamp_fusion), kind=kCustom, calls=%fused_computation.5 | custom fusion | bytes 13148160 | tf_op jit(solution)/shard_map/jit(_take)/gather | solution.py:77
  210.8 9.8 %copy.33 = bf16[10240,320]{0,1:T(8,128)(2,1)} copy(bf16[10240,320]{1,0:T(8,128)(2,1)} %gather_fusion.1) | data formatting | bytes 13107200 | tf_op jit(solution)/shard_map/jit(_take)/gather | solution.py:77
  220.6 7.7 %multiply_convert_fusion = bf16[10240,320]{0,1:T(8,128)(2,1)} fusion(f32[320]{0:T(512)S(1)} %pad_dynamic-slice_fusion.2, f32[10240]{0:T(1024)S(1)} %concatenate.83, bf16[10240,320]{0,1:T(8,128)(2,1)} %copy.33, pred[10240]{0:T(1024)(128)(4,1)S(1)} %get-tuple-element.12), kind=kLoop, calls=%fused_computation.7 | loop fusion | flops 16384000 | bytes 13159680 | tf_op jit(solution)/shard_map/convert_element_type | solution.py:78
  228.4 7.1 %multiply_convert_fusion.1 = (bf16[256,320]{0,1:T(8,128)(2,1)}, f32[256,320]{0,1:T(8,128)S(1)}) fusion(bf16[10240,320]{0,1:T(8,128)(2,1)} %multiply_convert_fusion, bf16[256,10240]{1,0:T(8,128)(2,1)} %all-gather.2.cloned.1.call-done), kind=kOutput, calls=%fused_computation.38 | convolution fusion | flops 1678458880 | bytes 12288000 | tf_op jit(solution)/shard_map/dot_general | solution.py:85
  235.5 4.8 fusion
  240.3 10.6 %bitcast_convert_fusion.1 = (bf16[160,10240]{0,1:T(8,128)(2,1)}, bf16[160,10240]{0,1:T(8,128)(2,1)}) fusion(bf16[10240,160]{1,0:T(8,128)(2,1)} %gather_fusion.2, pred[10240]{0:T(1024)(128)(4,1)S(1)} %get-tuple-element.11, bf16[10240,160]{1,0:T(8,128)(2,1)} %gather_fusion.4), kind=kLoop, calls=%fused_computation.10 | loop fusion | flops 3276800 | bytes 13117440 | tf_op jit(solution)/shard_map/convert_element_type | solution.py:71
  251.0 7.5 %copy.35 = bf16[160,32,320]{2,0,1:T(8,128)(2,1)} copy(bf16[160,32,320]{0,2,1:T(8,128)(2,1)} %bitcast.32) | data formatting | bytes 6553600 | tf_op jit(solution)/shard_map/all_to_all | solution.py:70
  258.5 9.1 %all-to-all-start.1 = ((bf16[160,32,320]{2,0,1:T(8,128)(2,1)}), bf16[160,32,320]{2,0,1:T(8,128)(2,1)}, u32[]{:S(2)}, u32[]{:S(2)}) async-start(bf16[160,32,320]{2,0,1:T(8,128)(2,1)} %copy.35), calls=%async_computation.1 | async-start | bytes 7864320 | tf_op jit(solution)/shard_map/all_to_all | solution.py:70
  267.6 7.5 %copy.38 = bf16[160,32,320]{2,0,1:T(8,128)(2,1)} copy(bf16[160,32,320]{0,2,1:T(8,128)(2,1)} %bitcast.31) | data formatting | bytes 6553600 | tf_op jit(solution)/shard_map/all_to_all | solution.py:73
  275.0 126.1 %all-to-all-done.1 = bf16[160,32,320]{2,0,1:T(8,128)(2,1)} async-done(((bf16[160,32,320]{2,0,1:T(8,128)(2,1)}), bf16[160,32,320]{2,0,1:T(8,128)(2,1)}, u32[]{:S(2)}, u32[]{:S(2)}) %all-to-all-start.1) | async-done | bytes 3276832 | tf_op jit(solution)/shard_map/all_to_all | solution.py:70
  401.1 6.5 %all-to-all-start.2 = ((bf16[160,32,320]{2,0,1:T(8,128)(2,1)}), bf16[160,32,320]{2,0,1:T(8,128)(2,1)}, u32[]{:S(2)}, u32[]{:S(2)}) async-start(bf16[160,32,320]{2,0,1:T(8,128)(2,1)} %copy.38), calls=%async_computation.3 | async-start | bytes 7864320 | tf_op jit(solution)/shard_map/all_to_all | solution.py:73
  407.7 6.1 %convert_element_type.82 = f32[160,32,320]{2,0,1:T(8,128)} convert(bf16[160,32,320]{2,0,1:T(8,128)(2,1)} %all-to-all-done.1) | non-fusion elementwise | flops 1638400 | bytes 9830400 | tf_op jit(solution)/shard_map/convert_element_type | solution.py:72
  413.8 7.0 %gather_fusion.3 = f32[1280,320]{1,0:T(8,128)S(1)} fusion(f32[5120,320]{1,0:T(8,128)} %bitcast.30, s32[2048]{0:T(1024)S(1)} %pad_clamp_fusion), kind=kCustom, calls=%fused_computation.1.clone | custom fusion | bytes 3281920 | tf_op jit(solution)/shard_map/jit(_take)/gather | solution.py:82
  420.8 1.7 copy.36
  422.5 76.3 %all-to-all-done.2 = bf16[160,32,320]{2,0,1:T(8,128)(2,1)} async-done(((bf16[160,32,320]{2,0,1:T(8,128)(2,1)}), bf16[160,32,320]{2,0,1:T(8,128)(2,1)}, u32[]{:S(2)}, u32[]{:S(2)}) %all-to-all-start.2) | async-done | bytes 3276832 | tf_op jit(solution)/shard_map/all_to_all | solution.py:73
  498.8 6.1 %convert_element_type.83 = f32[160,32,320]{2,0,1:T(8,128)} convert(bf16[160,32,320]{2,0,1:T(8,128)(2,1)} %all-to-all-done.2) | non-fusion elementwise | flops 1638400 | bytes 9830400 | tf_op jit(solution)/shard_map/convert_element_type | solution.py:75
  505.0 7.0 %gather_fusion.5 = f32[1280,320]{1,0:T(8,128)S(1)} fusion(f32[5120,320]{1,0:T(8,128)} %bitcast.29, s32[2048]{0:T(1024)S(1)} %pad_clamp_fusion), kind=kCustom, calls=%fused_computation.3.clone | custom fusion | bytes 3281920 | tf_op jit(solution)/shard_map/jit(_take)/gather | solution.py:83
  511.9 1.7 copy.39
  513.6 5.3 %fusion.3 = (bf16[1280,320]{0,1:T(8,128)(2,1)}, f32[1280,320]{0,1:T(8,128)}, f32[1280,320]{0,1:T(8,128)}) fusion(bf16[10240,320]{0,1:T(8,128)(2,1)} %multiply_convert_fusion, s32[]{:T(128)S(6)} %select_n.68, bf16[1280,320]{0,1:T(8,128)(2,1)} %reduce-scatter.2.cloned.1.call-done, f32[1280,320]{0,1:T(8,128)} %copy.39, ...), kind=kLoop, calls=%fused_computation.18 | loop fusion | flops 7372800 | bytes 9012484 | tf_op jit(solution)/shard_map/convert_element_type | solution.py:38
  (33 shorter events, 0.6 us)
Async XLA Ops:
  7.2 221.2 %all-gather.2.cloned.1.call-start = ((), (), s32[]{:S(2)}) async-start(), calls=%async_computation.4 | async-start | bytes 5406720 | tf_op jit(solution)/shard_map/all_gather | solution.py:84
  65.9 13.0 %copy-start.1 = (f32[160,5120]{1,0:T(8,128)S(1)}, f32[160,5120]{1,0:T(8,128)}, u32[]{:S(2)}) copy-start(f32[160,5120]{1,0:T(8,128)} %param.16) | copy-start | bytes 9830404
  65.9 101.9 %all-to-all-start = ((bf16[160,32,320]{2,0,1:T(8,128)(2,1)}), bf16[160,32,320]{2,0,1:T(8,128)(2,1)}, u32[]{:S(2)}, u32[]{:S(2)}) async-start(bf16[160,32,320]{2,0,1:T(8,128)(2,1)} %broadcast_select_fusion), calls=%async_computation | async-start | bytes 7864320 | tf_op jit(solution)/shard_map/all_to_all | solution.py:66
  78.6 435.0 %reduce-scatter.2.cloned.1.call-start = ((), (), s32[]{:S(2)}) async-start(), calls=%async_computation.5 | async-start | bytes 7372800 | tf_op jit(solution)/shard_map/reduce_scatter | solution.py:89
  81.5 3.4 copy-start.2
  125.7 41.2 %copy-start.5 = (s32[5120]{0:T(1024)S(1)}, s32[5120]{0:T(1024)}, u32[]{:S(2)}) copy-start(s32[5120]{0:T(1024)} %param.20) | copy-start | bytes 61444
  125.7 41.2 %copy-start.6 = (s32[5120]{0:T(1024)S(1)}, s32[5120]{0:T(1024)}, u32[]{:S(2)}) copy-start(s32[5120]{0:T(1024)} %param.21) | copy-start | bytes 61444
  125.7 41.3 %copy-start.4 = (s32[5120]{0:T(1024)S(1)}, s32[5120]{0:T(1024)}, u32[]{:S(2)}) copy-start(s32[5120]{0:T(1024)} %param.18) | copy-start | bytes 61444
  228.4 7.1 %copy-start.3 = (bf16[256,320]{0,1:T(8,128)(2,1)S(1)}, bf16[256,320]{0,1:T(8,128)(2,1)}, u32[]{:S(2)}) copy-start(bf16[256,320]{0,1:T(8,128)(2,1)} %param.14) | copy-start | bytes 491524
  228.4 7.1 %copy-start = (bf16[256,10240]{1,0:T(8,128)(2,1)S(1)}, bf16[256,10240]{1,0:T(8,128)(2,1)}, u32[]{:S(2)}) copy-start(bf16[256,10240]{1,0:T(8,128)(2,1)} %all-gather.2.cloned.1.call-done) | copy-start | bytes 15728644
  258.5 142.6 %all-to-all-start.1 = ((bf16[160,32,320]{2,0,1:T(8,128)(2,1)}), bf16[160,32,320]{2,0,1:T(8,128)(2,1)}, u32[]{:S(2)}, u32[]{:S(2)}) async-start(bf16[160,32,320]{2,0,1:T(8,128)(2,1)} %copy.35), calls=%async_computation.1 | async-start | bytes 7864320 | tf_op jit(solution)/shard_map/all_to_all | solution.py:70
  401.1 97.7 %all-to-all-start.2 = ((bf16[160,32,320]{2,0,1:T(8,128)(2,1)}), bf16[160,32,320]{2,0,1:T(8,128)(2,1)}, u32[]{:S(2)}, u32[]{:S(2)}) async-start(bf16[160,32,320]{2,0,1:T(8,128)(2,1)} %copy.38), calls=%async_computation.3 | async-start | bytes 7864320 | tf_op jit(solution)/shard_map/all_to_all | solution.py:73
Sparse Core Ops, SparseCore 0:
  10.5 68.7 all-gather.1
  240.5 162.6 reduce-scatter.1
where the time goes:
time: 527 us; the launch traced here: 526 us
  local copies, waits for them, and re-layouts  226 us (43%)
  waiting for transfers between devices  204 us (39%)
  other arithmetic  41.5 us (8%)
  starting transfers between devices  28.5 us (5%)
  between operations  14.2 us (3%)
  matrix products  11.9 us (2%)
    all_to_all x1, waiting for transfers between devices, shards(): lax.all_to_all(wide_first.astype(jnp.bfloat16), 'tensor', split_axis=1, c...  126 us
    all_to_all x1, waiting for transfers between devices, shards(): lax.all_to_all(wide_second.astype(jnp.bfloat16), 'tensor', split_axis=1,...  76.3 us
    gather x2, local copies, waits for them, and re-layouts, shards(): copied = jnp.take(rows_weight, row_map, axis=0)  52.9 us
    gather x2, local copies, waits for them, and re-layouts, shards(): wide_weight = jnp.take(old_weight, col_map, axis=1)  48.7 us
    gather x1, local copies, waits for them, and re-layouts, shards(): wide_second = jnp.take(old_second, col_map, axis=1)  41.1 us
    gather x1, local copies, waits for them, and re-layouts, shards(): wide_first = jnp.take(old_first, col_map, axis=1)  40.7 us
    all_to_all x1, starting transfers between devices, shards(): lax.all_to_all(wide_weight, 'tensor', split_axis=1, concat_axis=0, tiled=...  12.7 us
    convert_element_type x2, other arithmetic, shards(): rows_first, rows_second = (lax.all_to_all(wide_first.astype(jnp.bfloat16)...  12.3 us
  transfers between devices with their start and end apart: 5, of which 3 were waited for; matrix products, arithmetic and copies ran while one was open for 50% of the time, Pallas kernels for 0%

commit v1 on v0

v1 whole, which is shorter than its diff:
```python
import functools

import jax
import jax.numpy as jnp
from jax import lax
from jax.experimental import pallas as pl
from jax.experimental.pallas import tpu as pltpu
from jax.sharding import PartitionSpec as P

beta_one = 0.9
beta_two = 0.95
adam_eps = 1e-08
learn_rate = 0.01
weight_decay = 0.1
adam_step = 1000.0

LANES = 128
F32 = jnp.float32
BF16 = jnp.bfloat16
VMEM_BYTES = 56 * 1024 * 1024


def growth_maps(row_source, col_source, row_level, col_level, old_width):
    identity = jnp.arange(old_width, dtype=jnp.int32)
    row_map = jnp.concatenate([identity, row_source])
    col_map = jnp.concatenate([identity, col_source])
    unit_scale = jnp.ones((old_width,), F32)
    row_scale = jnp.concatenate([unit_scale, (row_level.astype(F32) + 1.0) / 5.0])
    col_scale = jnp.concatenate([unit_scale, (col_level.astype(F32) + 1.0) / 5.0])
    return (row_map, col_map, row_scale, col_scale)


def activate(values):
    return jax.nn.gelu(values, approximate=True)


def chosen(index_row, depth, start=0):
    at = lax.broadcasted_iota(jnp.int32, (depth, index_row.shape[1]), 0) + start
    return jnp.where(at == index_row, 1.0, 0.0).astype(BF16)


def dot(a, b):
    return jnp.dot(a, b, preferred_element_type=F32)


def column_kernel(slabs_step, copy_ref, own_ref, place_ref, w_ref, m_ref, v_ref, out_ref, total, own_place):
    step = pl.program_id(0)
    rows, depth = w_ref.shape
    parts = [w_ref[...], m_ref[...].astype(BF16), v_ref[...].astype(BF16)]

    @pl.when(step == 0)
    def _():
        for k in range(3):
            own_place[k] = chosen(own_ref[k : k + 1, :], depth)

    same = functools.reduce(
        lambda a, b: a + b,
        [dot(part, own_place[k]) for k, part in enumerate(parts)],
    ).astype(BF16)
    for j in range(slabs_step):
        out_ref[step * slabs_step + j] = same[:, j * LANES : (j + 1) * LANES]
    picked = dot(jnp.concatenate(parts, axis=0), chosen(copy_ref[...], depth, step * depth))

    @pl.when(step == 0)
    def _():
        total[...] = picked

    @pl.when(step > 0)
    def _():
        total[...] += picked

    @pl.when(step == pl.num_programs(0) - 1)
    def _():
        half = out_ref.shape[0] // 2
        width = total.shape[1]
        held = [total[k * rows : (k + 1) * rows, :].astype(BF16) for k in range(3)]
        spread = functools.reduce(
            lambda a, b: a + b,
            [dot(part, chosen(place_ref[k : k + 1, :], width)) for k, part in enumerate(held)],
        ).astype(BF16)
        for j in range(half):
            out_ref[half + j] = spread[:, j * LANES : (j + 1) * LANES]


def grow_columns(old_weight, old_first, old_second, col_source, slabs, slab_width, pieces, piece_at):
    rows, old_width = old_weight.shape
    piece = slab_width // pieces
    half = slabs // 2
    slabs_step = 2
    depth = slabs_step * slab_width
    copy_index = lax.dynamic_slice_in_dim(
        col_source.reshape(half, pieces, piece), piece_at, 1, 1
    ).reshape(1, half * piece)
    lane = jnp.arange(LANES, dtype=jnp.int32)[None, :] - piece * jnp.arange(3, dtype=jnp.int32)[:, None]
    inside = (lane >= 0) & (lane < piece)

    def spread_index(count, stride, offset):
        slab = jnp.arange(count, dtype=jnp.int32)[None, :, None] * stride + offset
        return jnp.where(inside[:, None, :], lane[:, None, :] + slab, -1).reshape(3, count * LANES)

    own_index = spread_index(slabs_step, slab_width, piece_at * piece)
    place_index = spread_index(half, piece, 0)
    return pl.pallas_call(
        functools.partial(column_kernel, slabs_step),
        grid=(half // slabs_step,),
        in_specs=[
            pl.BlockSpec((1, half * piece), lambda s: (0, 0)),
            pl.BlockSpec((3, slabs_step * LANES), lambda s: (0, 0)),
            pl.BlockSpec((3, half * LANES), lambda s: (0, 0)),
            pl.BlockSpec((rows, depth), lambda s: (0, s)),
            pl.BlockSpec((rows, depth), lambda s: (0, s)),
            pl.BlockSpec((rows, depth), lambda s: (0, s)),
        ],
        out_specs=pl.BlockSpec((slabs, rows, LANES), lambda s: (0, 0, 0)),
        out_shape=jax.ShapeDtypeStruct((slabs, rows, LANES), BF16),
        scratch_shapes=[
            pltpu.VMEM((3 * rows, half * piece), F32),
            pltpu.VMEM((3, depth, slabs_step * LANES), BF16),
        ],
        compiler_params=pltpu.CompilerParams(vmem_limit_bytes=VMEM_BYTES),
        cost_estimate=pl.CostEstimate(flops=1000, bytes_accessed=1000, transcendentals=0),
        name="grow_columns",
    )(copy_index, own_index, place_index, old_weight, old_first, old_second)


def row_kernel(index_ref, in_ref, out_ref, wide, picked):
    old = in_ref.shape[0]
    chunk = 512
    for c in range(0, old, chunk):
        part = in_ref[c : c + chunk, :]
        out_ref[c : c + chunk, :] = part
        wide[c : c + chunk, :] = part.astype(F32)

    def body(c, carry):
        for i in range(32):
            at = c * 32 + i
            picked[pl.ds(at, 1), :] = wide[pl.ds(index_ref[at], 1), :]
        return carry

    lax.fori_loop(0, old // 32, body, 0)
    for c in range(0, old, chunk):
        out_ref[old + c : old + c + chunk, :] = picked[c : c + chunk, :].astype(BF16)


def grow_rows(columns, row_source):
    old = columns.shape[0]
    return pl.pallas_call(
        row_kernel,
        in_specs=[
            pl.BlockSpec(memory_space=pltpu.SMEM),
            pl.BlockSpec(memory_space=pltpu.VMEM),
        ],
        out_specs=pl.BlockSpec(memory_space=pltpu.VMEM),
        out_shape=jax.ShapeDtypeStruct((2 * old, LANES), BF16),
        scratch_shapes=[pltpu.VMEM((old, LANES), F32), pltpu.VMEM((old, LANES), F32)],
        compiler_params=pltpu.CompilerParams(vmem_limit_bytes=VMEM_BYTES),
        cost_estimate=pl.CostEstimate(flops=1000, bytes_accessed=1000, transcendentals=0),
        name="grow_rows",
    )(row_source, columns)


def assemble(blocks_ref, array_at, piece, slab_width):
    pieces = blocks_ref.shape[0]
    row = lax.broadcasted_iota(jnp.int32, (slab_width, LANES), 0)
    at = lax.broadcasted_iota(jnp.int32, (slab_width, LANES), 1) - array_at * piece
    inside = (at >= 0) & (at < piece)
    place = jnp.concatenate(
        [jnp.where(inside & (d * piece + at == row), 1.0, 0.0).astype(BF16) for d in range(pieces)], axis=1
    )
    block = jnp.concatenate([blocks_ref[d] for d in range(pieces)], axis=1)
    return lax.dot_general(place, block, (((1,), (1,)), ((), ())), preferred_element_type=F32)


def weight_kernel(piece, blocks_ref, row_scale_ref, col_scale_ref, weight_ref):
    copied = assemble(blocks_ref, 0, piece, weight_ref.shape[0])
    weight_ref[...] = (copied * row_scale_ref[...] * col_scale_ref[...]).astype(BF16)


def moments_kernel(piece, blocks_ref, first_ref, second_ref):
    for a, ref in enumerate((first_ref, second_ref)):
        ref[...] = assemble(blocks_ref, a + 1, piece, ref.shape[0]).astype(BF16)


def grown_block(kernel, operands, results, block_rows, slab_width, piece):
    shape = jax.ShapeDtypeStruct((slab_width, block_rows), BF16)
    return pl.pallas_call(
        functools.partial(kernel, piece),
        in_specs=[pl.BlockSpec(memory_space=pltpu.VMEM)] * len(operands),
        out_specs=[pl.BlockSpec(memory_space=pltpu.VMEM)] * results,
        out_shape=[shape] * results,
        compiler_params=pltpu.CompilerParams(vmem_limit_bytes=VMEM_BYTES),
        cost_estimate=pl.CostEstimate(flops=1000, bytes_accessed=1000, transcendentals=0),
        name="grown_block_%d" % results,
    )(*operands)


def forward_kernel(place_ref, *refs):
    parts, weight_ref, out_ref = refs[:-2], refs[-2], refs[-1]
    step = pl.program_id(0)
    half = pl.num_programs(0)
    core = place_ref[1]
    count = len(parts) // 2
    for refs_of, at in ((parts[:count], core), (parts[count:], 1 - core)):
        group = jnp.concatenate([ref[...].reshape(-1, ref.shape[-1]) for ref in refs_of], axis=0)
        out_ref[at * half + step] = lax.dot_general(
            weight_ref[...], group, (((1,), (1,)), ((), ())), preferred_element_type=F32
        ).astype(BF16)


def forward(place, parts, weight, groups):
    near, half, chip_rows, block_rows = parts[0].shape
    shape = (groups, weight.shape[0], len(parts) // 2 * near * chip_rows)
    tokens = pl.BlockSpec((near, 1, chip_rows, block_rows), lambda s: (0, s, 0, 0))
    return pl.pallas_call(
        forward_kernel,
        grid=(half,),
        in_specs=[pl.BlockSpec(memory_space=pltpu.SMEM)]
        + [tokens] * len(parts)
        + [pl.BlockSpec(weight.shape, lambda s: (0, 0))],
        out_specs=pl.BlockSpec(shape, lambda s: (0, 0, 0)),
        out_shape=jax.ShapeDtypeStruct(shape, BF16),
        compiler_params=pltpu.CompilerParams(vmem_limit_bytes=VMEM_BYTES),
        cost_estimate=pl.CostEstimate(flops=1000, bytes_accessed=1000, transcendentals=0),
        name="forward_terms",
    )(place, *parts, weight)


def adam_kernel(groups, place_ref, *refs):
    parts, grads, refs = refs[: -groups - 7], refs[-groups - 7 : -7], refs[-7:]
    first_ref, second_ref, weight_ref, new_weight_ref, new_first_ref, new_second_ref, held = refs
    step_rows = weight_ref.shape[1]
    half = parts[0].shape[1]
    core = place_ref[1]
    count = len(parts) // 2

    @pl.when(pl.program_id(0) == 0)
    def _():
        for k, ref in enumerate(grads):
            held[jnp.bitwise_xor(place_ref[0], k)] = ref[...]

    gradient = None
    for refs_of, at in ((parts[:count], core), (parts[count:], 1 - core)):
        for j in range(half):
            group = jnp.concatenate([ref[:, j].reshape(-1, step_rows) for ref in refs_of], axis=0)
            term = dot(held[at * half + j], group)
            gradient = term if gradient is None else gradient + term
    weight = weight_ref[...].astype(F32)
    new_first = beta_one * first_ref[...].astype(F32) + (1.0 - beta_one) * gradient
    new_second = beta_two * second_ref[...].astype(F32) + (1.0 - beta_two) * gradient * gradient
    first_corr = 1.0 - beta_one**adam_step
    second_corr = 1.0 - beta_two**adam_step
    update = (
        new_first * (1.0 / first_corr) / (jnp.sqrt(new_second * (1.0 / second_corr)) + adam_eps)
        + weight_decay * weight
    )
    new_weight_ref[...] = (weight - learn_rate * update).astype(BF16)
    new_first_ref[...] = new_first
    new_second_ref[...] = new_second


def backward(place, parts, grads, first, second, weight):
    near, half, chip_rows, block_rows = parts[0].shape
    slab_width = weight.shape[0]
    step_rows = 256
    tokens = pl.BlockSpec((near, half, chip_rows, step_rows), lambda s: (0, 0, 0, s))
    block = pl.BlockSpec((slab_width, step_rows), lambda s: (0, s))
    return pl.pallas_call(
        functools.partial(adam_kernel, len(grads)),
        grid=(block_rows // step_rows,),
        in_specs=[pl.BlockSpec(memory_space=pltpu.SMEM)]
        + [tokens] * len(parts)
        + [pl.BlockSpec(grads[0].shape, lambda s: (0, 0))] * len(grads)
        + [block, block, block],
        out_specs=[block, block, block],
        out_shape=[
            jax.ShapeDtypeStruct((slab_width, block_rows), BF16),
            jax.ShapeDtypeStruct((slab_width, block_rows), F32),
            jax.ShapeDtypeStruct((slab_width, block_rows), F32),
        ],
        scratch_shapes=[pltpu.VMEM((len(grads),) + grads[0].shape, BF16)],
        compiler_params=pltpu.CompilerParams(vmem_limit_bytes=VMEM_BYTES),
        cost_estimate=pl.CostEstimate(flops=1000, bytes_accessed=1000, transcendentals=0),
        name="gradient_adam",
    )(place, *parts, *grads, first, second, weight)


DIM_X, DIM_Z = 4, 4


def shifted(dx, dz, dc):
    places = [(x, z, c) for x in range(DIM_X) for z in range(DIM_Z) for c in range(2)]

    def at(x, z, c):
        return ((x % DIM_X) * DIM_Z + z % DIM_Z) * 2 + c % 2

    return [(at(x, z, c), at(x + dx, z + dz, c + dc)) for x, z, c in places]


def stack_kernel(*refs):
    for k, ref in enumerate(refs[:-1]):
        refs[-1][k] = ref[0]


def stacked(values):
    shape = (len(values),) + values[0].shape[1:]
    return pl.pallas_call(
        stack_kernel,
        in_specs=[pl.BlockSpec(memory_space=pltpu.VMEM)] * len(values),
        out_specs=pl.BlockSpec(memory_space=pltpu.VMEM),
        out_shape=jax.ShapeDtypeStruct(shape, values[0].dtype),
        compiler_params=pltpu.CompilerParams(vmem_limit_bytes=VMEM_BYTES),
        cost_estimate=pl.CostEstimate(flops=1000, bytes_accessed=1000, transcendentals=0),
        name="stack_tokens",
    )(*values)


def chip_tokens(part, core):
    groups, rows, block_rows = part.shape
    half = groups // 2
    mine = lax.dynamic_slice_in_dim(part, core * half, half, 0)
    away = lax.dynamic_slice_in_dim(part, (1 - core) * half, half, 0)
    theirs = lax.ppermute(away, "tensor", shifted(0, 0, 1))
    chip = jnp.stack([jnp.where(core == 0, mine, theirs), jnp.where(core == 0, theirs, mine)], axis=1)
    return chip.reshape(1, half, 2 * rows, block_rows)


def to_groups(values):
    groups = lax.axis_size("dp")
    return [values] + [lax.ppermute(values, "dp", [(i, i ^ k) for i in range(groups)]) for k in range(1, groups)]


def in_order(values, *others):
    return lax.optimization_barrier((values, *others))


def shards(tokens, cotangent, old_weight, old_first, old_second, row_source, col_source, row_level, col_level):
    slabs = lax.axis_size("tensor")
    groups = lax.axis_size("dp")
    slab_at, group_at = lax.axis_index("tensor"), lax.axis_index("dp")
    core = slab_at % 2
    place = jnp.stack([group_at, core]).astype(jnp.int32)
    rows = tokens.shape[0]
    old_width = old_weight.shape[1]
    new_width = old_width + row_source.shape[0]
    slab_width = new_width // slabs
    block_rows = new_width // groups
    piece = slab_width // groups
    _, _, row_scale, col_scale = growth_maps(row_source, col_source, row_level, col_level, old_width)
    row_scale = lax.dynamic_slice_in_dim(row_scale, group_at * block_rows, block_rows)[None, :]
    col_scale = lax.dynamic_slice_in_dim(col_scale, slab_at * slab_width, slab_width)[:, None]

    def exchange(values, axis):
        return lax.all_to_all(values, axis, split_axis=0, concat_axis=0, tiled=True)

    chip_at = slab_at // 2
    lane = jnp.arange(slabs * rows, dtype=jnp.int32)
    away, within = lane // (2 * rows), lane % (2 * rows)
    chip_x = (chip_at // DIM_Z - away // DIM_Z) % DIM_X
    chip_z = (chip_at % DIM_Z - away % DIM_Z) % DIM_Z
    real = (chip_x * DIM_Z + chip_z) * 2 * rows + within
    to_real = (real[:, None] == lane[None, :]).astype(BF16)

    part = lax.all_to_all(tokens, "dp", split_axis=1, concat_axis=0, tiled=True)
    columns = grow_columns(old_weight, old_first, old_second, col_source, slabs, slab_width, groups, group_at)
    part, columns = in_order(part, columns)
    columns = exchange(columns, "tensor")
    chip = chip_tokens(part.reshape(groups, rows, block_rows), core)
    along_z = [chip] + [lax.ppermute(chip, "tensor", shifted(0, k, 0)) for k in range(1, DIM_Z)]
    along_z = stacked(along_z)
    own = [along_z] + [lax.ppermute(along_z, "tensor", shifted(k, 0, 0)) for k in range(1, DIM_X)]
    grown = grow_rows(columns.reshape(old_width, LANES), row_source)
    blocks = exchange(grown.reshape(groups, block_rows, LANES), "dp")
    blocks, *own = in_order(blocks, *own)
    parts = own + [lax.ppermute(values, "tensor", shifted(0, 0, 1)) for values in own]
    (weight,) = grown_block(weight_kernel, (blocks, row_scale, col_scale), 1, block_rows, slab_width, piece)

    terms = exchange(forward(place, parts, weight, groups), "dp")
    first, second = grown_block(moments_kernel, (blocks,), 2, block_rows, slab_width, piece)
    terms, first, second = in_order(terms, first, second)
    turned_grad = dot(cotangent.T, to_real.T)
    hidden = terms.astype(F32).sum(axis=0)
    activation = activate(hidden).astype(BF16)
    _, pullback = jax.vjp(activate, hidden)
    hidden_grad = pullback(turned_grad)[0].astype(BF16)
    activation = dot(activation, to_real).astype(BF16)

    grads = to_groups(hidden_grad)
    news = backward(place, parts, grads, first, second, weight)
    return (activation.T,) + tuple(new.T for new in news)


def solution(mesh):
    placed = (
        P(("dp", "tensor"), None),
        P("dp", "tensor"),
        P("tensor", None),
        P("tensor", None),
        P("tensor", None),
        P(),
        P(),
        P(),
        P(),
    )
    return jax.shard_map(
        shards,
        mesh=mesh,
        in_specs=placed,
        out_specs=(P("dp", "tensor"), P("dp", "tensor"), P("dp", "tensor"), P("dp", "tensor")),
        check_vma=False,
    )
```

time: 527 us -> 232 us (0.44)
  local copies, waits for them, and re-layouts: 226 us -> 5.45 us
  waiting for transfers between devices: 204 us -> 94.7 us
  Pallas kernels: 0 us -> 47 us
  blocking collectives: 0 us -> 42.4 us
  other arithmetic: 41.5 us -> 2.24 us
  between operations: 14.2 us -> 1.03 us
  matrix products: 11.9 us -> 1.39 us
  starting transfers between devices: 28.5 us -> 37.4 us
    gather x10 -> x0, local copies, waits for them, and re-layouts: 201 us -> none  [the longest x2 52.9 us: shards(): copied = jnp.take(rows_weight, row_map, axis=0)]
    all_to_all x3, waiting for transfers between devices: 203 us -> 13.2 us  [the longest x2 13.2 us: exchange(): return lax.all_to_all(values, axis, split_axis=0, concat_axis=0, tiled=True)]
    ppermute x0 -> x18, waiting for transfers between devices: none -> 81.5 us  [the longest x3 38.5 us: shards(): lax.ppermute(chip, 'tensor', shifted(0, k, 0))]
    pallas_call x0 -> x7, Pallas kernels: none -> 47 us  [the longest x1 13.3 us: grow_columns(): pl.pallas_call(functools.partial(column_kernel, slabs_step), grid=(half /...]
    all_to_all x0 -> x1, blocking collectives: none -> 42.4 us  [exchange(): return lax.all_to_all(values, axis, split_axis=0, concat_axis=0, tiled=True)]
    convert_element_type x5 -> x0, other arithmetic: 35.9 us -> none  [the longest x2 12.3 us: shards(): rows_first, rows_second = (lax.all_to_all(wide_first.astype(jnp.bfloat16)...]
    ppermute x0 -> x18, starting transfers between devices: none -> 15.6 us  [the longest x7 7.81 us: to_groups(): lax.ppermute(values, 'dp', [(i, i ^ k) for i in range(groups)])]
    all_to_all x2 -> x0, local copies, waits for them, and re-layouts: 15 us -> none  [the longest x1 7.5 us: shards(): lax.all_to_all(wide_first.astype(jnp.bfloat16), 'tensor', split_axis=1, c...]
  transfers between devices with their start and end apart: 5 -> 21, of which waited for: 3 -> 14; matrix products, arithmetic and copies ran while one was open for 50% -> 3% of each run, Pallas kernels for 0% -> 10%
where the time goes in v1:
time: 232 us
  waiting for transfers between devices  94.7 us (41%)
  Pallas kernels  47 us (20%)
  blocking collectives  42.4 us (18%)
  starting transfers between devices  37.4 us (16%)
  local copies, waits for them, and re-layouts  5.45 us (2%)
    all_to_all x1, blocking collectives, exchange(): return lax.all_to_all(values, axis, split_axis=0, concat_axis=0, tiled=True)  42.4 us
    ppermute x3, waiting for transfers between devices, shards(): lax.ppermute(chip, 'tensor', shifted(0, k, 0))  38.5 us
    ppermute x3, waiting for transfers between devices, shards(): lax.ppermute(along_z, 'tensor', shifted(k, 0, 0))  30.4 us
    all_to_all x2, starting transfers between devices, exchange(): return lax.all_to_all(values, axis, split_axis=0, concat_axis=0, tiled=True)  15.3 us
    pallas_call x1, Pallas kernels, grow_columns(): pl.pallas_call(functools.partial(column_kernel, slabs_step), grid=(half /...  13.3 us
    all_to_all x2, waiting for transfers between devices, exchange(): return lax.all_to_all(values, axis, split_axis=0, concat_axis=0, tiled=True)  13.2 us
    ppermute x7, waiting for transfers between devices, to_groups(): lax.ppermute(values, 'dp', [(i, i ^ k) for i in range(groups)])  11.6 us
    pallas_call x1, Pallas kernels, backward(): pl.pallas_call(functools.partial(adam_kernel, len(grads)), grid=(block_ro...  9.11 us
  transfers between devices with their start and end apart: 21, of which 14 were waited for; matrix products, arithmetic and copies ran while one was open for 3% of the time, Pallas kernels for 10%

profile of v1, /device:TPU:1, one launch (start us, length us, event | category | flops | bytes accessed | tf_op | source)
XLA Modules:
  0.0 231.6 jit_solution(8957769879828145812)
XLA Ops:
  0.6 6.5 %all-to-all-start = ((bf16[8,8,1280]{2,0,1:T(8,128)(2,1)}), bf16[8,8,1280]{2,0,1:T(8,128)(2,1)S(1)}, u32[]{:S(2)}, u32[]{:S(2)}) async-start(bf16[8,8,1280]{2,0,1:T(8,128)(2,1)} %bitcast.51), calls=%async_computation | async-start | bytes 327680 | tf_op jit(solution)/shard_map/all_to_all | solution.py:363
  10.3 13.3 %grow_columns.1 = bf16[32,160,128]{2,1,0:T(8,128)(2,1)} custom-call(s32[1,640]{1,0:T(1,128)} %reshape.164.copy_ref, s32[3,256]{1,0:T(4,128)} %fusion.10.own_ref, s32[3,2048]{1,0:T(4,128)} %fusion.9.place_ref, bf16[160,5120]{1,0:T(8,128)(2,1)} %w_ref.1, f32[160,5120]{1,0:T(8,128)} %m_ref.1, f32[160,5120]{1,0:T(8,128)} %v_ref.1), custom_call_target="tpu_custom_call" | custom-call | flops 1000 | bytes 1000 | tf_op jit(solution)/shard_map/grow_columns/pallas_call | solution.py:103
  23.6 42.4 %all_to_all.34 = bf16[32,160,128]{2,1,0:T(8,128)(2,1)} all-to-all(bf16[32,160,128]{2,1,0:T(8,128)(2,1)} %grow_columns.1), channel_id=1, replica_groups=mesh['dp'=8,'tensor'=32] {'tensor'}, dimensions={0} | all-to-all | bytes 2621440 | tf_op jit(solution)/shard_map/all_to_all | solution.py:353
  66.0 8.1 %grow_rows.1 = bf16[10240,128]{1,0:T(8,128)(2,1)} custom-call(s32[5120]{0:T(1024)} %index_ref.1, bf16[5120,128]{1,0:T(8,128)(2,1)} %bitcast.48), custom_call_target="tpu_custom_call" | custom-call | flops 1000 | bytes 1000 | tf_op jit(solution)/shard_map/grow_rows/pallas_call | solution.py:147
  74.1 10.1 %all-to-all-start.2 = ((bf16[8,1280,128]{2,1,0:T(8,128)(2,1)}), bf16[8,1280,128]{2,1,0:T(8,128)(2,1)S(1)}, u32[]{:S(2)}, u32[]{:S(2)}) async-start(bf16[8,1280,128]{2,1,0:T(8,128)(2,1)} %bitcast.47), calls=%async_computation.2 | async-start | bytes 5242880 | tf_op jit(solution)/shard_map/all_to_all | solution.py:353
  84.8 0.9 collective-permute-done
  85.8 1.5 collective-permute-start.3
  87.3 1.9 collective-permute-start.2
  89.8 2.5 %collective-permute-done.3.refs_3_ = bf16[1,4,16,1280]{3,2,1,0:T(8,128)(2,1)S(1)} collective-permute-done((bf16[1,4,16,1280]{3,2,1,0:T(8,128)(2,1)S(1)}, bf16[1,4,16,1280]{3,2,1,0:T(8,128)(2,1)S(1)}, u32[]{:S(2)}, u32[]{:S(2)}) %collective-permute-start.3) | collective-permute-done | bytes 163872 | tf_op jit(solution)/shard_map/ppermute | solution.py:368
  92.3 31.1 %collective-permute-done.2.refs_2_ = bf16[1,4,16,1280]{3,2,1,0:T(8,128)(2,1)S(1)} collective-permute-done((bf16[1,4,16,1280]{3,2,1,0:T(8,128)(2,1)S(1)}, bf16[1,4,16,1280]{3,2,1,0:T(8,128)(2,1)S(1)}, u32[]{:S(2)}, u32[]{:S(2)}) %collective-permute-start.2) | collective-permute-done | bytes 163872 | tf_op jit(solution)/shard_map/ppermute | solution.py:368
  123.4 4.8 %collective-permute-done.1.refs_1_ = bf16[1,4,16,1280]{3,2,1,0:T(8,128)(2,1)S(1)} collective-permute-done((bf16[1,4,16,1280]{3,2,1,0:T(8,128)(2,1)S(1)}, bf16[1,4,16,1280]{3,2,1,0:T(8,128)(2,1)S(1)}, u32[]{:S(2)}, u32[]{:S(2)}) %collective-permute-start.1) | collective-permute-done | bytes 163872 | tf_op jit(solution)/shard_map/ppermute | solution.py:368
  128.9 2.0 stack_tokens.1.refs_0_
  131.0 0.9 collective-permute-start.6
  131.8 1.2 collective-permute-start.5
  133.1 13.1 %collective-permute-done.6.refs_3_ = bf16[4,4,16,1280]{3,2,1,0:T(8,128)(2,1)S(1)} collective-permute-done((bf16[4,4,16,1280]{3,2,1,0:T(8,128)(2,1)}, bf16[4,4,16,1280]{3,2,1,0:T(8,128)(2,1)S(1)}, u32[]{:S(2)}, u32[]{:S(2)}) %collective-permute-start.6) | collective-permute-done | bytes 655392 | tf_op jit(solution)/shard_map/ppermute | solution.py:370
  146.2 2.1 collective-permute-done.5.refs_2_
  148.3 0.8 copy-done.3
  149.2 15.2 %collective-permute-done.4.refs_1_ = bf16[4,4,16,1280]{3,2,1,0:T(8,128)(2,1)} collective-permute-done((bf16[4,4,16,1280]{3,2,1,0:T(8,128)(2,1)}, bf16[4,4,16,1280]{3,2,1,0:T(8,128)(2,1)}, u32[]{:S(2)}, u32[]{:S(2)}) %collective-permute-start.4) | collective-permute-done | bytes 655392 | tf_op jit(solution)/shard_map/ppermute | solution.py:370
  167.7 3.7 %grown_block_1.1.refs_8_.refs_18_ = bf16[320,1280]{1,0:T(8,128)(2,1)} custom-call(bf16[8,1280,128]{2,1,0:T(8,128)(2,1)} %copy-done.1, f32[1,1280]{1,0:T(1,128)} %broadcast_in_dim.50.row_scale_ref, f32[320,1]{1,0:T(8,128)} %broadcast_in_dim.52.col_scale_ref), custom_call_target="tpu_custom_call" | custom-call | flops 1000 | bytes 1000 | tf_op jit(solution)/shard_map/grown_block_1/pallas_call | solution.py:186
  171.4 6.2 %forward_terms.1 = bf16[8,320,256]{2,1,0:T(8,128)(2,1)} custom-call(s32[2]{0:T(128)} %pad_add_fusion.place_ref, bf16[4,4,16,1280]{3,2,1,0:T(8,128)(2,1)} %stack_tokens.1.refs_0_, bf16[4,4,16,1280]{3,2,1,0:T(8,128)(2,1)} %collective-permute-done.4.refs_1_, bf16[4,4,16,1280]{3,2,1,0:T(8,128)(2,1)} %copy-done.3, bf16[4,4,16,1280]{3,2,1,0:T(8,128)(2,1)} %copy-done.2, ...), custom_call_target="tpu_custom_call" | custom-call | flops 1000 | bytes 1000 | tf_op jit(solution)/shard_map/forward_terms/pallas_call | solution.py:214
  177.6 5.2 %all-to-all-start.3 = ((bf16[8,320,256]{2,1,0:T(8,128)(2,1)}), bf16[8,320,256]{2,1,0:T(8,128)(2,1)S(1)}, u32[]{:S(2)}, u32[]{:S(2)}) async-start(bf16[8,320,256]{2,1,0:T(8,128)(2,1)} %forward_terms.1), calls=%async_computation.3 | async-start | bytes 2621440 | tf_op jit(solution)/shard_map/all_to_all | solution.py:353
  182.8 4.6 %grown_block_2.1 = (bf16[320,1280]{1,0:T(8,128)(2,1)}, bf16[320,1280]{1,0:T(8,128)(2,1)}) custom-call(bf16[8,1280,128]{2,1,0:T(8,128)(2,1)} %copy-done.1), custom_call_target="tpu_custom_call" | custom-call | flops 1000 | bytes 1000 | tf_op jit(solution)/shard_map/grown_block_2/pallas_call | solution.py:186
  187.3 13.2 %all-to-all-done.3 = bf16[8,320,256]{2,1,0:T(8,128)(2,1)S(1)} async-done(((bf16[8,320,256]{2,1,0:T(8,128)(2,1)}), bf16[8,320,256]{2,1,0:T(8,128)(2,1)S(1)}, u32[]{:S(2)}, u32[]{:S(2)}) %all-to-all-start.3) | async-done | bytes 1310752 | tf_op jit(solution)/shard_map/all_to_all | solution.py:353
  201.1 2.5 %collective-permute-start.17 = (bf16[320,256]{1,0:T(8,128)(2,1)S(1)}, bf16[320,256]{1,0:T(8,128)(2,1)S(1)}, u32[]{:S(2)}, u32[]{:S(2)}) collective-permute-start(bf16[320,256]{1,0:T(8,128)(2,1)S(1)} %fusion.6.refs_8_), channel_id=1, source_target_pairs={{0,224},{32,192},{64,160},{96,128},{128,96},{160,64},{192,32},{224... | collective-permute-start | bytes 491528 | tf_op jit(solution)/shard_map/ppermute | solution.py:329
  203.9 2.4 %collective-permute-start.15 = (bf16[320,256]{1,0:T(8,128)(2,1)S(1)}, bf16[320,256]{1,0:T(8,128)(2,1)S(1)}, u32[]{:S(2)}, u32[]{:S(2)}) collective-permute-start(bf16[320,256]{1,0:T(8,128)(2,1)S(1)} %fusion.6.refs_8_), channel_id=1, source_target_pairs={{0,160},{32,128},{64,224},{96,192},{128,32},{160,0},{192,96},{224,... | collective-permute-start | bytes 491528 | tf_op jit(solution)/shard_map/ppermute | solution.py:329
  206.6 1.2 collective-permute-start.13
  209.0 2.9 %collective-permute-done.16.refs_14_ = bf16[320,256]{1,0:T(8,128)(2,1)S(1)} collective-permute-done((bf16[320,256]{1,0:T(8,128)(2,1)S(1)}, bf16[320,256]{1,0:T(8,128)(2,1)S(1)}, u32[]{:S(2)}, u32[]{:S(2)}) %collective-permute-start.16) | collective-permute-done | bytes 163872 | tf_op jit(solution)/shard_map/ppermute | solution.py:329
  212.4 1.0 convolution_convert_fusion
  213.9 3.9 %collective-permute-done.14.refs_12_ = bf16[320,256]{1,0:T(8,128)(2,1)S(1)} collective-permute-done((bf16[320,256]{1,0:T(8,128)(2,1)S(1)}, bf16[320,256]{1,0:T(8,128)(2,1)S(1)}, u32[]{:S(2)}, u32[]{:S(2)}) %collective-permute-start.14) | collective-permute-done | bytes 163872 | tf_op jit(solution)/shard_map/ppermute | solution.py:329
  217.8 1.6 collective-permute-done.13.refs_11_
  219.4 2.2 collective-permute-done.11.refs_9_
  222.3 9.1 %gradient_adam.1 = (bf16[320,1280]{1,0:T(8,128)(2,1)}, f32[320,1280]{1,0:T(8,128)}, f32[320,1280]{1,0:T(8,128)}) custom-call(s32[2]{0:T(128)} %pad_add_fusion.place_ref, bf16[4,4,16,1280]{3,2,1,0:T(8,128)(2,1)} %stack_tokens.1.refs_0_, bf16[4,4,16,1280]{3,2,1,0:T(8,128)(2,1)} %collective-permute-done.4.refs_1_, bf16[4,4,16,1280]{3,2,1,0:T(8,128)(2,1)} %copy-done.3, ...), custom_call_target="tpu_custom_call" | custom-call | flops 1000 | bytes 1000 | tf_op jit(solution)/shard_map/gradient_adam/pallas_call | solution.py:267
  (83 shorter events, 12.5 us)
Async XLA Ops:
  0.6 200.1 %copy-start = (bf16[256,320]{0,1:T(8,128)(2,1)S(1)}, bf16[256,320]{0,1:T(8,128)(2,1)}, u32[]{:S(2)}) copy-start(bf16[256,320]{0,1:T(8,128)(2,1)} %param.10) | copy-start | bytes 491524
  0.6 22.9 %all-to-all-start = ((bf16[8,8,1280]{2,0,1:T(8,128)(2,1)}), bf16[8,8,1280]{2,0,1:T(8,128)(2,1)S(1)}, u32[]{:S(2)}, u32[]{:S(2)}) async-start(bf16[8,8,1280]{2,0,1:T(8,128)(2,1)} %bitcast.51), calls=%async_computation | async-start | bytes 327680 | tf_op jit(solution)/shard_map/all_to_all | solution.py:363
  74.1 90.3 %all-to-all-start.2 = ((bf16[8,1280,128]{2,1,0:T(8,128)(2,1)}), bf16[8,1280,128]{2,1,0:T(8,128)(2,1)S(1)}, u32[]{:S(2)}, u32[]{:S(2)}) async-start(bf16[8,1280,128]{2,1,0:T(8,128)(2,1)} %bitcast.47), calls=%async_computation.2 | async-start | bytes 5242880 | tf_op jit(solution)/shard_map/all_to_all | solution.py:353
  84.2 81.3 %copy-start.16 = (s32[5120]{0:T(1024)S(1)}, s32[5120]{0:T(1024)}, u32[]{:S(2)}) copy-start(s32[5120]{0:T(1024)} %param.16) | copy-start | bytes 61444
  84.2 82.0 %copy-start.17 = (s32[5120]{0:T(1024)S(1)}, s32[5120]{0:T(1024)}, u32[]{:S(2)}) copy-start(s32[5120]{0:T(1024)} %param.17) | copy-start | bytes 61444
  84.2 1.5 collective-permute-start
  85.8 42.4 %copy-start.4 = (bf16[1,4,16,1280]{3,2,1,0:T(8,128)(2,1)}, bf16[1,4,16,1280]{3,2,1,0:T(8,128)(2,1)S(1)}, u32[]{:S(2)}) copy-start(bf16[1,4,16,1280]{3,2,1,0:T(8,128)(2,1)S(1)} %maximum_bitcast_fusion.refs_0_) | copy-start | bytes 491524
  85.8 6.5 %collective-permute-start.3 = (bf16[1,4,16,1280]{3,2,1,0:T(8,128)(2,1)S(1)}, bf16[1,4,16,1280]{3,2,1,0:T(8,128)(2,1)S(1)}, u32[]{:S(2)}, u32[]{:S(2)}) collective-permute-start(bf16[1,4,16,1280]{3,2,1,0:T(8,128)(2,1)S(1)} %maximum_bitcast_fusion.refs_0_), channel_id=1, source_target_pairs={{0,6},{1,7},{2,0},{3,1},{4,2},{5,3},{6,4},{7,5},{8,14},{9,15},{10,... | collective-permute-start | bytes 491528 | tf_op jit(solution)/shard_map/ppermute | solution.py:368
  87.3 36.1 %collective-permute-start.2 = (bf16[1,4,16,1280]{3,2,1,0:T(8,128)(2,1)S(1)}, bf16[1,4,16,1280]{3,2,1,0:T(8,128)(2,1)S(1)}, u32[]{:S(2)}, u32[]{:S(2)}) collective-permute-start(bf16[1,4,16,1280]{3,2,1,0:T(8,128)(2,1)S(1)} %maximum_bitcast_fusion.refs_0_), channel_id=1, source_target_pairs={{0,4},{1,5},{2,6},{3,7},{4,0},{5,1},{6,2},{7,3},{8,12},{9,13},{10,... | collective-permute-start | bytes 491528 | tf_op jit(solution)/shard_map/ppermute | solution.py:368
  89.2 39.1 %collective-permute-start.1 = (bf16[1,4,16,1280]{3,2,1,0:T(8,128)(2,1)S(1)}, bf16[1,4,16,1280]{3,2,1,0:T(8,128)(2,1)S(1)}, u32[]{:S(2)}, u32[]{:S(2)}) collective-permute-start(bf16[1,4,16,1280]{3,2,1,0:T(8,128)(2,1)S(1)} %maximum_bitcast_fusion.refs_0_), channel_id=1, source_target_pairs={{0,2},{1,3},{2,4},{3,5},{4,6},{5,7},{6,0},{7,1},{8,10},{9,11},{10,... | collective-permute-start | bytes 491528 | tf_op jit(solution)/shard_map/ppermute | solution.py:368
  92.3 36.0 %copy-start.5 = (bf16[1,4,16,1280]{3,2,1,0:T(8,128)(2,1)}, bf16[1,4,16,1280]{3,2,1,0:T(8,128)(2,1)S(1)}, u32[]{:S(2)}) copy-start(bf16[1,4,16,1280]{3,2,1,0:T(8,128)(2,1)S(1)} %collective-permute-done.3.refs_3_) | copy-start | bytes 491524
  123.4 4.9 %copy-start.6 = (bf16[1,4,16,1280]{3,2,1,0:T(8,128)(2,1)}, bf16[1,4,16,1280]{3,2,1,0:T(8,128)(2,1)S(1)}, u32[]{:S(2)}) copy-start(bf16[1,4,16,1280]{3,2,1,0:T(8,128)(2,1)S(1)} %collective-permute-done.2.refs_2_) | copy-start | bytes 491524
  131.0 15.2 %collective-permute-start.6 = (bf16[4,4,16,1280]{3,2,1,0:T(8,128)(2,1)}, bf16[4,4,16,1280]{3,2,1,0:T(8,128)(2,1)S(1)}, u32[]{:S(2)}, u32[]{:S(2)}) collective-permute-start(bf16[4,4,16,1280]{3,2,1,0:T(8,128)(2,1)} %stack_tokens.1.refs_0_), channel_id=1, source_target_pairs={{0,24},{1,25},{2,26},{3,27},{4,28},{5,29},{6,30},{7,31},{8,0},{9,1... | collective-permute-start | bytes 1966088 | tf_op jit(solution)/shard_map/ppermute | solution.py:370
  131.8 16.5 %collective-permute-start.5 = (bf16[4,4,16,1280]{3,2,1,0:T(8,128)(2,1)}, bf16[4,4,16,1280]{3,2,1,0:T(8,128)(2,1)S(1)}, u32[]{:S(2)}, u32[]{:S(2)}) collective-permute-start(bf16[4,4,16,1280]{3,2,1,0:T(8,128)(2,1)} %stack_tokens.1.refs_0_), channel_id=1, source_target_pairs={{0,16},{1,17},{2,18},{3,19},{4,20},{5,21},{6,22},{7,23},{8,24},{9,... | collective-permute-start | bytes 1966088 | tf_op jit(solution)/shard_map/ppermute | solution.py:370
  133.1 31.3 %collective-permute-start.4 = (bf16[4,4,16,1280]{3,2,1,0:T(8,128)(2,1)}, bf16[4,4,16,1280]{3,2,1,0:T(8,128)(2,1)}, u32[]{:S(2)}, u32[]{:S(2)}) collective-permute-start(bf16[4,4,16,1280]{3,2,1,0:T(8,128)(2,1)} %stack_tokens.1.refs_0_), channel_id=1, source_target_pairs={{0,8},{1,9},{2,10},{3,11},{4,12},{5,13},{6,14},{7,15},{8,16},{9,17... | collective-permute-start | bytes 1966088 | tf_op jit(solution)/shard_map/ppermute | solution.py:370
  146.2 25.2 %copy-start.2 = (bf16[4,4,16,1280]{3,2,1,0:T(8,128)(2,1)}, bf16[4,4,16,1280]{3,2,1,0:T(8,128)(2,1)S(1)}, u32[]{:S(2)}) copy-start(bf16[4,4,16,1280]{3,2,1,0:T(8,128)(2,1)S(1)} %collective-permute-done.6.refs_3_) | copy-start | bytes 1966084
  164.4 7.0 %collective-permute-start.7 = (bf16[4,4,16,1280]{3,2,1,0:T(8,128)(2,1)}, bf16[4,4,16,1280]{3,2,1,0:T(8,128)(2,1)}, u32[]{:S(2)}, u32[]{:S(2)}) collective-permute-start(bf16[4,4,16,1280]{3,2,1,0:T(8,128)(2,1)} %stack_tokens.1.refs_0_), channel_id=1, source_target_pairs={{0,1},{1,0},{2,3},{3,2},{4,5},{5,4},{6,7},{7,6},{8,9},{9,8},{10,11... | collective-permute-start | bytes 1966088 | tf_op jit(solution)/shard_map/ppermute | solution.py:374
  164.9 6.5 %collective-permute-start.8 = (bf16[4,4,16,1280]{3,2,1,0:T(8,128)(2,1)}, bf16[4,4,16,1280]{3,2,1,0:T(8,128)(2,1)}, u32[]{:S(2)}, u32[]{:S(2)}) collective-permute-start(bf16[4,4,16,1280]{3,2,1,0:T(8,128)(2,1)} %collective-permute-done.4.refs_1_), channel_id=1, source_target_pairs={{0,1},{1,0},{2,3},{3,2},{4,5},{5,4},{6,7},{7,6},{8,9},{9,8},{10,11... | collective-permute-start | bytes 1966088 | tf_op jit(solution)/shard_map/ppermute | solution.py:374
  165.0 6.4 %collective-permute-start.9 = (bf16[4,4,16,1280]{3,2,1,0:T(8,128)(2,1)}, bf16[4,4,16,1280]{3,2,1,0:T(8,128)(2,1)}, u32[]{:S(2)}, u32[]{:S(2)}) collective-permute-start(bf16[4,4,16,1280]{3,2,1,0:T(8,128)(2,1)} %copy-done.3), channel_id=1, source_target_pairs={{0,1},{1,0},{2,3},{3,2},{4,5},{5,4},{6,7},{7,6},{8,9},{9,8},{10,11... | collective-permute-start | bytes 1966088 | tf_op jit(solution)/shard_map/ppermute | solution.py:374
  165.4 6.0 %collective-permute-start.10 = (bf16[4,4,16,1280]{3,2,1,0:T(8,128)(2,1)S(1)}, bf16[4,4,16,1280]{3,2,1,0:T(8,128)(2,1)}, u32[]{:S(2)}, u32[]{:S(2)}) collective-permute-start(bf16[4,4,16,1280]{3,2,1,0:T(8,128)(2,1)S(1)} %collective-permute-done.6.refs_3_), channel_id=1, source_target_pairs={{0,1},{1,0},{2,3},{3,2},{4,5},{5,4},{6,7},{7,6},{8,9},{9,8},{10,11... | collective-permute-start | bytes 1966088 | tf_op jit(solution)/shard_map/ppermute | solution.py:374
  177.6 22.9 %all-to-all-start.3 = ((bf16[8,320,256]{2,1,0:T(8,128)(2,1)}), bf16[8,320,256]{2,1,0:T(8,128)(2,1)S(1)}, u32[]{:S(2)}, u32[]{:S(2)}) async-start(bf16[8,320,256]{2,1,0:T(8,128)(2,1)} %forward_terms.1), calls=%async_computation.3 | async-start | bytes 2621440 | tf_op jit(solution)/shard_map/all_to_all | solution.py:353
  201.1 20.5 %copy-start.8 = (bf16[320,256]{1,0:T(8,128)(2,1)}, bf16[320,256]{1,0:T(8,128)(2,1)S(1)}, u32[]{:S(2)}) copy-start(bf16[320,256]{1,0:T(8,128)(2,1)S(1)} %fusion.6.refs_8_) | copy-start | bytes 491524
  201.1 7.1 %collective-permute-start.17 = (bf16[320,256]{1,0:T(8,128)(2,1)S(1)}, bf16[320,256]{1,0:T(8,128)(2,1)S(1)}, u32[]{:S(2)}, u32[]{:S(2)}) collective-permute-start(bf16[320,256]{1,0:T(8,128)(2,1)S(1)} %fusion.6.refs_8_), channel_id=1, source_target_pairs={{0,224},{32,192},{64,160},{96,128},{128,96},{160,64},{192,32},{224... | collective-permute-start | bytes 491528 | tf_op jit(solution)/shard_map/ppermute | solution.py:329
  203.6 8.3 %collective-permute-start.16 = (bf16[320,256]{1,0:T(8,128)(2,1)S(1)}, bf16[320,256]{1,0:T(8,128)(2,1)S(1)}, u32[]{:S(2)}, u32[]{:S(2)}) collective-permute-start(bf16[320,256]{1,0:T(8,128)(2,1)S(1)} %fusion.6.refs_8_), channel_id=1, source_target_pairs={{0,192},{32,224},{64,128},{96,160},{128,64},{160,96},{192,0},{224,... | collective-permute-start | bytes 491528 | tf_op jit(solution)/shard_map/ppermute | solution.py:329
  203.9 10.1 %collective-permute-start.15 = (bf16[320,256]{1,0:T(8,128)(2,1)S(1)}, bf16[320,256]{1,0:T(8,128)(2,1)S(1)}, u32[]{:S(2)}, u32[]{:S(2)}) collective-permute-start(bf16[320,256]{1,0:T(8,128)(2,1)S(1)} %fusion.6.refs_8_), channel_id=1, source_target_pairs={{0,160},{32,128},{64,224},{96,192},{128,32},{160,0},{192,96},{224,... | collective-permute-start | bytes 491528 | tf_op jit(solution)/shard_map/ppermute | solution.py:329
  206.3 11.5 %collective-permute-start.14 = (bf16[320,256]{1,0:T(8,128)(2,1)S(1)}, bf16[320,256]{1,0:T(8,128)(2,1)S(1)}, u32[]{:S(2)}, u32[]{:S(2)}) collective-permute-start(bf16[320,256]{1,0:T(8,128)(2,1)S(1)} %fusion.6.refs_8_), channel_id=1, source_target_pairs={{0,128},{32,160},{64,192},{96,224},{128,0},{160,32},{192,64},{224,... | collective-permute-start | bytes 491528 | tf_op jit(solution)/shard_map/ppermute | solution.py:329
  206.6 12.8 %collective-permute-start.13 = (bf16[320,256]{1,0:T(8,128)(2,1)S(1)}, bf16[320,256]{1,0:T(8,128)(2,1)S(1)}, u32[]{:S(2)}, u32[]{:S(2)}) collective-permute-start(bf16[320,256]{1,0:T(8,128)(2,1)S(1)} %fusion.6.refs_8_), channel_id=1, source_target_pairs={{0,96},{32,64},{64,32},{96,0},{128,224},{160,192},{192,160},{224,1... | collective-permute-start | bytes 491528 | tf_op jit(solution)/shard_map/ppermute | solution.py:329
  208.3 13.3 %copy-start.9 = (bf16[320,256]{1,0:T(8,128)(2,1)}, bf16[320,256]{1,0:T(8,128)(2,1)S(1)}, u32[]{:S(2)}) copy-start(bf16[320,256]{1,0:T(8,128)(2,1)S(1)} %collective-permute-done.17.refs_15_) | copy-start | bytes 491524
  208.3 11.1 %collective-permute-start.12 = (bf16[320,256]{1,0:T(8,128)(2,1)S(1)}, bf16[320,256]{1,0:T(8,128)(2,1)S(1)}, u32[]{:S(2)}, u32[]{:S(2)}) collective-permute-start(bf16[320,256]{1,0:T(8,128)(2,1)S(1)} %fusion.6.refs_8_), channel_id=1, source_target_pairs={{0,64},{32,96},{64,0},{96,32},{128,192},{160,224},{192,128},{224,1... | collective-permute-start | bytes 491528 | tf_op jit(solution)/shard_map/ppermute | solution.py:329
  211.9 9.7 %copy-start.10 = (bf16[320,256]{1,0:T(8,128)(2,1)}, bf16[320,256]{1,0:T(8,128)(2,1)S(1)}, u32[]{:S(2)}) copy-start(bf16[320,256]{1,0:T(8,128)(2,1)S(1)} %collective-permute-done.16.refs_14_) | copy-start | bytes 491524
  211.9 9.7 %collective-permute-start.11 = (bf16[320,256]{1,0:T(8,128)(2,1)S(1)}, bf16[320,256]{1,0:T(8,128)(2,1)S(1)}, u32[]{:S(2)}, u32[]{:S(2)}) collective-permute-start(bf16[320,256]{1,0:T(8,128)(2,1)S(1)} %fusion.6.refs_8_), channel_id=1, source_target_pairs={{0,32},{32,0},{64,96},{96,64},{128,160},{160,128},{192,224},{224,1... | collective-permute-start | bytes 491528 | tf_op jit(solution)/shard_map/ppermute | solution.py:329
  213.9 7.7 %copy-start.11 = (bf16[320,256]{1,0:T(8,128)(2,1)}, bf16[320,256]{1,0:T(8,128)(2,1)S(1)}, u32[]{:S(2)}) copy-start(bf16[320,256]{1,0:T(8,128)(2,1)S(1)} %collective-permute-done.15.refs_13_) | copy-start | bytes 491524
  (7 other events, 13.7 us)

commit v2 on v1

--- a/solution.py
+++ b/solution.py
@@ -43,7 +43,7 @@
     return jnp.dot(a, b, preferred_element_type=F32)
 
 
-def column_kernel(slabs_step, copy_ref, own_ref, place_ref, w_ref, m_ref, v_ref, out_ref, total, own_place):
+def column_kernel(slabs_step, piece, copy_ref, own_ref, place_ref, w_ref, m_ref, v_ref, out_ref, total, own_place):
     step = pl.program_id(0)
     rows, depth = w_ref.shape
     parts = [w_ref[...], m_ref[...].astype(BF16), v_ref[...].astype(BF16)]
@@ -73,13 +73,21 @@
     def _():
         half = out_ref.shape[0] // 2
         width = total.shape[1]
+        window = 2 * LANES
         held = [total[k * rows : (k + 1) * rows, :].astype(BF16) for k in range(3)]
-        spread = functools.reduce(
-            lambda a, b: a + b,
-            [dot(part, chosen(place_ref[k : k + 1, :], width)) for k, part in enumerate(held)],
-        ).astype(BF16)
-        for j in range(half):
-            out_ref[half + j] = spread[:, j * LANES : (j + 1) * LANES]
+        starts = [min(j * piece // LANES * LANES, width - window) for j in range(half)]
+        for start in sorted(set(starts)):
+            slabs = [j for j in range(half) if starts[j] == start]
+            lanes = slice(slabs[0] * LANES, (slabs[-1] + 1) * LANES)
+            spread = functools.reduce(
+                lambda a, b: a + b,
+                [
+                    dot(part[:, start : start + window], chosen(place_ref[k : k + 1, lanes], window, start))
+                    for k, part in enumerate(held)
+                ],
+            ).astype(BF16)
+            for i, j in enumerate(slabs):
+                out_ref[half + j] = spread[:, i * LANES : (i + 1) * LANES]
 
 
 def grow_columns(old_weight, old_first, old_second, col_source, slabs, slab_width, pieces, piece_at):
@@ -101,7 +109,7 @@
     own_index = spread_index(slabs_step, slab_width, piece_at * piece)
     place_index = spread_index(half, piece, 0)
     return pl.pallas_call(
-        functools.partial(column_kernel, slabs_step),
+        functools.partial(column_kernel, slabs_step, piece),
         grid=(half // slabs_step,),
         in_specs=[
             pl.BlockSpec((1, half * piece), lambda s: (0, 0)),
@@ -199,12 +207,13 @@
     step = pl.program_id(0)
     half = pl.num_programs(0)
     core = place_ref[1]
-    count = len(parts) // 2
-    for refs_of, at in ((parts[:count], core), (parts[count:], 1 - core)):
-        group = jnp.concatenate([ref[...].reshape(-1, ref.shape[-1]) for ref in refs_of], axis=0)
-        out_ref[at * half + step] = lax.dot_general(
-            weight_ref[...], group, (((1,), (1,)), ((), ())), preferred_element_type=F32
-        ).astype(BF16)
+    both = [ref[...].reshape(-1, ref.shape[-1]) for ref in parts]
+    term = lax.dot_general(
+        weight_ref[...], jnp.concatenate(both, axis=0), (((1,), (1,)), ((), ())), preferred_element_type=F32
+    ).astype(BF16)
+    width = out_ref.shape[2]
+    out_ref[core * half + step] = term[:, :width]
+    out_ref[(1 - core) * half + step] = term[:, width:]
 
 
 def forward(place, parts, weight, groups):
@@ -238,12 +247,12 @@
         for k, ref in enumerate(grads):
             held[jnp.bitwise_xor(place_ref[0], k)] = ref[...]
 
-    gradient = None
+    grads_in_order, groups_in_order = [], []
     for refs_of, at in ((parts[:count], core), (parts[count:], 1 - core)):
         for j in range(half):
-            group = jnp.concatenate([ref[:, j].reshape(-1, step_rows) for ref in refs_of], axis=0)
-            term = dot(held[at * half + j], group)
-            gradient = term if gradient is None else gradient + term
+            grads_in_order.append(held[at * half + j])
+            groups_in_order += [ref[:, j].reshape(-1, step_rows) for ref in refs_of]
+    gradient = dot(jnp.concatenate(grads_in_order, axis=1), jnp.concatenate(groups_in_order, axis=0))
     weight = weight_ref[...].astype(F32)
     new_first = beta_one * first_ref[...].astype(F32) + (1.0 - beta_one) * gradient
     new_second = beta_two * second_ref[...].astype(F32) + (1.0 - beta_two) * gradient * gradient
@@ -355,22 +364,30 @@
     chip_at = slab_at // 2
     lane = jnp.arange(slabs * rows, dtype=jnp.int32)
     away, within = lane // (2 * rows), lane % (2 * rows)
-    chip_x = (chip_at // DIM_Z - away // DIM_Z) % DIM_X
-    chip_z = (chip_at % DIM_Z - away % DIM_Z) % DIM_Z
+    part_at, within_part = away // (DIM_Z // 2), away % (DIM_Z // 2)
+    chip_x = (chip_at // DIM_Z - part_at % DIM_X) % DIM_X
+    chip_z = (chip_at % DIM_Z - within_part - part_at // DIM_X * (DIM_Z // 2)) % DIM_Z
     real = (chip_x * DIM_Z + chip_z) * 2 * rows + within
     to_real = (real[:, None] == lane[None, :]).astype(BF16)
 
     part = lax.all_to_all(tokens, "dp", split_axis=1, concat_axis=0, tiled=True)
+    chip = chip_tokens(part.reshape(groups, rows, block_rows), core)
+    old_weight, chip = in_order(old_weight, chip)
+    along_z = [chip] + [lax.ppermute(chip, "tensor", shifted(0, k, 0)) for k in range(1, DIM_Z)]
     columns = grow_columns(old_weight, old_first, old_second, col_source, slabs, slab_width, groups, group_at)
-    part, columns = in_order(part, columns)
+    columns, *along_z = in_order(columns, *along_z)
     columns = exchange(columns, "tensor")
-    chip = chip_tokens(part.reshape(groups, rows, block_rows), core)
-    along_z = [chip] + [lax.ppermute(chip, "tensor", shifted(0, k, 0)) for k in range(1, DIM_Z)]
-    along_z = stacked(along_z)
-    own = [along_z] + [lax.ppermute(along_z, "tensor", shifted(k, 0, 0)) for k in range(1, DIM_X)]
+
+    def along_x(values):
+        return [values] + [lax.ppermute(values, "tensor", shifted(k, 0, 0)) for k in range(1, DIM_X)]
+
+    near = along_x(stacked(along_z[: DIM_Z // 2]))
+    columns, row_scale, col_scale, place, *near = in_order(columns, row_scale, col_scale, place, *near)
+    far = along_x(stacked(along_z[DIM_Z // 2 :]))
     grown = grow_rows(columns.reshape(old_width, LANES), row_source)
     blocks = exchange(grown.reshape(groups, block_rows, LANES), "dp")
-    blocks, *own = in_order(blocks, *own)
+    blocks, *far = in_order(blocks, *far)
+    own = near + far
     parts = own + [lax.ppermute(values, "tensor", shifted(0, 0, 1)) for values in own]
     (weight,) = grown_block(weight_kernel, (blocks, row_scale, col_scale), 1, block_rows, slab_width, piece)
 

time: 232 us -> 193 us (0.83)
  blocking collectives: 42.4 us -> 0 us
  starting transfers between devices: 37.4 us -> 56.5 us
  waiting for transfers between devices: 94.7 us -> 76.7 us
    all_to_all x1 -> x0, blocking collectives: 42.4 us -> none  [exchange(): return lax.all_to_all(values, axis, split_axis=0, concat_axis=0, tiled=True)]
    ppermute x3, waiting for transfers between devices: 38.5 us -> 0.01 us  [shards(): lax.ppermute(chip, 'tensor', shifted(0, k, 0))]
    all_to_all x2 -> x3, waiting for transfers between devices: 13.2 us -> 24 us  [exchange(): return lax.all_to_all(values, axis, split_axis=0, concat_axis=0, tiled=True)]
    ppermute x4 -> x8, starting transfers between devices: 1.1 us -> 7.98 us  [shards(): lax.ppermute(values, 'tensor', shifted(0, 0, 1))]
    ppermute x3 -> x6, waiting for transfers between devices: 30.4 us -> 36.3 us  [along_x(): lax.ppermute(values, 'tensor', shifted(k, 0, 0))]
    all_to_all x1, waiting for transfers between devices: 0.01 us -> 4.75 us  [shards(): part = lax.all_to_all(tokens, 'dp', split_axis=1, concat_axis=0, tiled=True)]
    ppermute x3, starting transfers between devices: 3.96 us -> 8.45 us  [shards(): lax.ppermute(chip, 'tensor', shifted(0, k, 0))]
    ppermute x3 -> x6, starting transfers between devices: 2.12 us -> 5.8 us  [along_x(): lax.ppermute(values, 'tensor', shifted(k, 0, 0))]
  transfers between devices with their start and end apart: 21 -> 29, of which waited for: 14 -> 14; matrix products, arithmetic and copies ran while one was open for 3% -> 3% of each run, Pallas kernels for 10% -> 13%
where the time goes in v2:
time: 193 us; the launch traced here: 192 us
  waiting for transfers between devices  76.7 us (40%)
  starting transfers between devices  56.5 us (29%)
  Pallas kernels  47.2 us (24%)
  local copies, waits for them, and re-layouts  7.07 us (4%)
  other arithmetic  2.24 us (1%)
    ppermute x6, waiting for transfers between devices, along_x(): lax.ppermute(values, 'tensor', shifted(k, 0, 0))  36.3 us
    all_to_all x3, waiting for transfers between devices, exchange(): return lax.all_to_all(values, axis, split_axis=0, concat_axis=0, tiled=True)  24 us
    all_to_all x3, starting transfers between devices, exchange(): return lax.all_to_all(values, axis, split_axis=0, concat_axis=0, tiled=True)  17.9 us
    pallas_call x1, Pallas kernels, grow_columns(): pl.pallas_call(functools.partial(column_kernel, slabs_step, piece), grid=...  12.3 us
    ppermute x7, waiting for transfers between devices, to_groups(): lax.ppermute(values, 'dp', [(i, i ^ k) for i in range(groups)])  11.6 us
    pallas_call x1, Pallas kernels, backward(): pl.pallas_call(functools.partial(adam_kernel, len(grads)), grid=(block_ro...  8.78 us
    ppermute x3, starting transfers between devices, shards(): lax.ppermute(chip, 'tensor', shifted(0, k, 0))  8.45 us
    pallas_call x2, Pallas kernels, grown_block(): pl.pallas_call(functools.partial(kernel, piece), in_specs=[pl.BlockSpec(m...  8.27 us
  transfers between devices with their start and end apart: 29, of which 14 were waited for; matrix products, arithmetic and copies ran while one was open for 3% of the time, Pallas kernels for 13%

profile of v2, /device:TPU:1, one launch (start us, length us, event | category | flops | bytes accessed | tf_op | source)
XLA Modules:
  0.0 192.2 jit_solution(4285614098870418194)
XLA Ops:
  0.6 6.5 %all-to-all-start = ((bf16[8,8,1280]{2,0,1:T(8,128)(2,1)}), bf16[8,8,1280]{2,0,1:T(8,128)(2,1)S(1)}, u32[]{:S(2)}, u32[]{:S(2)}) async-start(bf16[8,8,1280]{2,0,1:T(8,128)(2,1)} %bitcast.54), calls=%async_computation | async-start | bytes 327680 | tf_op jit(solution)/shard_map/all_to_all | solution.py:373
  8.1 4.8 %all-to-all-done = bf16[8,8,1280]{2,0,1:T(8,128)(2,1)S(1)} async-done(((bf16[8,8,1280]{2,0,1:T(8,128)(2,1)}), bf16[8,8,1280]{2,0,1:T(8,128)(2,1)S(1)}, u32[]{:S(2)}, u32[]{:S(2)}) %all-to-all-start) | async-done | bytes 163872 | tf_op jit(solution)/shard_map/all_to_all | solution.py:373
  12.8 2.1 %collective-permute-start = (bf16[4,8,1280]{2,1,0:T(8,128)(2,1)S(1)}, bf16[4,8,1280]{2,1,0:T(8,128)(2,1)S(1)}, u32[]{:S(2)}, u32[]{:S(2)}) collective-permute-start(bf16[4,8,1280]{2,1,0:T(8,128)(2,1)S(1)} %dynamic-slice_bitcast_fusion), channel_id=1, source_target_pairs={{0,1},{1,0},{2,3},{3,2},{4,5},{5,4},{6,7},{7,6},{8,9},{9,8},{10,11... | collective-permute-start | bytes 245768 | tf_op jit(solution)/shard_map/ppermute | solution.py:331
  16.6 5.2 %collective-permute-start.3 = (bf16[1,4,16,1280]{3,2,1,0:T(8,128)(2,1)S(1)}, bf16[1,4,16,1280]{3,2,1,0:T(8,128)(2,1)S(1)}, u32[]{:S(2)}, u32[]{:S(2)}) collective-permute-start(bf16[1,4,16,1280]{3,2,1,0:T(8,128)(2,1)S(1)} %maximum_bitcast_fusion.refs_0_), channel_id=1, source_target_pairs={{0,6},{1,7},{2,0},{3,1},{4,2},{5,3},{6,4},{7,5},{8,14},{9,15},{10,... | collective-permute-start | bytes 491528 | tf_op jit(solution)/shard_map/ppermute | solution.py:376
  22.9 2.1 %collective-permute-start.1 = (bf16[1,4,16,1280]{3,2,1,0:T(8,128)(2,1)S(1)}, bf16[1,4,16,1280]{3,2,1,0:T(8,128)(2,1)S(1)}, u32[]{:S(2)}, u32[]{:S(2)}) collective-permute-start(bf16[1,4,16,1280]{3,2,1,0:T(8,128)(2,1)S(1)} %maximum_bitcast_fusion.refs_0_), channel_id=1, source_target_pairs={{0,2},{1,3},{2,4},{3,5},{4,6},{5,7},{6,0},{7,1},{8,10},{9,11},{10,... | collective-permute-start | bytes 491528 | tf_op jit(solution)/shard_map/ppermute | solution.py:376
  25.6 12.3 %grow_columns.1 = bf16[32,160,128]{2,1,0:T(8,128)(2,1)} custom-call(s32[1,640]{1,0:T(1,128)} %reshape.193.copy_ref, s32[3,256]{1,0:T(4,128)} %fusion.12.own_ref, s32[3,2048]{1,0:T(4,128)} %fusion.11.place_ref, bf16[160,5120]{1,0:T(8,128)(2,1)} %w_ref, f32[160,5120]{1,0:T(8,128)} %m_ref.1, f32[160,5120]{1,0:T(8,128)} %v_ref.1), custom_call_target="tpu_custom_call" | custom-call | flops 1000 | bytes 1000 | tf_op jit(solution)/shard_map/grow_columns/pallas_call | solution.py:111
  39.3 8.9 %all-to-all-start.1 = ((bf16[32,160,128]{2,1,0:T(8,128)(2,1)}), bf16[32,160,128]{2,1,0:T(8,128)(2,1)S(1)}, u32[]{:S(2)}, u32[]{:S(2)}) async-start(bf16[32,160,128]{2,1,0:T(8,128)(2,1)} %grow_columns.1), calls=%async_computation.1 | async-start | bytes 2621440 | tf_op jit(solution)/shard_map/all_to_all | solution.py:362
  48.2 1.8 stack_tokens.2.refs_0_
  50.0 2.6 %collective-permute-start.6 = (bf16[2,4,16,1280]{3,2,1,0:T(8,128)(2,1)}, bf16[2,4,16,1280]{3,2,1,0:T(8,128)(2,1)S(1)}, u32[]{:S(2)}, u32[]{:S(2)}) collective-permute-start(bf16[2,4,16,1280]{3,2,1,0:T(8,128)(2,1)} %stack_tokens.2.refs_0_), channel_id=1, source_target_pairs={{0,24},{1,25},{2,26},{3,27},{4,28},{5,29},{6,30},{7,31},{8,0},{9,1... | collective-permute-start | bytes 983048 | tf_op jit(solution)/shard_map/ppermute | solution.py:382
  55.1 11.5 %collective-permute-done.6.refs_3_ = bf16[2,4,16,1280]{3,2,1,0:T(8,128)(2,1)S(1)} collective-permute-done((bf16[2,4,16,1280]{3,2,1,0:T(8,128)(2,1)}, bf16[2,4,16,1280]{3,2,1,0:T(8,128)(2,1)S(1)}, u32[]{:S(2)}, u32[]{:S(2)}) %collective-permute-start.6) | collective-permute-done | bytes 327712 | tf_op jit(solution)/shard_map/ppermute | solution.py:382
  66.6 5.2 %collective-permute-done.5.refs_2_ = bf16[2,4,16,1280]{3,2,1,0:T(8,128)(2,1)S(1)} collective-permute-done((bf16[2,4,16,1280]{3,2,1,0:T(8,128)(2,1)}, bf16[2,4,16,1280]{3,2,1,0:T(8,128)(2,1)S(1)}, u32[]{:S(2)}, u32[]{:S(2)}) %collective-permute-start.5) | collective-permute-done | bytes 327712 | tf_op jit(solution)/shard_map/ppermute | solution.py:382
  71.9 9.1 %collective-permute-done.4.refs_1_ = bf16[2,4,16,1280]{3,2,1,0:T(8,128)(2,1)S(1)} collective-permute-done((bf16[2,4,16,1280]{3,2,1,0:T(8,128)(2,1)}, bf16[2,4,16,1280]{3,2,1,0:T(8,128)(2,1)S(1)}, u32[]{:S(2)}, u32[]{:S(2)}) %collective-permute-start.4) | collective-permute-done | bytes 327712 | tf_op jit(solution)/shard_map/ppermute | solution.py:382
  82.1 8.1 %grow_rows.1 = bf16[10240,128]{1,0:T(8,128)(2,1)} custom-call(s32[5120]{0:T(1024)} %index_ref.1, bf16[5120,128]{1,0:T(8,128)(2,1)} %bitcast.53), custom_call_target="tpu_custom_call" | custom-call | flops 1000 | bytes 1000 | tf_op jit(solution)/shard_map/grow_rows/pallas_call | solution.py:155
  90.1 5.5 %all-to-all-start.2 = ((bf16[8,1280,128]{2,1,0:T(8,128)(2,1)}), bf16[8,1280,128]{2,1,0:T(8,128)(2,1)S(1)}, u32[]{:S(2)}, u32[]{:S(2)}) async-start(bf16[8,1280,128]{2,1,0:T(8,128)(2,1)} %bitcast.52), calls=%async_computation.2 | async-start | bytes 5242880 | tf_op jit(solution)/shard_map/all_to_all | solution.py:362
  95.6 1.7 stack_tokens.3.refs_4_
  100.4 5.6 %collective-permute-done.9.refs_7_ = bf16[2,4,16,1280]{3,2,1,0:T(8,128)(2,1)S(1)} collective-permute-done((bf16[2,4,16,1280]{3,2,1,0:T(8,128)(2,1)}, bf16[2,4,16,1280]{3,2,1,0:T(8,128)(2,1)S(1)}, u32[]{:S(2)}, u32[]{:S(2)}) %collective-permute-start.9) | collective-permute-done | bytes 327712 | tf_op jit(solution)/shard_map/ppermute | solution.py:382
  106.0 3.1 %collective-permute-start.12 = (bf16[2,4,16,1280]{3,2,1,0:T(8,128)(2,1)}, bf16[2,4,16,1280]{3,2,1,0:T(8,128)(2,1)}, u32[]{:S(2)}, u32[]{:S(2)}) collective-permute-start(bf16[2,4,16,1280]{3,2,1,0:T(8,128)(2,1)} %copy-done.5), channel_id=1, source_target_pairs={{0,1},{1,0},{2,3},{3,2},{4,5},{5,4},{6,7},{7,6},{8,9},{9,8},{10,11... | collective-permute-start | bytes 983048 | tf_op jit(solution)/shard_map/ppermute | solution.py:391
  109.1 2.4 %collective-permute-start.13 = (bf16[2,4,16,1280]{3,2,1,0:T(8,128)(2,1)S(1)}, bf16[2,4,16,1280]{3,2,1,0:T(8,128)(2,1)}, u32[]{:S(2)}, u32[]{:S(2)}) collective-permute-start(bf16[2,4,16,1280]{3,2,1,0:T(8,128)(2,1)S(1)} %collective-permute-done.6.refs_3_), channel_id=1, source_target_pairs={{0,1},{1,0},{2,3},{3,2},{4,5},{5,4},{6,7},{7,6},{8,9},{9,8},{10,11... | collective-permute-start | bytes 983048 | tf_op jit(solution)/shard_map/ppermute | solution.py:391
  111.5 4.9 %collective-permute-done.7.refs_5_ = bf16[2,4,16,1280]{3,2,1,0:T(8,128)(2,1)} collective-permute-done((bf16[2,4,16,1280]{3,2,1,0:T(8,128)(2,1)}, bf16[2,4,16,1280]{3,2,1,0:T(8,128)(2,1)}, u32[]{:S(2)}, u32[]{:S(2)}) %collective-permute-start.7) | collective-permute-done | bytes 327712 | tf_op jit(solution)/shard_map/ppermute | solution.py:382
  116.4 10.9 %all-to-all-done.2.blocks_ref = bf16[8,1280,128]{2,1,0:T(8,128)(2,1)S(1)} async-done(((bf16[8,1280,128]{2,1,0:T(8,128)(2,1)}), bf16[8,1280,128]{2,1,0:T(8,128)(2,1)S(1)}, u32[]{:S(2)}, u32[]{:S(2)}) %all-to-all-start.2) | async-done | bytes 2621472 | tf_op jit(solution)/shard_map/all_to_all | solution.py:362
  129.6 3.7 %grown_block_1.1.refs_16_.refs_26_ = bf16[320,1280]{1,0:T(8,128)(2,1)} custom-call(bf16[8,1280,128]{2,1,0:T(8,128)(2,1)} %copy-done.1, f32[1,1280]{1,0:T(1,128)} %broadcast_in_dim.50.row_scale_ref, f32[320,1]{1,0:T(8,128)} %copy.15.col_scale_ref), custom_call_target="tpu_custom_call" | custom-call | flops 1000 | bytes 1000 | tf_op jit(solution)/shard_map/grown_block_1/pallas_call | solution.py:194
  134.1 6.2 %forward_terms.1 = bf16[8,320,256]{2,1,0:T(8,128)(2,1)} custom-call(s32[2]{0:T(128)} %pad_add_fusion.place_ref, bf16[2,4,16,1280]{3,2,1,0:T(8,128)(2,1)} %stack_tokens.2.refs_0_, bf16[2,4,16,1280]{3,2,1,0:T(8,128)(2,1)} %copy-done.6, bf16[2,4,16,1280]{3,2,1,0:T(8,128)(2,1)} %copy-done.5, bf16[2,4,16,1280]{3,2,1,0:T(8,128)(2,1)} %copy-done.4, ...), custom_call_target="tpu_custom_call" | custom-call | flops 1000 | bytes 1000 | tf_op jit(solution)/shard_map/forward_terms/pallas_call | solution.py:223
  140.3 3.6 %all-to-all-start.3 = ((bf16[8,320,256]{2,1,0:T(8,128)(2,1)}), bf16[8,320,256]{2,1,0:T(8,128)(2,1)S(1)}, u32[]{:S(2)}, u32[]{:S(2)}) async-start(bf16[8,320,256]{2,1,0:T(8,128)(2,1)} %forward_terms.1), calls=%async_computation.3 | async-start | bytes 2621440 | tf_op jit(solution)/shard_map/all_to_all | solution.py:362
  144.0 4.6 %grown_block_2.1 = (bf16[320,1280]{1,0:T(8,128)(2,1)}, bf16[320,1280]{1,0:T(8,128)(2,1)}) custom-call(bf16[8,1280,128]{2,1,0:T(8,128)(2,1)} %copy-done.1), custom_call_target="tpu_custom_call" | custom-call | flops 1000 | bytes 1000 | tf_op jit(solution)/shard_map/grown_block_2/pallas_call | solution.py:194
  148.5 13.1 %all-to-all-done.3 = bf16[8,320,256]{2,1,0:T(8,128)(2,1)S(1)} async-done(((bf16[8,320,256]{2,1,0:T(8,128)(2,1)}), bf16[8,320,256]{2,1,0:T(8,128)(2,1)S(1)}, u32[]{:S(2)}, u32[]{:S(2)}) %all-to-all-start.3) | async-done | bytes 1310752 | tf_op jit(solution)/shard_map/all_to_all | solution.py:362
  162.2 2.4 %collective-permute-start.24 = (bf16[320,256]{1,0:T(8,128)(2,1)S(1)}, bf16[320,256]{1,0:T(8,128)(2,1)S(1)}, u32[]{:S(2)}, u32[]{:S(2)}) collective-permute-start(bf16[320,256]{1,0:T(8,128)(2,1)S(1)} %fusion.6.refs_16_), channel_id=1, source_target_pairs={{0,224},{32,192},{64,160},{96,128},{128,96},{160,64},{192,32},{224... | collective-permute-start | bytes 491528 | tf_op jit(solution)/shard_map/ppermute | solution.py:338
  164.9 2.4 %collective-permute-start.22 = (bf16[320,256]{1,0:T(8,128)(2,1)S(1)}, bf16[320,256]{1,0:T(8,128)(2,1)S(1)}, u32[]{:S(2)}, u32[]{:S(2)}) collective-permute-start(bf16[320,256]{1,0:T(8,128)(2,1)S(1)} %fusion.6.refs_16_), channel_id=1, source_target_pairs={{0,160},{32,128},{64,224},{96,192},{128,32},{160,0},{192,96},{224,... | collective-permute-start | bytes 491528 | tf_op jit(solution)/shard_map/ppermute | solution.py:338
  170.0 2.9 %collective-permute-done.23.refs_22_ = bf16[320,256]{1,0:T(8,128)(2,1)S(1)} collective-permute-done((bf16[320,256]{1,0:T(8,128)(2,1)S(1)}, bf16[320,256]{1,0:T(8,128)(2,1)S(1)}, u32[]{:S(2)}, u32[]{:S(2)}) %collective-permute-start.23) | collective-permute-done | bytes 163872 | tf_op jit(solution)/shard_map/ppermute | solution.py:338
  175.0 3.9 %collective-permute-done.21.refs_20_ = bf16[320,256]{1,0:T(8,128)(2,1)S(1)} collective-permute-done((bf16[320,256]{1,0:T(8,128)(2,1)S(1)}, bf16[320,256]{1,0:T(8,128)(2,1)S(1)}, u32[]{:S(2)}, u32[]{:S(2)}) %collective-permute-start.21) | collective-permute-done | bytes 163872 | tf_op jit(solution)/shard_map/ppermute | solution.py:338
  178.9 1.6 collective-permute-done.20.refs_19_
  180.4 2.1 %collective-permute-done.18.refs_17_ = bf16[320,256]{1,0:T(8,128)(2,1)S(1)} collective-permute-done((bf16[320,256]{1,0:T(8,128)(2,1)S(1)}, bf16[320,256]{1,0:T(8,128)(2,1)S(1)}, u32[]{:S(2)}, u32[]{:S(2)}) %collective-permute-start.18) | collective-permute-done | bytes 163872 | tf_op jit(solution)/shard_map/ppermute | solution.py:338
  183.3 8.8 %gradient_adam.1 = (bf16[320,1280]{1,0:T(8,128)(2,1)}, f32[320,1280]{1,0:T(8,128)}, f32[320,1280]{1,0:T(8,128)}) custom-call(s32[2]{0:T(128)} %pad_add_fusion.place_ref, bf16[2,4,16,1280]{3,2,1,0:T(8,128)(2,1)} %stack_tokens.2.refs_0_, bf16[2,4,16,1280]{3,2,1,0:T(8,128)(2,1)} %copy-done.6, bf16[2,4,16,1280]{3,2,1,0:T(8,128)(2,1)} %copy-done.5, ...), custom_call_target="tpu_custom_call" | custom-call | flops 1000 | bytes 1000 | tf_op jit(solution)/shard_map/gradient_adam/pallas_call | solution.py:276
  (112 shorter events, 21.5 us)
Async XLA Ops:
  0.6 161.1 %copy-start = (bf16[256,320]{0,1:T(8,128)(2,1)S(1)}, bf16[256,320]{0,1:T(8,128)(2,1)}, u32[]{:S(2)}) copy-start(bf16[256,320]{0,1:T(8,128)(2,1)} %param.10) | copy-start | bytes 491524
  0.6 12.2 %all-to-all-start = ((bf16[8,8,1280]{2,0,1:T(8,128)(2,1)}), bf16[8,8,1280]{2,0,1:T(8,128)(2,1)S(1)}, u32[]{:S(2)}, u32[]{:S(2)}) async-start(bf16[8,8,1280]{2,0,1:T(8,128)(2,1)} %bitcast.54), calls=%async_computation | async-start | bytes 327680 | tf_op jit(solution)/shard_map/all_to_all | solution.py:373
  12.8 3.7 %collective-permute-start = (bf16[4,8,1280]{2,1,0:T(8,128)(2,1)S(1)}, bf16[4,8,1280]{2,1,0:T(8,128)(2,1)S(1)}, u32[]{:S(2)}, u32[]{:S(2)}) collective-permute-start(bf16[4,8,1280]{2,1,0:T(8,128)(2,1)S(1)} %dynamic-slice_bitcast_fusion), channel_id=1, source_target_pairs={{0,1},{1,0},{2,3},{3,2},{4,5},{5,4},{6,7},{7,6},{8,9},{9,8},{10,11... | collective-permute-start | bytes 245768 | tf_op jit(solution)/shard_map/ppermute | solution.py:331
  16.5 21.4 %copy-start.10 = (bf16[1,4,16,1280]{3,2,1,0:T(8,128)(2,1)}, bf16[1,4,16,1280]{3,2,1,0:T(8,128)(2,1)S(1)}, u32[]{:S(2)}) copy-start(bf16[1,4,16,1280]{3,2,1,0:T(8,128)(2,1)S(1)} %maximum_bitcast_fusion.refs_0_) | copy-start | bytes 491524
  16.6 21.4 %collective-permute-start.3 = (bf16[1,4,16,1280]{3,2,1,0:T(8,128)(2,1)S(1)}, bf16[1,4,16,1280]{3,2,1,0:T(8,128)(2,1)S(1)}, u32[]{:S(2)}, u32[]{:S(2)}) collective-permute-start(bf16[1,4,16,1280]{3,2,1,0:T(8,128)(2,1)S(1)} %maximum_bitcast_fusion.refs_0_), channel_id=1, source_target_pairs={{0,6},{1,7},{2,0},{3,1},{4,2},{5,3},{6,4},{7,5},{8,14},{9,15},{10,... | collective-permute-start | bytes 491528 | tf_op jit(solution)/shard_map/ppermute | solution.py:376
  21.8 16.2 %collective-permute-start.2 = (bf16[1,4,16,1280]{3,2,1,0:T(8,128)(2,1)S(1)}, bf16[1,4,16,1280]{3,2,1,0:T(8,128)(2,1)S(1)}, u32[]{:S(2)}, u32[]{:S(2)}) collective-permute-start(bf16[1,4,16,1280]{3,2,1,0:T(8,128)(2,1)S(1)} %maximum_bitcast_fusion.refs_0_), channel_id=1, source_target_pairs={{0,4},{1,5},{2,6},{3,7},{4,0},{5,1},{6,2},{7,3},{8,12},{9,13},{10,... | collective-permute-start | bytes 491528 | tf_op jit(solution)/shard_map/ppermute | solution.py:376
  22.9 16.4 %collective-permute-start.1 = (bf16[1,4,16,1280]{3,2,1,0:T(8,128)(2,1)S(1)}, bf16[1,4,16,1280]{3,2,1,0:T(8,128)(2,1)S(1)}, u32[]{:S(2)}, u32[]{:S(2)}) collective-permute-start(bf16[1,4,16,1280]{3,2,1,0:T(8,128)(2,1)S(1)} %maximum_bitcast_fusion.refs_0_), channel_id=1, source_target_pairs={{0,2},{1,3},{2,4},{3,5},{4,6},{5,7},{6,0},{7,1},{8,10},{9,11},{10,... | collective-permute-start | bytes 491528 | tf_op jit(solution)/shard_map/ppermute | solution.py:376
  39.3 41.7 %all-to-all-start.1 = ((bf16[32,160,128]{2,1,0:T(8,128)(2,1)}), bf16[32,160,128]{2,1,0:T(8,128)(2,1)S(1)}, u32[]{:S(2)}, u32[]{:S(2)}) async-start(bf16[32,160,128]{2,1,0:T(8,128)(2,1)} %grow_columns.1), calls=%async_computation.1 | async-start | bytes 2621440 | tf_op jit(solution)/shard_map/all_to_all | solution.py:362
  50.0 16.6 %collective-permute-start.6 = (bf16[2,4,16,1280]{3,2,1,0:T(8,128)(2,1)}, bf16[2,4,16,1280]{3,2,1,0:T(8,128)(2,1)S(1)}, u32[]{:S(2)}, u32[]{:S(2)}) collective-permute-start(bf16[2,4,16,1280]{3,2,1,0:T(8,128)(2,1)} %stack_tokens.2.refs_0_), channel_id=1, source_target_pairs={{0,24},{1,25},{2,26},{3,27},{4,28},{5,29},{6,30},{7,31},{8,0},{9,1... | collective-permute-start | bytes 983048 | tf_op jit(solution)/shard_map/ppermute | solution.py:382
  52.7 19.2 %collective-permute-start.5 = (bf16[2,4,16,1280]{3,2,1,0:T(8,128)(2,1)}, bf16[2,4,16,1280]{3,2,1,0:T(8,128)(2,1)S(1)}, u32[]{:S(2)}, u32[]{:S(2)}) collective-permute-start(bf16[2,4,16,1280]{3,2,1,0:T(8,128)(2,1)} %stack_tokens.2.refs_0_), channel_id=1, source_target_pairs={{0,16},{1,17},{2,18},{3,19},{4,20},{5,21},{6,22},{7,23},{8,24},{9,... | collective-permute-start | bytes 983048 | tf_op jit(solution)/shard_map/ppermute | solution.py:382
  53.2 27.8 %collective-permute-start.4 = (bf16[2,4,16,1280]{3,2,1,0:T(8,128)(2,1)}, bf16[2,4,16,1280]{3,2,1,0:T(8,128)(2,1)S(1)}, u32[]{:S(2)}, u32[]{:S(2)}) collective-permute-start(bf16[2,4,16,1280]{3,2,1,0:T(8,128)(2,1)} %stack_tokens.2.refs_0_), channel_id=1, source_target_pairs={{0,8},{1,9},{2,10},{3,11},{4,12},{5,13},{6,14},{7,15},{8,16},{9,17... | collective-permute-start | bytes 983048 | tf_op jit(solution)/shard_map/ppermute | solution.py:382
  66.6 42.5 %copy-start.4 = (bf16[2,4,16,1280]{3,2,1,0:T(8,128)(2,1)}, bf16[2,4,16,1280]{3,2,1,0:T(8,128)(2,1)S(1)}, u32[]{:S(2)}) copy-start(bf16[2,4,16,1280]{3,2,1,0:T(8,128)(2,1)S(1)} %collective-permute-done.6.refs_3_) | copy-start | bytes 983044
  90.1 37.2 %all-to-all-start.2 = ((bf16[8,1280,128]{2,1,0:T(8,128)(2,1)}), bf16[8,1280,128]{2,1,0:T(8,128)(2,1)S(1)}, u32[]{:S(2)}, u32[]{:S(2)}) async-start(bf16[8,1280,128]{2,1,0:T(8,128)(2,1)} %bitcast.52), calls=%async_computation.2 | async-start | bytes 5242880 | tf_op jit(solution)/shard_map/all_to_all | solution.py:362
  97.3 8.6 %collective-permute-start.9 = (bf16[2,4,16,1280]{3,2,1,0:T(8,128)(2,1)}, bf16[2,4,16,1280]{3,2,1,0:T(8,128)(2,1)S(1)}, u32[]{:S(2)}, u32[]{:S(2)}) collective-permute-start(bf16[2,4,16,1280]{3,2,1,0:T(8,128)(2,1)} %stack_tokens.3.refs_4_), channel_id=1, source_target_pairs={{0,24},{1,25},{2,26},{3,27},{4,28},{5,29},{6,30},{7,31},{8,0},{9,1... | collective-permute-start | bytes 983048 | tf_op jit(solution)/shard_map/ppermute | solution.py:382
  98.0 11.1 %collective-permute-start.8 = (bf16[2,4,16,1280]{3,2,1,0:T(8,128)(2,1)}, bf16[2,4,16,1280]{3,2,1,0:T(8,128)(2,1)S(1)}, u32[]{:S(2)}, u32[]{:S(2)}) collective-permute-start(bf16[2,4,16,1280]{3,2,1,0:T(8,128)(2,1)} %stack_tokens.3.refs_4_), channel_id=1, source_target_pairs={{0,16},{1,17},{2,18},{3,19},{4,20},{5,21},{6,22},{7,23},{8,24},{9,... | collective-permute-start | bytes 983048 | tf_op jit(solution)/shard_map/ppermute | solution.py:382
  99.3 17.2 %collective-permute-start.7 = (bf16[2,4,16,1280]{3,2,1,0:T(8,128)(2,1)}, bf16[2,4,16,1280]{3,2,1,0:T(8,128)(2,1)}, u32[]{:S(2)}, u32[]{:S(2)}) collective-permute-start(bf16[2,4,16,1280]{3,2,1,0:T(8,128)(2,1)} %stack_tokens.3.refs_4_), channel_id=1, source_target_pairs={{0,8},{1,9},{2,10},{3,11},{4,12},{5,13},{6,14},{7,15},{8,16},{9,17... | collective-permute-start | bytes 983048 | tf_op jit(solution)/shard_map/ppermute | solution.py:382
  99.4 28.8 %collective-permute-start.10 = (bf16[2,4,16,1280]{3,2,1,0:T(8,128)(2,1)S(1)}, bf16[2,4,16,1280]{3,2,1,0:T(8,128)(2,1)}, u32[]{:S(2)}, u32[]{:S(2)}) collective-permute-start(bf16[2,4,16,1280]{3,2,1,0:T(8,128)(2,1)S(1)} %copy-done.3), channel_id=1, source_target_pairs={{0,1},{1,0},{2,3},{3,2},{4,5},{5,4},{6,7},{7,6},{8,9},{9,8},{10,11... | collective-permute-start | bytes 983048 | tf_op jit(solution)/shard_map/ppermute | solution.py:391
  100.4 27.9 %collective-permute-start.11 = (bf16[2,4,16,1280]{3,2,1,0:T(8,128)(2,1)}, bf16[2,4,16,1280]{3,2,1,0:T(8,128)(2,1)}, u32[]{:S(2)}, u32[]{:S(2)}) collective-permute-start(bf16[2,4,16,1280]{3,2,1,0:T(8,128)(2,1)} %copy-done.6), channel_id=1, source_target_pairs={{0,1},{1,0},{2,3},{3,2},{4,5},{5,4},{6,7},{7,6},{8,9},{9,8},{10,11... | collective-permute-start | bytes 983048 | tf_op jit(solution)/shard_map/ppermute | solution.py:391
  106.0 22.8 %collective-permute-start.12 = (bf16[2,4,16,1280]{3,2,1,0:T(8,128)(2,1)}, bf16[2,4,16,1280]{3,2,1,0:T(8,128)(2,1)}, u32[]{:S(2)}, u32[]{:S(2)}) collective-permute-start(bf16[2,4,16,1280]{3,2,1,0:T(8,128)(2,1)} %copy-done.5), channel_id=1, source_target_pairs={{0,1},{1,0},{2,3},{3,2},{4,5},{5,4},{6,7},{7,6},{8,9},{9,8},{10,11... | collective-permute-start | bytes 983048 | tf_op jit(solution)/shard_map/ppermute | solution.py:391
  109.1 24.3 %collective-permute-start.13 = (bf16[2,4,16,1280]{3,2,1,0:T(8,128)(2,1)S(1)}, bf16[2,4,16,1280]{3,2,1,0:T(8,128)(2,1)}, u32[]{:S(2)}, u32[]{:S(2)}) collective-permute-start(bf16[2,4,16,1280]{3,2,1,0:T(8,128)(2,1)S(1)} %collective-permute-done.6.refs_3_), channel_id=1, source_target_pairs={{0,1},{1,0},{2,3},{3,2},{4,5},{5,4},{6,7},{7,6},{8,9},{9,8},{10,11... | collective-permute-start | bytes 983048 | tf_op jit(solution)/shard_map/ppermute | solution.py:391
  127.4 6.0 %collective-permute-start.14 = (bf16[2,4,16,1280]{3,2,1,0:T(8,128)(2,1)}, bf16[2,4,16,1280]{3,2,1,0:T(8,128)(2,1)}, u32[]{:S(2)}, u32[]{:S(2)}) collective-permute-start(bf16[2,4,16,1280]{3,2,1,0:T(8,128)(2,1)} %stack_tokens.3.refs_4_), channel_id=1, source_target_pairs={{0,1},{1,0},{2,3},{3,2},{4,5},{5,4},{6,7},{7,6},{8,9},{9,8},{10,11... | collective-permute-start | bytes 983048 | tf_op jit(solution)/shard_map/ppermute | solution.py:391
  128.2 5.1 %collective-permute-start.15 = (bf16[2,4,16,1280]{3,2,1,0:T(8,128)(2,1)}, bf16[2,4,16,1280]{3,2,1,0:T(8,128)(2,1)S(1)}, u32[]{:S(2)}, u32[]{:S(2)}) collective-permute-start(bf16[2,4,16,1280]{3,2,1,0:T(8,128)(2,1)} %collective-permute-done.7.refs_5_), channel_id=1, source_target_pairs={{0,1},{1,0},{2,3},{3,2},{4,5},{5,4},{6,7},{7,6},{8,9},{9,8},{10,11... | collective-permute-start | bytes 983048 | tf_op jit(solution)/shard_map/ppermute | solution.py:391
  128.3 5.1 %collective-permute-start.16 = (bf16[2,4,16,1280]{3,2,1,0:T(8,128)(2,1)}, bf16[2,4,16,1280]{3,2,1,0:T(8,128)(2,1)}, u32[]{:S(2)}, u32[]{:S(2)}) collective-permute-start(bf16[2,4,16,1280]{3,2,1,0:T(8,128)(2,1)} %copy-done.8), channel_id=1, source_target_pairs={{0,1},{1,0},{2,3},{3,2},{4,5},{5,4},{6,7},{7,6},{8,9},{9,8},{10,11... | collective-permute-start | bytes 983048 | tf_op jit(solution)/shard_map/ppermute | solution.py:391
  128.7 4.7 %collective-permute-start.17 = (bf16[2,4,16,1280]{3,2,1,0:T(8,128)(2,1)}, bf16[2,4,16,1280]{3,2,1,0:T(8,128)(2,1)}, u32[]{:S(2)}, u32[]{:S(2)}) collective-permute-start(bf16[2,4,16,1280]{3,2,1,0:T(8,128)(2,1)} %copy-done.7), channel_id=1, source_target_pairs={{0,1},{1,0},{2,3},{3,2},{4,5},{5,4},{6,7},{7,6},{8,9},{9,8},{10,11... | collective-permute-start | bytes 983048 | tf_op jit(solution)/shard_map/ppermute | solution.py:391
  140.3 21.3 %all-to-all-start.3 = ((bf16[8,320,256]{2,1,0:T(8,128)(2,1)}), bf16[8,320,256]{2,1,0:T(8,128)(2,1)S(1)}, u32[]{:S(2)}, u32[]{:S(2)}) async-start(bf16[8,320,256]{2,1,0:T(8,128)(2,1)} %forward_terms.1), calls=%async_computation.3 | async-start | bytes 2621440 | tf_op jit(solution)/shard_map/all_to_all | solution.py:362
  162.2 7.1 %collective-permute-start.24 = (bf16[320,256]{1,0:T(8,128)(2,1)S(1)}, bf16[320,256]{1,0:T(8,128)(2,1)S(1)}, u32[]{:S(2)}, u32[]{:S(2)}) collective-permute-start(bf16[320,256]{1,0:T(8,128)(2,1)S(1)} %fusion.6.refs_16_), channel_id=1, source_target_pairs={{0,224},{32,192},{64,160},{96,128},{128,96},{160,64},{192,32},{224... | collective-permute-start | bytes 491528 | tf_op jit(solution)/shard_map/ppermute | solution.py:338
  164.7 8.3 %collective-permute-start.23 = (bf16[320,256]{1,0:T(8,128)(2,1)S(1)}, bf16[320,256]{1,0:T(8,128)(2,1)S(1)}, u32[]{:S(2)}, u32[]{:S(2)}) collective-permute-start(bf16[320,256]{1,0:T(8,128)(2,1)S(1)} %fusion.6.refs_16_), channel_id=1, source_target_pairs={{0,192},{32,224},{64,128},{96,160},{128,64},{160,96},{192,0},{224,... | collective-permute-start | bytes 491528 | tf_op jit(solution)/shard_map/ppermute | solution.py:338
  164.9 10.0 %collective-permute-start.22 = (bf16[320,256]{1,0:T(8,128)(2,1)S(1)}, bf16[320,256]{1,0:T(8,128)(2,1)S(1)}, u32[]{:S(2)}, u32[]{:S(2)}) collective-permute-start(bf16[320,256]{1,0:T(8,128)(2,1)S(1)} %fusion.6.refs_16_), channel_id=1, source_target_pairs={{0,160},{32,128},{64,224},{96,192},{128,32},{160,0},{192,96},{224,... | collective-permute-start | bytes 491528 | tf_op jit(solution)/shard_map/ppermute | solution.py:338
  167.4 11.5 %collective-permute-start.21 = (bf16[320,256]{1,0:T(8,128)(2,1)S(1)}, bf16[320,256]{1,0:T(8,128)(2,1)S(1)}, u32[]{:S(2)}, u32[]{:S(2)}) collective-permute-start(bf16[320,256]{1,0:T(8,128)(2,1)S(1)} %fusion.6.refs_16_), channel_id=1, source_target_pairs={{0,128},{32,160},{64,192},{96,224},{128,0},{160,32},{192,64},{224,... | collective-permute-start | bytes 491528 | tf_op jit(solution)/shard_map/ppermute | solution.py:338
  167.6 12.8 %collective-permute-start.20 = (bf16[320,256]{1,0:T(8,128)(2,1)S(1)}, bf16[320,256]{1,0:T(8,128)(2,1)S(1)}, u32[]{:S(2)}, u32[]{:S(2)}) collective-permute-start(bf16[320,256]{1,0:T(8,128)(2,1)S(1)} %fusion.6.refs_16_), channel_id=1, source_target_pairs={{0,96},{32,64},{64,32},{96,0},{128,224},{160,192},{192,160},{224,1... | collective-permute-start | bytes 491528 | tf_op jit(solution)/shard_map/ppermute | solution.py:338
  169.4 11.1 %collective-permute-start.19 = (bf16[320,256]{1,0:T(8,128)(2,1)S(1)}, bf16[320,256]{1,0:T(8,128)(2,1)S(1)}, u32[]{:S(2)}, u32[]{:S(2)}) collective-permute-start(bf16[320,256]{1,0:T(8,128)(2,1)S(1)} %fusion.6.refs_16_), channel_id=1, source_target_pairs={{0,64},{32,96},{64,0},{96,32},{128,192},{160,224},{192,128},{224,1... | collective-permute-start | bytes 491528 | tf_op jit(solution)/shard_map/ppermute | solution.py:338
  172.9 9.6 %collective-permute-start.18 = (bf16[320,256]{1,0:T(8,128)(2,1)S(1)}, bf16[320,256]{1,0:T(8,128)(2,1)S(1)}, u32[]{:S(2)}, u32[]{:S(2)}) collective-permute-start(bf16[320,256]{1,0:T(8,128)(2,1)S(1)} %fusion.6.refs_16_), channel_id=1, source_target_pairs={{0,32},{32,0},{64,96},{96,64},{128,160},{160,128},{192,224},{224,1... | collective-permute-start | bytes 491528 | tf_op jit(solution)/shard_map/ppermute | solution.py:338
  (21 other events, 139.2 us)

commit v3 on v2

--- a/solution.py
+++ b/solution.py
@@ -43,34 +43,39 @@
     return jnp.dot(a, b, preferred_element_type=F32)
 
 
-def column_kernel(slabs_step, piece, copy_ref, own_ref, place_ref, w_ref, m_ref, v_ref, out_ref, total, own_place):
-    step = pl.program_id(0)
-    rows, depth = w_ref.shape
-    parts = [w_ref[...], m_ref[...].astype(BF16), v_ref[...].astype(BF16)]
-
-    @pl.when(step == 0)
-    def _():
+def column_kernel(slabs_step, piece, copy_ref, own_ref, place_ref, *refs):
+    sources, out_ref, total, own_place, held_refs, sems = refs[:3], refs[3], refs[4], refs[5], refs[6:9], refs[9]
+    rows = total.shape[0] // 3
+    depth = own_place.shape[1]
+    steps = held_refs[0].shape[0]
+
+    def copy(k, step):
+        lanes = pl.ds(pl.multiple_of(step * depth, LANES), depth)
+        return pltpu.make_async_copy(sources[k].at[:, lanes], held_refs[k].at[step], sems.at[k, step])
+
+    for step in range(steps):
         for k in range(3):
-            own_place[k] = chosen(own_ref[k : k + 1, :], depth)
-
-    same = functools.reduce(
-        lambda a, b: a + b,
-        [dot(part, own_place[k]) for k, part in enumerate(parts)],
-    ).astype(BF16)
-    for j in range(slabs_step):
-        out_ref[step * slabs_step + j] = same[:, j * LANES : (j + 1) * LANES]
-    picked = dot(jnp.concatenate(parts, axis=0), chosen(copy_ref[...], depth, step * depth))
-
-    @pl.when(step == 0)
-    def _():
-        total[...] = picked
-
-    @pl.when(step > 0)
-    def _():
-        total[...] += picked
-
-    @pl.when(step == pl.num_programs(0) - 1)
-    def _():
+            copy(k, step).start()
+    for k in range(3):
+        own_place[k] = chosen(own_ref[k : k + 1, :], depth)
+    total[...] = jnp.zeros_like(total)
+
+    def body(step, carry):
+        for k in range(3):
+            copy(k, step).wait()
+        parts = [ref[step].astype(BF16) for ref in held_refs]
+        same = functools.reduce(
+            lambda a, b: a + b,
+            [dot(part, own_place[k]) for k, part in enumerate(parts)],
+        ).astype(BF16)
+        for j in range(slabs_step):
+            out_ref[step * slabs_step + j] = same[:, j * LANES : (j + 1) * LANES]
+        total[...] += dot(jnp.concatenate(parts, axis=0), chosen(copy_ref[...], depth, step * depth))
+        return carry
+
+    lax.fori_loop(0, steps, body, 0)
+
+    def finish():
         half = out_ref.shape[0] // 2
         width = total.shape[1]
         window = 2 * LANES
@@ -89,6 +94,8 @@
             for i, j in enumerate(slabs):
                 out_ref[half + j] = spread[:, i * LANES : (i + 1) * LANES]
 
+    finish()
+
 
 def grow_columns(old_weight, old_first, old_second, col_source, slabs, slab_width, pieces, piece_at):
     rows, old_width = old_weight.shape
@@ -110,20 +117,16 @@
     place_index = spread_index(half, piece, 0)
     return pl.pallas_call(
         functools.partial(column_kernel, slabs_step, piece),
-        grid=(half // slabs_step,),
-        in_specs=[
-            pl.BlockSpec((1, half * piece), lambda s: (0, 0)),
-            pl.BlockSpec((3, slabs_step * LANES), lambda s: (0, 0)),
-            pl.BlockSpec((3, half * LANES), lambda s: (0, 0)),
-            pl.BlockSpec((rows, depth), lambda s: (0, s)),
-            pl.BlockSpec((rows, depth), lambda s: (0, s)),
-            pl.BlockSpec((rows, depth), lambda s: (0, s)),
-        ],
-        out_specs=pl.BlockSpec((slabs, rows, LANES), lambda s: (0, 0, 0)),
+        in_specs=[pl.BlockSpec(memory_space=pltpu.VMEM)] * 3 + [pl.BlockSpec(memory_space=pl.ANY)] * 3,
+        out_specs=pl.BlockSpec(memory_space=pltpu.VMEM),
         out_shape=jax.ShapeDtypeStruct((slabs, rows, LANES), BF16),
         scratch_shapes=[
             pltpu.VMEM((3 * rows, half * piece), F32),
             pltpu.VMEM((3, depth, slabs_step * LANES), BF16),
+            pltpu.VMEM((half // slabs_step, rows, depth), BF16),
+            pltpu.VMEM((half // slabs_step, rows, depth), F32),
+            pltpu.VMEM((half // slabs_step, rows, depth), F32),
+            pltpu.SemaphoreType.DMA((3, half // slabs_step)),
         ],
         compiler_params=pltpu.CompilerParams(vmem_limit_bytes=VMEM_BYTES),
         cost_estimate=pl.CostEstimate(flops=1000, bytes_accessed=1000, transcendentals=0),
@@ -179,11 +182,6 @@
     return lax.dot_general(place, block, (((1,), (1,)), ((), ())), preferred_element_type=F32)
 
 
-def weight_kernel(piece, blocks_ref, row_scale_ref, col_scale_ref, weight_ref):
-    copied = assemble(blocks_ref, 0, piece, weight_ref.shape[0])
-    weight_ref[...] = (copied * row_scale_ref[...] * col_scale_ref[...]).astype(BF16)
-
-
 def moments_kernel(piece, blocks_ref, first_ref, second_ref):
     for a, ref in enumerate((first_ref, second_ref)):
         ref[...] = assemble(blocks_ref, a + 1, piece, ref.shape[0]).astype(BF16)
@@ -202,91 +200,143 @@
     )(*operands)
 
 
-def forward_kernel(place_ref, *refs):
-    parts, weight_ref, out_ref = refs[:-2], refs[-2], refs[-1]
-    step = pl.program_id(0)
-    half = pl.num_programs(0)
+def forward_kernel(count, piece, place_ref, *refs):
+    parts, refs = refs[:count], refs[count:]
+    blocks_ref, row_scale_ref, col_scale_ref, weight_ref, out_ref, held, sems = refs
+    half = held.shape[0]
     core = place_ref[1]
-    both = [ref[...].reshape(-1, ref.shape[-1]) for ref in parts]
-    term = lax.dot_general(
-        weight_ref[...], jnp.concatenate(both, axis=0), (((1,), (1,)), ((), ())), preferred_element_type=F32
-    ).astype(BF16)
-    width = out_ref.shape[2]
-    out_ref[core * half + step] = term[:, :width]
-    out_ref[(1 - core) * half + step] = term[:, width:]
-
-
-def forward(place, parts, weight, groups):
+
+    def copy(p, j):
+        return pltpu.make_async_copy(parts[p].at[:, j], held.at[j, p], sems.at[j, p])
+
+    for j in range(half):
+        for p in range(count):
+            copy(p, j).start()
+    copied = assemble(blocks_ref, 0, piece, weight_ref.shape[0])
+    weight_ref[...] = (copied * row_scale_ref[...] * col_scale_ref[...]).astype(BF16)
+
+    def body(j, carry):
+        for p in range(count):
+            copy(p, j).wait()
+        both = held[j].reshape(-1, weight_ref.shape[1])
+        term = lax.dot_general(
+            weight_ref[...], both, (((1,), (1,)), ((), ())), preferred_element_type=F32
+        ).astype(BF16)
+        width = out_ref.shape[2]
+        out_ref[core * half + j] = term[:, :width]
+        out_ref[(1 - core) * half + j] = term[:, width:]
+        return carry
+
+    lax.fori_loop(0, half, body, 0)
+
+
+def forward(place, parts, blocks, row_scale, col_scale, groups, piece):
     near, half, chip_rows, block_rows = parts[0].shape
-    shape = (groups, weight.shape[0], len(parts) // 2 * near * chip_rows)
-    tokens = pl.BlockSpec((near, 1, chip_rows, block_rows), lambda s: (0, s, 0, 0))
-    return pl.pallas_call(
-        forward_kernel,
-        grid=(half,),
+    slab_width = blocks.shape[0] * piece
+    count = len(parts)
+    shape = (groups, slab_width, count // 2 * near * chip_rows)
+    vmem = pl.BlockSpec(memory_space=pltpu.VMEM)
+    return pl.pallas_call(
+        functools.partial(forward_kernel, count, piece),
         in_specs=[pl.BlockSpec(memory_space=pltpu.SMEM)]
-        + [tokens] * len(parts)
-        + [pl.BlockSpec(weight.shape, lambda s: (0, 0))],
-        out_specs=pl.BlockSpec(shape, lambda s: (0, 0, 0)),
-        out_shape=jax.ShapeDtypeStruct(shape, BF16),
+        + [pl.BlockSpec(memory_space=pl.ANY)] * count
+        + [vmem] * 3,
+        out_specs=[vmem, vmem],
+        out_shape=[
+            jax.ShapeDtypeStruct((slab_width, block_rows), BF16),
+            jax.ShapeDtypeStruct(shape, BF16),
+        ],
+        scratch_shapes=[
+            pltpu.VMEM((half, count, near, chip_rows, block_rows), BF16),
+            pltpu.SemaphoreType.DMA((half, count)),
+        ],
         compiler_params=pltpu.CompilerParams(vmem_limit_bytes=VMEM_BYTES),
         cost_estimate=pl.CostEstimate(flops=1000, bytes_accessed=1000, transcendentals=0),
         name="forward_terms",
-    )(place, *parts, weight)
-
-
-def adam_kernel(groups, place_ref, *refs):
-    parts, grads, refs = refs[: -groups - 7], refs[-groups - 7 : -7], refs[-7:]
-    first_ref, second_ref, weight_ref, new_weight_ref, new_first_ref, new_second_ref, held = refs
-    step_rows = weight_ref.shape[1]
-    half = parts[0].shape[1]
+    )(place, *parts, blocks, row_scale, col_scale)
+
+
+def adam_kernel(count, groups, place_ref, *refs):
+    parts, grads, refs = refs[:count], refs[count : count + groups], refs[count + groups :]
+    first_ref, second_ref, weight_ref = refs[:3]
+    results, held, tokens, kept, in_sems, out_sems = refs[3:6], refs[6], refs[7], refs[8:11], refs[11], refs[12]
+    steps, _, _, half, _, step_rows = tokens.shape
     core = place_ref[1]
-    count = len(parts) // 2
-
-    @pl.when(pl.program_id(0) == 0)
-    def _():
-        for k, ref in enumerate(grads):
-            held[jnp.bitwise_xor(place_ref[0], k)] = ref[...]
-
-    grads_in_order, groups_in_order = [], []
-    for refs_of, at in ((parts[:count], core), (parts[count:], 1 - core)):
-        for j in range(half):
-            grads_in_order.append(held[at * half + j])
-            groups_in_order += [ref[:, j].reshape(-1, step_rows) for ref in refs_of]
-    gradient = dot(jnp.concatenate(grads_in_order, axis=1), jnp.concatenate(groups_in_order, axis=0))
-    weight = weight_ref[...].astype(F32)
-    new_first = beta_one * first_ref[...].astype(F32) + (1.0 - beta_one) * gradient
-    new_second = beta_two * second_ref[...].astype(F32) + (1.0 - beta_two) * gradient * gradient
-    first_corr = 1.0 - beta_one**adam_step
-    second_corr = 1.0 - beta_two**adam_step
-    update = (
-        new_first * (1.0 / first_corr) / (jnp.sqrt(new_second * (1.0 / second_corr)) + adam_eps)
-        + weight_decay * weight
-    )
-    new_weight_ref[...] = (weight - learn_rate * update).astype(BF16)
-    new_first_ref[...] = new_first
-    new_second_ref[...] = new_second
+
+    def columns(step):
+        return pl.ds(pl.multiple_of(step * step_rows, LANES), step_rows)
+
+    def copy_in(p, step):
+        return pltpu.make_async_copy(parts[p].at[:, :, :, columns(step)], tokens.at[step, p], in_sems.at[step, p])
+
+    def copy_out(k, step):
+        return pltpu.make_async_copy(kept[k].at[step], results[k].at[:, columns(step)], out_sems.at[k, step])
+
+    for step in range(steps):
+        for p in range(count):
+            copy_in(p, step).start()
+    for k, ref in enumerate(grads):
+        held[jnp.bitwise_xor(place_ref[0], k)] = ref[...]
+
+    def body(step, carry):
+        for p in range(count):
+            copy_in(p, step).wait()
+        grads_in_order, groups_in_order = [], []
+        for mine, at in ((range(count // 2), core), (range(count // 2, count), 1 - core)):
+            for j in range(half):
+                grads_in_order.append(held[at * half + j])
+                groups_in_order += [tokens[step, p, :, j].reshape(-1, step_rows) for p in mine]
+        gradient = dot(jnp.concatenate(grads_in_order, axis=1), jnp.concatenate(groups_in_order, axis=0))
+        weight = weight_ref[:, columns(step)].astype(F32)
+        first = first_ref[:, columns(step)].astype(F32)
+        second = second_ref[:, columns(step)].astype(F32)
+        new_first = beta_one * first + (1.0 - beta_one) * gradient
+        new_second = beta_two * second + (1.0 - beta_two) * gradient * gradient
+        first_corr = 1.0 - beta_one**adam_step
+        second_corr = 1.0 - beta_two**adam_step
+        update = (
+            new_first * (1.0 / first_corr) / (jnp.sqrt(new_second * (1.0 / second_corr)) + adam_eps)
+            + weight_decay * weight
+        )
+        kept[0][step] = (weight - learn_rate * update).astype(BF16)
+        kept[1][step] = new_first
+        kept[2][step] = new_second
+        for k in range(3):
+            copy_out(k, step).start()
+        return carry
+
+    lax.fori_loop(0, steps, body, 0)
+    for step in range(steps):
+        for k in range(3):
+            copy_out(k, step).wait()
 
 
 def backward(place, parts, grads, first, second, weight):
     near, half, chip_rows, block_rows = parts[0].shape
     slab_width = weight.shape[0]
     step_rows = 256
-    tokens = pl.BlockSpec((near, half, chip_rows, step_rows), lambda s: (0, 0, 0, s))
-    block = pl.BlockSpec((slab_width, step_rows), lambda s: (0, s))
-    return pl.pallas_call(
-        functools.partial(adam_kernel, len(grads)),
-        grid=(block_rows // step_rows,),
-        in_specs=[pl.BlockSpec(memory_space=pltpu.SMEM)]
-        + [tokens] * len(parts)
-        + [pl.BlockSpec(grads[0].shape, lambda s: (0, 0))] * len(grads)
-        + [block, block, block],
-        out_specs=[block, block, block],
+    steps = block_rows // step_rows
+    count, groups = len(parts), len(grads)
+    vmem, anywhere = pl.BlockSpec(memory_space=pltpu.VMEM), pl.BlockSpec(memory_space=pl.ANY)
+    kept = (steps, slab_width, step_rows)
+    return pl.pallas_call(
+        functools.partial(adam_kernel, count, groups),
+        in_specs=[pl.BlockSpec(memory_space=pltpu.SMEM)] + [anywhere] * count + [vmem] * (groups + 3),
+        out_specs=[anywhere] * 3,
         out_shape=[
             jax.ShapeDtypeStruct((slab_width, block_rows), BF16),
             jax.ShapeDtypeStruct((slab_width, block_rows), F32),
             jax.ShapeDtypeStruct((slab_width, block_rows), F32),
         ],
-        scratch_shapes=[pltpu.VMEM((len(grads),) + grads[0].shape, BF16)],
+        scratch_shapes=[
+            pltpu.VMEM((groups,) + grads[0].shape, BF16),
+            pltpu.VMEM((steps, count, near, half, chip_rows, step_rows), BF16),
+            pltpu.VMEM(kept, BF16),
+            pltpu.VMEM(kept, F32),
+            pltpu.VMEM(kept, F32),
+            pltpu.SemaphoreType.DMA((steps, count)),
+            pltpu.SemaphoreType.DMA((3, steps)),
+        ],
         compiler_params=pltpu.CompilerParams(vmem_limit_bytes=VMEM_BYTES),
         cost_estimate=pl.CostEstimate(flops=1000, bytes_accessed=1000, transcendentals=0),
         name="gradient_adam",
@@ -386,12 +436,12 @@
     far = along_x(stacked(along_z[DIM_Z // 2 :]))
     grown = grow_rows(columns.reshape(old_width, LANES), row_source)
     blocks = exchange(grown.reshape(groups, block_rows, LANES), "dp")
-    blocks, *far = in_order(blocks, *far)
     own = near + far
-    parts = own + [lax.ppermute(values, "tensor", shifted(0, 0, 1)) for values in own]
-    (weight,) = grown_block(weight_kernel, (blocks, row_scale, col_scale), 1, block_rows, slab_width, piece)
-
-    terms = exchange(forward(place, parts, weight, groups), "dp")
+    other = [lax.ppermute(values, "tensor", shifted(0, 0, 1)) for values in own]
+    blocks, *parts = in_order(blocks, *own, *other)
+
+    weight, terms = forward(place, parts, blocks, row_scale, col_scale, groups, piece)
+    terms = exchange(terms, "dp")
     first, second = grown_block(moments_kernel, (blocks,), 2, block_rows, slab_width, piece)
     terms, first, second = in_order(terms, first, second)
     turned_grad = dot(cotangent.T, to_real.T)

time: 193 us -> 189 us (0.979)
  Pallas kernels: 47.2 us -> 43.4 us
  waiting for transfers between devices: 76.7 us -> 73.6 us
  local copies, waits for them, and re-layouts: 7.07 us -> 9.12 us
    all_to_all x3, waiting for transfers between devices: 24 us -> 19.8 us  [exchange(): return lax.all_to_all(values, axis, split_axis=0, concat_axis=0, tiled=True)]
    pallas_call x2 -> x1, Pallas kernels: 8.27 us -> 4.56 us  [grown_block(): pl.pallas_call(functools.partial(kernel, piece), in_specs=[pl.BlockSpec(m...]
    unnamed x51 -> x55, local copies, waits for them, and re-layouts: 3.82 us -> 5.9 us
  transfers between devices with their start and end apart: 29 -> 29, of which waited for: 14 -> 16; matrix products, arithmetic and copies ran while one was open for 3% -> 3% of each run, Pallas kernels for 13% -> 10%
where the time goes in v3:
time: 189 us; the launch traced here: 188 us
  waiting for transfers between devices  73.6 us (39%)
  starting transfers between devices  57.5 us (30%)
  Pallas kernels  43.4 us (23%)
  local copies, waits for them, and re-layouts  9.12 us (5%)
  other arithmetic  2.26 us (1%)
    ppermute x6, waiting for transfers between devices, along_x(): lax.ppermute(values, 'tensor', shifted(k, 0, 0))  36.3 us
    all_to_all x3, waiting for transfers between devices, exchange(): return lax.all_to_all(values, axis, split_axis=0, concat_axis=0, tiled=True)  19.8 us
    all_to_all x3, starting transfers between devices, exchange(): return lax.all_to_all(values, axis, split_axis=0, concat_axis=0, tiled=True)  19.1 us
    ppermute x7, waiting for transfers between devices, to_groups(): lax.ppermute(values, 'dp', [(i, i ^ k) for i in range(groups)])  11.8 us
    pallas_call x1, Pallas kernels, grow_columns(): pl.pallas_call(functools.partial(column_kernel, slabs_step, piece), in_sp...  11.2 us
    pallas_call x1, Pallas kernels, backward(): pl.pallas_call(functools.partial(adam_kernel, count, groups), in_specs=[p...  8.74 us
    ppermute x3, starting transfers between devices, shards(): lax.ppermute(chip, 'tensor', shifted(0, k, 0))  8.45 us
    pallas_call x1, Pallas kernels, grow_rows(): pl.pallas_call(row_kernel, in_specs=[pl.BlockSpec(memory_space=pltpu.SMEM...  8.06 us
  transfers between devices with their start and end apart: 29, of which 16 were waited for; matrix products, arithmetic and copies ran while one was open for 3% of the time, Pallas kernels for 10%

profile of v3, /device:TPU:1, one launch (start us, length us, event | category | flops | bytes accessed | tf_op | source)
XLA Modules:
  0.0 188.4 jit_solution(3240581363372003525)
XLA Ops:
  0.6 6.5 %all-to-all-start = ((bf16[8,8,1280]{2,0,1:T(8,128)(2,1)}), bf16[8,8,1280]{2,0,1:T(8,128)(2,1)S(1)}, u32[]{:S(2)}, u32[]{:S(2)}) async-start(bf16[8,8,1280]{2,0,1:T(8,128)(2,1)} %bitcast.54), calls=%async_computation | async-start | bytes 327680 | tf_op jit(solution)/shard_map/all_to_all | solution.py:423
  8.1 4.8 %all-to-all-done = bf16[8,8,1280]{2,0,1:T(8,128)(2,1)S(1)} async-done(((bf16[8,8,1280]{2,0,1:T(8,128)(2,1)}), bf16[8,8,1280]{2,0,1:T(8,128)(2,1)S(1)}, u32[]{:S(2)}, u32[]{:S(2)}) %all-to-all-start) | async-done | bytes 163872 | tf_op jit(solution)/shard_map/all_to_all | solution.py:423
  12.8 2.1 %collective-permute-start = (bf16[4,8,1280]{2,1,0:T(8,128)(2,1)S(1)}, bf16[4,8,1280]{2,1,0:T(8,128)(2,1)S(1)}, u32[]{:S(2)}, u32[]{:S(2)}) collective-permute-start(bf16[4,8,1280]{2,1,0:T(8,128)(2,1)S(1)} %dynamic-slice_bitcast_fusion), channel_id=1, source_target_pairs={{0,1},{1,0},{2,3},{3,2},{4,5},{5,4},{6,7},{7,6},{8,9},{9,8},{10,11... | collective-permute-start | bytes 245768 | tf_op jit(solution)/shard_map/ppermute | solution.py:381
  16.5 5.2 %collective-permute-start.3 = (bf16[1,4,16,1280]{3,2,1,0:T(8,128)(2,1)S(1)}, bf16[1,4,16,1280]{3,2,1,0:T(8,128)(2,1)S(1)}, u32[]{:S(2)}, u32[]{:S(2)}) collective-permute-start(bf16[1,4,16,1280]{3,2,1,0:T(8,128)(2,1)S(1)} %maximum_bitcast_fusion.refs_0_), channel_id=1, source_target_pairs={{0,6},{1,7},{2,0},{3,1},{4,2},{5,3},{6,4},{7,5},{8,14},{9,15},{10,... | collective-permute-start | bytes 491528 | tf_op jit(solution)/shard_map/ppermute | solution.py:426
  22.9 2.1 %collective-permute-start.1 = (bf16[1,4,16,1280]{3,2,1,0:T(8,128)(2,1)S(1)}, bf16[1,4,16,1280]{3,2,1,0:T(8,128)(2,1)S(1)}, u32[]{:S(2)}, u32[]{:S(2)}) collective-permute-start(bf16[1,4,16,1280]{3,2,1,0:T(8,128)(2,1)S(1)} %maximum_bitcast_fusion.refs_0_), channel_id=1, source_target_pairs={{0,2},{1,3},{2,4},{3,5},{4,6},{5,7},{6,0},{7,1},{8,10},{9,11},{10,... | collective-permute-start | bytes 491528 | tf_op jit(solution)/shard_map/ppermute | solution.py:426
  25.6 11.2 %grow_columns.1 = bf16[32,160,128]{2,1,0:T(8,128)(2,1)} custom-call(s32[1,640]{1,0:T(1,128)} %reshape.193.copy_ref, s32[3,256]{1,0:T(4,128)} %fusion.12.own_ref, s32[3,2048]{1,0:T(4,128)} %fusion.11.place_ref, bf16[160,5120]{1,0:T(8,128)(2,1)} %refs_0_, f32[160,5120]{1,0:T(8,128)} %refs_1_.1, f32[160,5120]{1,0:T(8,128)} %refs_2_.1), custom_call_target="tpu_custom_call" | custom-call | flops 1000 | bytes 1000 | tf_op jit(solution)/shard_map/grow_columns/pallas_call | solution.py:118
  38.2 9.9 %all-to-all-start.1 = ((bf16[32,160,128]{2,1,0:T(8,128)(2,1)}), bf16[32,160,128]{2,1,0:T(8,128)(2,1)S(1)}, u32[]{:S(2)}, u32[]{:S(2)}) async-start(bf16[32,160,128]{2,1,0:T(8,128)(2,1)} %grow_columns.1), calls=%async_computation.1 | async-start | bytes 2621440 | tf_op jit(solution)/shard_map/all_to_all | solution.py:412
  48.2 1.7 stack_tokens.2.refs_0_
  50.0 2.6 %collective-permute-start.6 = (bf16[2,4,16,1280]{3,2,1,0:T(8,128)(2,1)}, bf16[2,4,16,1280]{3,2,1,0:T(8,128)(2,1)S(1)}, u32[]{:S(2)}, u32[]{:S(2)}) collective-permute-start(bf16[2,4,16,1280]{3,2,1,0:T(8,128)(2,1)} %stack_tokens.2.refs_0_), channel_id=1, source_target_pairs={{0,24},{1,25},{2,26},{3,27},{4,28},{5,29},{6,30},{7,31},{8,0},{9,1... | collective-permute-start | bytes 983048 | tf_op jit(solution)/shard_map/ppermute | solution.py:432
  55.1 11.5 %collective-permute-done.6.refs_3_ = bf16[2,4,16,1280]{3,2,1,0:T(8,128)(2,1)S(1)} collective-permute-done((bf16[2,4,16,1280]{3,2,1,0:T(8,128)(2,1)}, bf16[2,4,16,1280]{3,2,1,0:T(8,128)(2,1)S(1)}, u32[]{:S(2)}, u32[]{:S(2)}) %collective-permute-start.6) | collective-permute-done | bytes 327712 | tf_op jit(solution)/shard_map/ppermute | solution.py:432
  66.6 5.2 %collective-permute-done.5.refs_2_ = bf16[2,4,16,1280]{3,2,1,0:T(8,128)(2,1)S(1)} collective-permute-done((bf16[2,4,16,1280]{3,2,1,0:T(8,128)(2,1)}, bf16[2,4,16,1280]{3,2,1,0:T(8,128)(2,1)S(1)}, u32[]{:S(2)}, u32[]{:S(2)}) %collective-permute-start.5) | collective-permute-done | bytes 327712 | tf_op jit(solution)/shard_map/ppermute | solution.py:432
  71.9 9.1 %collective-permute-done.4.refs_1_ = bf16[2,4,16,1280]{3,2,1,0:T(8,128)(2,1)S(1)} collective-permute-done((bf16[2,4,16,1280]{3,2,1,0:T(8,128)(2,1)}, bf16[2,4,16,1280]{3,2,1,0:T(8,128)(2,1)S(1)}, u32[]{:S(2)}, u32[]{:S(2)}) %collective-permute-start.4) | collective-permute-done | bytes 327712 | tf_op jit(solution)/shard_map/ppermute | solution.py:432
  82.0 8.1 %grow_rows.1 = bf16[10240,128]{1,0:T(8,128)(2,1)} custom-call(s32[5120]{0:T(1024)} %index_ref.1, bf16[5120,128]{1,0:T(8,128)(2,1)} %bitcast.53), custom_call_target="tpu_custom_call" | custom-call | flops 1000 | bytes 1000 | tf_op jit(solution)/shard_map/grow_rows/pallas_call | solution.py:158
  90.1 5.5 %all-to-all-start.2 = ((bf16[8,1280,128]{2,1,0:T(8,128)(2,1)}), bf16[8,1280,128]{2,1,0:T(8,128)(2,1)S(1)}, u32[]{:S(2)}, u32[]{:S(2)}) async-start(bf16[8,1280,128]{2,1,0:T(8,128)(2,1)} %bitcast.52), calls=%async_computation.2 | async-start | bytes 5242880 | tf_op jit(solution)/shard_map/all_to_all | solution.py:412
  95.6 1.7 stack_tokens.3.refs_4_
  100.3 5.6 %collective-permute-done.9.refs_7_ = bf16[2,4,16,1280]{3,2,1,0:T(8,128)(2,1)S(1)} collective-permute-done((bf16[2,4,16,1280]{3,2,1,0:T(8,128)(2,1)}, bf16[2,4,16,1280]{3,2,1,0:T(8,128)(2,1)S(1)}, u32[]{:S(2)}, u32[]{:S(2)}) %collective-permute-start.9) | collective-permute-done | bytes 327712 | tf_op jit(solution)/shard_map/ppermute | solution.py:432
  105.9 3.1 %collective-permute-start.17 = (bf16[2,4,16,1280]{3,2,1,0:T(8,128)(2,1)S(1)}, bf16[2,4,16,1280]{3,2,1,0:T(8,128)(2,1)S(1)}, u32[]{:S(2)}, u32[]{:S(2)}) collective-permute-start(bf16[2,4,16,1280]{3,2,1,0:T(8,128)(2,1)S(1)} %collective-permute-done.9.refs_7_), channel_id=1, source_target_pairs={{0,1},{1,0},{2,3},{3,2},{4,5},{5,4},{6,7},{7,6},{8,9},{9,8},{10,11... | collective-permute-start | bytes 983048 | tf_op jit(solution)/shard_map/ppermute | solution.py:440
  109.1 2.4 %collective-permute-start.16 = (bf16[2,4,16,1280]{3,2,1,0:T(8,128)(2,1)S(1)}, bf16[2,4,16,1280]{3,2,1,0:T(8,128)(2,1)S(1)}, u32[]{:S(2)}, u32[]{:S(2)}) collective-permute-start(bf16[2,4,16,1280]{3,2,1,0:T(8,128)(2,1)S(1)} %collective-permute-done.8.refs_6_), channel_id=1, source_target_pairs={{0,1},{1,0},{2,3},{3,2},{4,5},{5,4},{6,7},{7,6},{8,9},{9,8},{10,11... | collective-permute-start | bytes 983048 | tf_op jit(solution)/shard_map/ppermute | solution.py:440
  111.5 4.9 %collective-permute-done.7.refs_5_ = bf16[2,4,16,1280]{3,2,1,0:T(8,128)(2,1)} collective-permute-done((bf16[2,4,16,1280]{3,2,1,0:T(8,128)(2,1)}, bf16[2,4,16,1280]{3,2,1,0:T(8,128)(2,1)}, u32[]{:S(2)}, u32[]{:S(2)}) %collective-permute-start.7) | collective-permute-done | bytes 327712 | tf_op jit(solution)/shard_map/ppermute | solution.py:432
  120.6 6.7 %all-to-all-done.2.refs_16_.blocks_ref = bf16[8,1280,128]{2,1,0:T(8,128)(2,1)S(1)} async-done(((bf16[8,1280,128]{2,1,0:T(8,128)(2,1)}), bf16[8,1280,128]{2,1,0:T(8,128)(2,1)S(1)}, u32[]{:S(2)}, u32[]{:S(2)}) %all-to-all-start.2) | async-done | bytes 2621472 | tf_op jit(solution)/shard_map/all_to_all | solution.py:412
  127.3 1.5 copy-done.1
  128.8 7.4 %forward_terms.1 = (bf16[320,1280]{1,0:T(8,128)(2,1)}, bf16[8,320,256]{2,1,0:T(8,128)(2,1)}) custom-call(s32[2]{0:T(128)} %pad_add_fusion.place_ref, bf16[2,4,16,1280]{3,2,1,0:T(8,128)(2,1)} %stack_tokens.2.refs_0_, bf16[2,4,16,1280]{3,2,1,0:T(8,128)(2,1)} %copy-done.6, bf16[2,4,16,1280]{3,2,1,0:T(8,128)(2,1)} %copy-done.5, ...), custom_call_target="tpu_custom_call" | custom-call | flops 1000 | bytes 1000 | tf_op jit(solution)/shard_map/forward_terms/pallas_call | solution.py:239
  136.2 3.7 %all-to-all-start.3 = ((bf16[8,320,256]{2,1,0:T(8,128)(2,1)}), bf16[8,320,256]{2,1,0:T(8,128)(2,1)S(1)}, u32[]{:S(2)}, u32[]{:S(2)}) async-start(bf16[8,320,256]{2,1,0:T(8,128)(2,1)} %get-tuple-element.78), calls=%async_computation.3 | async-start | bytes 2621440 | tf_op jit(solution)/shard_map/all_to_all | solution.py:412
  139.9 4.6 %grown_block_2.1 = (bf16[320,1280]{1,0:T(8,128)(2,1)}, bf16[320,1280]{1,0:T(8,128)(2,1)}) custom-call(bf16[8,1280,128]{2,1,0:T(8,128)(2,1)} %copy-done.1), custom_call_target="tpu_custom_call" | custom-call | flops 1000 | bytes 1000 | tf_op jit(solution)/shard_map/grown_block_2/pallas_call | solution.py:192
  144.5 13.2 %all-to-all-done.3 = bf16[8,320,256]{2,1,0:T(8,128)(2,1)S(1)} async-done(((bf16[8,320,256]{2,1,0:T(8,128)(2,1)}), bf16[8,320,256]{2,1,0:T(8,128)(2,1)S(1)}, u32[]{:S(2)}, u32[]{:S(2)}) %all-to-all-start.3) | async-done | bytes 1310752 | tf_op jit(solution)/shard_map/all_to_all | solution.py:412
  158.3 2.5 %collective-permute-start.24 = (bf16[320,256]{1,0:T(8,128)(2,1)S(1)}, bf16[320,256]{1,0:T(8,128)(2,1)S(1)}, u32[]{:S(2)}, u32[]{:S(2)}) collective-permute-start(bf16[320,256]{1,0:T(8,128)(2,1)S(1)} %fusion.6.refs_16_), channel_id=1, source_target_pairs={{0,224},{32,192},{64,160},{96,128},{128,96},{160,64},{192,32},{224... | collective-permute-start | bytes 491528 | tf_op jit(solution)/shard_map/ppermute | solution.py:388
  161.0 2.4 %collective-permute-start.22 = (bf16[320,256]{1,0:T(8,128)(2,1)S(1)}, bf16[320,256]{1,0:T(8,128)(2,1)S(1)}, u32[]{:S(2)}, u32[]{:S(2)}) collective-permute-start(bf16[320,256]{1,0:T(8,128)(2,1)S(1)} %fusion.6.refs_16_), channel_id=1, source_target_pairs={{0,160},{32,128},{64,224},{96,192},{128,32},{160,0},{192,96},{224,... | collective-permute-start | bytes 491528 | tf_op jit(solution)/shard_map/ppermute | solution.py:388
  166.1 2.9 %collective-permute-done.23.refs_22_ = bf16[320,256]{1,0:T(8,128)(2,1)S(1)} collective-permute-done((bf16[320,256]{1,0:T(8,128)(2,1)S(1)}, bf16[320,256]{1,0:T(8,128)(2,1)S(1)}, u32[]{:S(2)}, u32[]{:S(2)}) %collective-permute-start.23) | collective-permute-done | bytes 163872 | tf_op jit(solution)/shard_map/ppermute | solution.py:388
  171.1 3.9 %collective-permute-done.21.refs_20_ = bf16[320,256]{1,0:T(8,128)(2,1)S(1)} collective-permute-done((bf16[320,256]{1,0:T(8,128)(2,1)S(1)}, bf16[320,256]{1,0:T(8,128)(2,1)S(1)}, u32[]{:S(2)}, u32[]{:S(2)}) %collective-permute-start.21) | collective-permute-done | bytes 163872 | tf_op jit(solution)/shard_map/ppermute | solution.py:388
  175.0 1.6 collective-permute-done.20.refs_19_
  176.5 2.3 %collective-permute-done.18.refs_17_ = bf16[320,256]{1,0:T(8,128)(2,1)S(1)} collective-permute-done((bf16[320,256]{1,0:T(8,128)(2,1)S(1)}, bf16[320,256]{1,0:T(8,128)(2,1)S(1)}, u32[]{:S(2)}, u32[]{:S(2)}) %collective-permute-start.18) | collective-permute-done | bytes 163872 | tf_op jit(solution)/shard_map/ppermute | solution.py:388
  179.5 8.7 %gradient_adam.1 = (bf16[320,1280]{1,0:T(8,128)(2,1)}, f32[320,1280]{1,0:T(8,128)}, f32[320,1280]{1,0:T(8,128)}) custom-call(s32[2]{0:T(128)} %pad_add_fusion.place_ref, bf16[2,4,16,1280]{3,2,1,0:T(8,128)(2,1)} %stack_tokens.2.refs_0_, bf16[2,4,16,1280]{3,2,1,0:T(8,128)(2,1)} %copy-done.6, bf16[2,4,16,1280]{3,2,1,0:T(8,128)(2,1)} %copy-done.5, ...), custom_call_target="tpu_custom_call" | custom-call | flops 1000 | bytes 1000 | tf_op jit(solution)/shard_map/gradient_adam/pallas_call | solution.py:322
  (115 shorter events, 22.7 us)
Async XLA Ops:
  0.6 157.2 %copy-start = (bf16[256,320]{0,1:T(8,128)(2,1)S(1)}, bf16[256,320]{0,1:T(8,128)(2,1)}, u32[]{:S(2)}) copy-start(bf16[256,320]{0,1:T(8,128)(2,1)} %param.10) | copy-start | bytes 491524
  0.6 12.2 %all-to-all-start = ((bf16[8,8,1280]{2,0,1:T(8,128)(2,1)}), bf16[8,8,1280]{2,0,1:T(8,128)(2,1)S(1)}, u32[]{:S(2)}, u32[]{:S(2)}) async-start(bf16[8,8,1280]{2,0,1:T(8,128)(2,1)} %bitcast.54), calls=%async_computation | async-start | bytes 327680 | tf_op jit(solution)/shard_map/all_to_all | solution.py:423
  12.8 3.7 %collective-permute-start = (bf16[4,8,1280]{2,1,0:T(8,128)(2,1)S(1)}, bf16[4,8,1280]{2,1,0:T(8,128)(2,1)S(1)}, u32[]{:S(2)}, u32[]{:S(2)}) collective-permute-start(bf16[4,8,1280]{2,1,0:T(8,128)(2,1)S(1)} %dynamic-slice_bitcast_fusion), channel_id=1, source_target_pairs={{0,1},{1,0},{2,3},{3,2},{4,5},{5,4},{6,7},{7,6},{8,9},{9,8},{10,11... | collective-permute-start | bytes 245768 | tf_op jit(solution)/shard_map/ppermute | solution.py:381
  16.5 20.3 %collective-permute-start.3 = (bf16[1,4,16,1280]{3,2,1,0:T(8,128)(2,1)S(1)}, bf16[1,4,16,1280]{3,2,1,0:T(8,128)(2,1)S(1)}, u32[]{:S(2)}, u32[]{:S(2)}) collective-permute-start(bf16[1,4,16,1280]{3,2,1,0:T(8,128)(2,1)S(1)} %maximum_bitcast_fusion.refs_0_), channel_id=1, source_target_pairs={{0,6},{1,7},{2,0},{3,1},{4,2},{5,3},{6,4},{7,5},{8,14},{9,15},{10,... | collective-permute-start | bytes 491528 | tf_op jit(solution)/shard_map/ppermute | solution.py:426
  21.7 15.2 %collective-permute-start.2 = (bf16[1,4,16,1280]{3,2,1,0:T(8,128)(2,1)S(1)}, bf16[1,4,16,1280]{3,2,1,0:T(8,128)(2,1)S(1)}, u32[]{:S(2)}, u32[]{:S(2)}) collective-permute-start(bf16[1,4,16,1280]{3,2,1,0:T(8,128)(2,1)S(1)} %maximum_bitcast_fusion.refs_0_), channel_id=1, source_target_pairs={{0,4},{1,5},{2,6},{3,7},{4,0},{5,1},{6,2},{7,3},{8,12},{9,13},{10,... | collective-permute-start | bytes 491528 | tf_op jit(solution)/shard_map/ppermute | solution.py:426
  22.9 15.3 %collective-permute-start.1 = (bf16[1,4,16,1280]{3,2,1,0:T(8,128)(2,1)S(1)}, bf16[1,4,16,1280]{3,2,1,0:T(8,128)(2,1)S(1)}, u32[]{:S(2)}, u32[]{:S(2)}) collective-permute-start(bf16[1,4,16,1280]{3,2,1,0:T(8,128)(2,1)S(1)} %maximum_bitcast_fusion.refs_0_), channel_id=1, source_target_pairs={{0,2},{1,3},{2,4},{3,5},{4,6},{5,7},{6,0},{7,1},{8,10},{9,11},{10,... | collective-permute-start | bytes 491528 | tf_op jit(solution)/shard_map/ppermute | solution.py:426
  38.2 42.7 %all-to-all-start.1 = ((bf16[32,160,128]{2,1,0:T(8,128)(2,1)}), bf16[32,160,128]{2,1,0:T(8,128)(2,1)S(1)}, u32[]{:S(2)}, u32[]{:S(2)}) async-start(bf16[32,160,128]{2,1,0:T(8,128)(2,1)} %grow_columns.1), calls=%async_computation.1 | async-start | bytes 2621440 | tf_op jit(solution)/shard_map/all_to_all | solution.py:412
  50.0 16.6 %collective-permute-start.6 = (bf16[2,4,16,1280]{3,2,1,0:T(8,128)(2,1)}, bf16[2,4,16,1280]{3,2,1,0:T(8,128)(2,1)S(1)}, u32[]{:S(2)}, u32[]{:S(2)}) collective-permute-start(bf16[2,4,16,1280]{3,2,1,0:T(8,128)(2,1)} %stack_tokens.2.refs_0_), channel_id=1, source_target_pairs={{0,24},{1,25},{2,26},{3,27},{4,28},{5,29},{6,30},{7,31},{8,0},{9,1... | collective-permute-start | bytes 983048 | tf_op jit(solution)/shard_map/ppermute | solution.py:432
  52.6 19.2 %collective-permute-start.5 = (bf16[2,4,16,1280]{3,2,1,0:T(8,128)(2,1)}, bf16[2,4,16,1280]{3,2,1,0:T(8,128)(2,1)S(1)}, u32[]{:S(2)}, u32[]{:S(2)}) collective-permute-start(bf16[2,4,16,1280]{3,2,1,0:T(8,128)(2,1)} %stack_tokens.2.refs_0_), channel_id=1, source_target_pairs={{0,16},{1,17},{2,18},{3,19},{4,20},{5,21},{6,22},{7,23},{8,24},{9,... | collective-permute-start | bytes 983048 | tf_op jit(solution)/shard_map/ppermute | solution.py:432
  53.2 27.8 %collective-permute-start.4 = (bf16[2,4,16,1280]{3,2,1,0:T(8,128)(2,1)}, bf16[2,4,16,1280]{3,2,1,0:T(8,128)(2,1)S(1)}, u32[]{:S(2)}, u32[]{:S(2)}) collective-permute-start(bf16[2,4,16,1280]{3,2,1,0:T(8,128)(2,1)} %stack_tokens.2.refs_0_), channel_id=1, source_target_pairs={{0,8},{1,9},{2,10},{3,11},{4,12},{5,13},{6,14},{7,15},{8,16},{9,17... | collective-permute-start | bytes 983048 | tf_op jit(solution)/shard_map/ppermute | solution.py:432
  66.6 50.9 %copy-start.4 = (bf16[2,4,16,1280]{3,2,1,0:T(8,128)(2,1)}, bf16[2,4,16,1280]{3,2,1,0:T(8,128)(2,1)S(1)}, u32[]{:S(2)}) copy-start(bf16[2,4,16,1280]{3,2,1,0:T(8,128)(2,1)S(1)} %collective-permute-done.6.refs_3_) | copy-start | bytes 983044
  90.1 26.8 %copy-start.3 = (bf16[2,4,16,1280]{3,2,1,0:T(8,128)(2,1)S(1)}, bf16[2,4,16,1280]{3,2,1,0:T(8,128)(2,1)}, u32[]{:S(2)}) copy-start(bf16[2,4,16,1280]{3,2,1,0:T(8,128)(2,1)} %stack_tokens.2.refs_0_) | copy-start | bytes 983044
  90.1 37.2 %all-to-all-start.2 = ((bf16[8,1280,128]{2,1,0:T(8,128)(2,1)}), bf16[8,1280,128]{2,1,0:T(8,128)(2,1)S(1)}, u32[]{:S(2)}, u32[]{:S(2)}) async-start(bf16[8,1280,128]{2,1,0:T(8,128)(2,1)} %bitcast.52), calls=%async_computation.2 | async-start | bytes 5242880 | tf_op jit(solution)/shard_map/all_to_all | solution.py:412
  97.3 8.6 %collective-permute-start.9 = (bf16[2,4,16,1280]{3,2,1,0:T(8,128)(2,1)}, bf16[2,4,16,1280]{3,2,1,0:T(8,128)(2,1)S(1)}, u32[]{:S(2)}, u32[]{:S(2)}) collective-permute-start(bf16[2,4,16,1280]{3,2,1,0:T(8,128)(2,1)} %stack_tokens.3.refs_4_), channel_id=1, source_target_pairs={{0,24},{1,25},{2,26},{3,27},{4,28},{5,29},{6,30},{7,31},{8,0},{9,1... | collective-permute-start | bytes 983048 | tf_op jit(solution)/shard_map/ppermute | solution.py:432
  97.9 11.1 %collective-permute-start.8 = (bf16[2,4,16,1280]{3,2,1,0:T(8,128)(2,1)}, bf16[2,4,16,1280]{3,2,1,0:T(8,128)(2,1)S(1)}, u32[]{:S(2)}, u32[]{:S(2)}) collective-permute-start(bf16[2,4,16,1280]{3,2,1,0:T(8,128)(2,1)} %stack_tokens.3.refs_4_), channel_id=1, source_target_pairs={{0,16},{1,17},{2,18},{3,19},{4,20},{5,21},{6,22},{7,23},{8,24},{9,... | collective-permute-start | bytes 983048 | tf_op jit(solution)/shard_map/ppermute | solution.py:432
  99.2 17.2 %collective-permute-start.7 = (bf16[2,4,16,1280]{3,2,1,0:T(8,128)(2,1)}, bf16[2,4,16,1280]{3,2,1,0:T(8,128)(2,1)}, u32[]{:S(2)}, u32[]{:S(2)}) collective-permute-start(bf16[2,4,16,1280]{3,2,1,0:T(8,128)(2,1)} %stack_tokens.3.refs_4_), channel_id=1, source_target_pairs={{0,8},{1,9},{2,10},{3,11},{4,12},{5,13},{6,14},{7,15},{8,16},{9,17... | collective-permute-start | bytes 983048 | tf_op jit(solution)/shard_map/ppermute | solution.py:432
  99.3 17.6 %collective-permute-start.14 = (bf16[2,4,16,1280]{3,2,1,0:T(8,128)(2,1)}, bf16[2,4,16,1280]{3,2,1,0:T(8,128)(2,1)S(1)}, u32[]{:S(2)}, u32[]{:S(2)}) collective-permute-start(bf16[2,4,16,1280]{3,2,1,0:T(8,128)(2,1)} %stack_tokens.3.refs_4_), channel_id=1, source_target_pairs={{0,1},{1,0},{2,3},{3,2},{4,5},{5,4},{6,7},{7,6},{8,9},{9,8},{10,11... | collective-permute-start | bytes 983048 | tf_op jit(solution)/shard_map/ppermute | solution.py:440
  105.9 11.5 %collective-permute-start.17 = (bf16[2,4,16,1280]{3,2,1,0:T(8,128)(2,1)S(1)}, bf16[2,4,16,1280]{3,2,1,0:T(8,128)(2,1)S(1)}, u32[]{:S(2)}, u32[]{:S(2)}) collective-permute-start(bf16[2,4,16,1280]{3,2,1,0:T(8,128)(2,1)S(1)} %collective-permute-done.9.refs_7_), channel_id=1, source_target_pairs={{0,1},{1,0},{2,3},{3,2},{4,5},{5,4},{6,7},{7,6},{8,9},{9,8},{10,11... | collective-permute-start | bytes 983048 | tf_op jit(solution)/shard_map/ppermute | solution.py:440
  109.1 8.5 %collective-permute-start.16 = (bf16[2,4,16,1280]{3,2,1,0:T(8,128)(2,1)S(1)}, bf16[2,4,16,1280]{3,2,1,0:T(8,128)(2,1)S(1)}, u32[]{:S(2)}, u32[]{:S(2)}) collective-permute-start(bf16[2,4,16,1280]{3,2,1,0:T(8,128)(2,1)S(1)} %collective-permute-done.8.refs_6_), channel_id=1, source_target_pairs={{0,1},{1,0},{2,3},{3,2},{4,5},{5,4},{6,7},{7,6},{8,9},{9,8},{10,11... | collective-permute-start | bytes 983048 | tf_op jit(solution)/shard_map/ppermute | solution.py:440
  116.4 3.4 %collective-permute-start.15 = (bf16[2,4,16,1280]{3,2,1,0:T(8,128)(2,1)}, bf16[2,4,16,1280]{3,2,1,0:T(8,128)(2,1)}, u32[]{:S(2)}, u32[]{:S(2)}) collective-permute-start(bf16[2,4,16,1280]{3,2,1,0:T(8,128)(2,1)} %collective-permute-done.7.refs_5_), channel_id=1, source_target_pairs={{0,1},{1,0},{2,3},{3,2},{4,5},{5,4},{6,7},{7,6},{8,9},{9,8},{10,11... | collective-permute-start | bytes 983048 | tf_op jit(solution)/shard_map/ppermute | solution.py:440
  116.9 2.9 %collective-permute-start.10 = (bf16[2,4,16,1280]{3,2,1,0:T(8,128)(2,1)S(1)}, bf16[2,4,16,1280]{3,2,1,0:T(8,128)(2,1)}, u32[]{:S(2)}, u32[]{:S(2)}) collective-permute-start(bf16[2,4,16,1280]{3,2,1,0:T(8,128)(2,1)S(1)} %copy-done.3), channel_id=1, source_target_pairs={{0,1},{1,0},{2,3},{3,2},{4,5},{5,4},{6,7},{7,6},{8,9},{9,8},{10,11... | collective-permute-start | bytes 983048 | tf_op jit(solution)/shard_map/ppermute | solution.py:440
  116.9 2.9 %collective-permute-start.11 = (bf16[2,4,16,1280]{3,2,1,0:T(8,128)(2,1)}, bf16[2,4,16,1280]{3,2,1,0:T(8,128)(2,1)}, u32[]{:S(2)}, u32[]{:S(2)}) collective-permute-start(bf16[2,4,16,1280]{3,2,1,0:T(8,128)(2,1)} %copy-done.6), channel_id=1, source_target_pairs={{0,1},{1,0},{2,3},{3,2},{4,5},{5,4},{6,7},{7,6},{8,9},{9,8},{10,11... | collective-permute-start | bytes 983048 | tf_op jit(solution)/shard_map/ppermute | solution.py:440
  117.4 2.5 %collective-permute-start.12 = (bf16[2,4,16,1280]{3,2,1,0:T(8,128)(2,1)}, bf16[2,4,16,1280]{3,2,1,0:T(8,128)(2,1)}, u32[]{:S(2)}, u32[]{:S(2)}) collective-permute-start(bf16[2,4,16,1280]{3,2,1,0:T(8,128)(2,1)} %copy-done.5), channel_id=1, source_target_pairs={{0,1},{1,0},{2,3},{3,2},{4,5},{5,4},{6,7},{7,6},{8,9},{9,8},{10,11... | collective-permute-start | bytes 983048 | tf_op jit(solution)/shard_map/ppermute | solution.py:440
  118.9 1.8 collective-permute-start.13
  136.2 21.5 %all-to-all-start.3 = ((bf16[8,320,256]{2,1,0:T(8,128)(2,1)}), bf16[8,320,256]{2,1,0:T(8,128)(2,1)S(1)}, u32[]{:S(2)}, u32[]{:S(2)}) async-start(bf16[8,320,256]{2,1,0:T(8,128)(2,1)} %get-tuple-element.78), calls=%async_computation.3 | async-start | bytes 2621440 | tf_op jit(solution)/shard_map/all_to_all | solution.py:412
  158.3 7.1 %collective-permute-start.24 = (bf16[320,256]{1,0:T(8,128)(2,1)S(1)}, bf16[320,256]{1,0:T(8,128)(2,1)S(1)}, u32[]{:S(2)}, u32[]{:S(2)}) collective-permute-start(bf16[320,256]{1,0:T(8,128)(2,1)S(1)} %fusion.6.refs_16_), channel_id=1, source_target_pairs={{0,224},{32,192},{64,160},{96,128},{128,96},{160,64},{192,32},{224... | collective-permute-start | bytes 491528 | tf_op jit(solution)/shard_map/ppermute | solution.py:388
  160.8 8.3 %collective-permute-start.23 = (bf16[320,256]{1,0:T(8,128)(2,1)S(1)}, bf16[320,256]{1,0:T(8,128)(2,1)S(1)}, u32[]{:S(2)}, u32[]{:S(2)}) collective-permute-start(bf16[320,256]{1,0:T(8,128)(2,1)S(1)} %fusion.6.refs_16_), channel_id=1, source_target_pairs={{0,192},{32,224},{64,128},{96,160},{128,64},{160,96},{192,0},{224,... | collective-permute-start | bytes 491528 | tf_op jit(solution)/shard_map/ppermute | solution.py:388
  161.0 10.1 %collective-permute-start.22 = (bf16[320,256]{1,0:T(8,128)(2,1)S(1)}, bf16[320,256]{1,0:T(8,128)(2,1)S(1)}, u32[]{:S(2)}, u32[]{:S(2)}) collective-permute-start(bf16[320,256]{1,0:T(8,128)(2,1)S(1)} %fusion.6.refs_16_), channel_id=1, source_target_pairs={{0,160},{32,128},{64,224},{96,192},{128,32},{160,0},{192,96},{224,... | collective-permute-start | bytes 491528 | tf_op jit(solution)/shard_map/ppermute | solution.py:388
  163.4 11.6 %collective-permute-start.21 = (bf16[320,256]{1,0:T(8,128)(2,1)S(1)}, bf16[320,256]{1,0:T(8,128)(2,1)S(1)}, u32[]{:S(2)}, u32[]{:S(2)}) collective-permute-start(bf16[320,256]{1,0:T(8,128)(2,1)S(1)} %fusion.6.refs_16_), channel_id=1, source_target_pairs={{0,128},{32,160},{64,192},{96,224},{128,0},{160,32},{192,64},{224,... | collective-permute-start | bytes 491528 | tf_op jit(solution)/shard_map/ppermute | solution.py:388
  163.7 12.8 %collective-permute-start.20 = (bf16[320,256]{1,0:T(8,128)(2,1)S(1)}, bf16[320,256]{1,0:T(8,128)(2,1)S(1)}, u32[]{:S(2)}, u32[]{:S(2)}) collective-permute-start(bf16[320,256]{1,0:T(8,128)(2,1)S(1)} %fusion.6.refs_16_), channel_id=1, source_target_pairs={{0,96},{32,64},{64,32},{96,0},{128,224},{160,192},{192,160},{224,1... | collective-permute-start | bytes 491528 | tf_op jit(solution)/shard_map/ppermute | solution.py:388
  165.4 11.2 %collective-permute-start.19 = (bf16[320,256]{1,0:T(8,128)(2,1)S(1)}, bf16[320,256]{1,0:T(8,128)(2,1)S(1)}, u32[]{:S(2)}, u32[]{:S(2)}) collective-permute-start(bf16[320,256]{1,0:T(8,128)(2,1)S(1)} %fusion.6.refs_16_), channel_id=1, source_target_pairs={{0,64},{32,96},{64,0},{96,32},{128,192},{160,224},{192,128},{224,1... | collective-permute-start | bytes 491528 | tf_op jit(solution)/shard_map/ppermute | solution.py:388
  169.0 9.9 %collective-permute-start.18 = (bf16[320,256]{1,0:T(8,128)(2,1)S(1)}, bf16[320,256]{1,0:T(8,128)(2,1)S(1)}, u32[]{:S(2)}, u32[]{:S(2)}) collective-permute-start(bf16[320,256]{1,0:T(8,128)(2,1)S(1)} %fusion.6.refs_16_), channel_id=1, source_target_pairs={{0,32},{32,0},{64,96},{96,64},{128,160},{160,128},{192,224},{224,1... | collective-permute-start | bytes 491528 | tf_op jit(solution)/shard_map/ppermute | solution.py:388
  (23 other events, 167.8 us)

commit v4 on v3

--- a/solution.py
+++ b/solution.py
@@ -97,12 +97,9 @@
     finish()
 
 
-def grow_columns(old_weight, old_first, old_second, col_source, slabs, slab_width, pieces, piece_at):
-    rows, old_width = old_weight.shape
+def column_indices(col_source, slabs, slab_width, pieces, piece_at):
     piece = slab_width // pieces
     half = slabs // 2
-    slabs_step = 2
-    depth = slabs_step * slab_width
     copy_index = lax.dynamic_slice_in_dim(
         col_source.reshape(half, pieces, piece), piece_at, 1, 1
     ).reshape(1, half * piece)
@@ -113,8 +110,15 @@
         slab = jnp.arange(count, dtype=jnp.int32)[None, :, None] * stride + offset
         return jnp.where(inside[:, None, :], lane[:, None, :] + slab, -1).reshape(3, count * LANES)
 
-    own_index = spread_index(slabs_step, slab_width, piece_at * piece)
-    place_index = spread_index(half, piece, 0)
+    return copy_index, spread_index(2, slab_width, piece_at * piece), spread_index(half, piece, 0)
+
+
+def grow_columns(indices, old_weight, old_first, old_second, slabs, slab_width, pieces):
+    rows = old_weight.shape[0]
+    piece = slab_width // pieces
+    half = slabs // 2
+    slabs_step = 2
+    depth = slabs_step * slab_width
     return pl.pallas_call(
         functools.partial(column_kernel, slabs_step, piece),
         in_specs=[pl.BlockSpec(memory_space=pltpu.VMEM)] * 3 + [pl.BlockSpec(memory_space=pl.ANY)] * 3,
@@ -131,7 +135,7 @@
         compiler_params=pltpu.CompilerParams(vmem_limit_bytes=VMEM_BYTES),
         cost_estimate=pl.CostEstimate(flops=1000, bytes_accessed=1000, transcendentals=0),
         name="grow_columns",
-    )(copy_index, own_index, place_index, old_weight, old_first, old_second)
+    )(*indices, old_weight, old_first, old_second)
 
 
 def row_kernel(index_ref, in_ref, out_ref, wide, picked):
@@ -164,7 +168,7 @@
         out_specs=pl.BlockSpec(memory_space=pltpu.VMEM),
         out_shape=jax.ShapeDtypeStruct((2 * old, LANES), BF16),
         scratch_shapes=[pltpu.VMEM((old, LANES), F32), pltpu.VMEM((old, LANES), F32)],
-        compiler_params=pltpu.CompilerParams(vmem_limit_bytes=VMEM_BYTES),
+        compiler_params=pltpu.CompilerParams(vmem_limit_bytes=16 * 1024 * 1024),
         cost_estimate=pl.CostEstimate(flops=1000, bytes_accessed=1000, transcendentals=0),
         name="grow_rows",
     )(row_source, columns)
@@ -421,10 +425,12 @@
     to_real = (real[:, None] == lane[None, :]).astype(BF16)
 
     part = lax.all_to_all(tokens, "dp", split_axis=1, concat_axis=0, tiled=True)
+    indices = column_indices(col_source, slabs, slab_width, groups, group_at)
+    part, *indices = in_order(part, *indices)
     chip = chip_tokens(part.reshape(groups, rows, block_rows), core)
     old_weight, chip = in_order(old_weight, chip)
     along_z = [chip] + [lax.ppermute(chip, "tensor", shifted(0, k, 0)) for k in range(1, DIM_Z)]
-    columns = grow_columns(old_weight, old_first, old_second, col_source, slabs, slab_width, groups, group_at)
+    columns = grow_columns(indices, old_weight, old_first, old_second, slabs, slab_width, groups)
     columns, *along_z = in_order(columns, *along_z)
     columns = exchange(columns, "tensor")
 

time: 189 us -> 187 us (0.989)
    all_to_all x1, waiting for transfers between devices: 4.75 us -> 2.56 us  [shards(): part = lax.all_to_all(tokens, 'dp', split_axis=1, concat_axis=0, tiled=True)]
  transfers between devices with their start and end apart: 29 -> 29, of which waited for: 16 -> 17; matrix products, arithmetic and copies ran while one was open for 3% -> 3% of each run, Pallas kernels for 10% -> 10%
where the time goes in v4:
time: 187 us; the launch traced here: 186 us
  waiting for transfers between devices  72.3 us (39%)
  starting transfers between devices  58.7 us (31%)
  Pallas kernels  43 us (23%)
  local copies, waits for them, and re-layouts  7.46 us (4%)
  other arithmetic  2.26 us (1%)
    ppermute x6, waiting for transfers between devices, along_x(): lax.ppermute(values, 'tensor', shifted(k, 0, 0))  36.3 us
    all_to_all x3, starting transfers between devices, exchange(): return lax.all_to_all(values, axis, split_axis=0, concat_axis=0, tiled=True)  20.3 us
    all_to_all x3, waiting for transfers between devices, exchange(): return lax.all_to_all(values, axis, split_axis=0, concat_axis=0, tiled=True)  19.8 us
    ppermute x7, waiting for transfers between devices, to_groups(): lax.ppermute(values, 'dp', [(i, i ^ k) for i in range(groups)])  11.8 us
    pallas_call x1, Pallas kernels, grow_columns(): pl.pallas_call(functools.partial(column_kernel, slabs_step, piece), in_sp...  11.3 us
    pallas_call x1, Pallas kernels, backward(): pl.pallas_call(functools.partial(adam_kernel, count, groups), in_specs=[p...  8.74 us
    ppermute x3, starting transfers between devices, shards(): lax.ppermute(chip, 'tensor', shifted(0, k, 0))  8.45 us
    ppermute x7, starting transfers between devices, to_groups(): lax.ppermute(values, 'dp', [(i, i ^ k) for i in range(groups)])  7.82 us
  transfers between devices with their start and end apart: 29, of which 17 were waited for; matrix products, arithmetic and copies ran while one was open for 3% of the time, Pallas kernels for 10%

profile of v4, /device:TPU:1, one launch (start us, length us, event | category | flops | bytes accessed | tf_op | source)
XLA Modules:
  0.0 186.2 jit_solution(1414900420052865020)
XLA Ops:
  0.6 6.5 %all-to-all-start = ((bf16[8,8,1280]{2,0,1:T(8,128)(2,1)}), bf16[8,8,1280]{2,0,1:T(8,128)(2,1)S(1)}, u32[]{:S(2)}, u32[]{:S(2)}) async-start(bf16[8,8,1280]{2,0,1:T(8,128)(2,1)} %bitcast.50), calls=%async_computation | async-start | bytes 327680 | tf_op jit(solution)/shard_map/all_to_all | solution.py:427
  10.3 2.6 %all-to-all-done = bf16[8,8,1280]{2,0,1:T(8,128)(2,1)S(1)} async-done(((bf16[8,8,1280]{2,0,1:T(8,128)(2,1)}), bf16[8,8,1280]{2,0,1:T(8,128)(2,1)S(1)}, u32[]{:S(2)}, u32[]{:S(2)}) %all-to-all-start) | async-done | bytes 163872 | tf_op jit(solution)/shard_map/all_to_all | solution.py:427
  12.8 2.1 %collective-permute-start = (bf16[4,8,1280]{2,1,0:T(8,128)(2,1)S(1)}, bf16[4,8,1280]{2,1,0:T(8,128)(2,1)S(1)}, u32[]{:S(2)}, u32[]{:S(2)}) collective-permute-start(bf16[4,8,1280]{2,1,0:T(8,128)(2,1)S(1)} %constant_dynamic-slice_fusion), channel_id=1, source_target_pairs={{0,1},{1,0},{2,3},{3,2},{4,5},{5,4},{6,7},{7,6},{8,9},{9,8},{10,11... | collective-permute-start | bytes 245768 | tf_op jit(solution)/shard_map/ppermute | solution.py:385
  15.9 5.2 %collective-permute-start.3 = (bf16[1,4,16,1280]{3,2,1,0:T(8,128)(2,1)S(1)}, bf16[1,4,16,1280]{3,2,1,0:T(8,128)(2,1)S(1)}, u32[]{:S(2)}, u32[]{:S(2)}) collective-permute-start(bf16[1,4,16,1280]{3,2,1,0:T(8,128)(2,1)S(1)} %maximum_bitcast_fusion.refs_0_), channel_id=1, source_target_pairs={{0,6},{1,7},{2,0},{3,1},{4,2},{5,3},{6,4},{7,5},{8,14},{9,15},{10,... | collective-permute-start | bytes 491528 | tf_op jit(solution)/shard_map/ppermute | solution.py:432
  22.2 2.1 %collective-permute-start.1 = (bf16[1,4,16,1280]{3,2,1,0:T(8,128)(2,1)S(1)}, bf16[1,4,16,1280]{3,2,1,0:T(8,128)(2,1)S(1)}, u32[]{:S(2)}, u32[]{:S(2)}) collective-permute-start(bf16[1,4,16,1280]{3,2,1,0:T(8,128)(2,1)S(1)} %maximum_bitcast_fusion.refs_0_), channel_id=1, source_target_pairs={{0,2},{1,3},{2,4},{3,5},{4,6},{5,7},{6,0},{7,1},{8,10},{9,11},{10,... | collective-permute-start | bytes 491528 | tf_op jit(solution)/shard_map/ppermute | solution.py:432
  24.3 11.3 %grow_columns.1 = bf16[32,160,128]{2,1,0:T(8,128)(2,1)} custom-call(s32[1,640]{1,0:T(1,128)} %reshape.192.copy_ref, s32[3,256]{1,0:T(4,128)} %fusion.10.own_ref, s32[3,2048]{1,0:T(4,128)} %fusion.9.place_ref, bf16[160,5120]{1,0:T(8,128)(2,1)} %refs_0_, f32[160,5120]{1,0:T(8,128)} %refs_1_.1, f32[160,5120]{1,0:T(8,128)} %refs_2_.1), custom_call_target="tpu_custom_call" | custom-call | flops 1000 | bytes 1000 | tf_op jit(solution)/shard_map/grow_columns/pallas_call | solution.py:122
  36.4 11.1 %all-to-all-start.1 = ((bf16[32,160,128]{2,1,0:T(8,128)(2,1)}), bf16[32,160,128]{2,1,0:T(8,128)(2,1)S(1)}, u32[]{:S(2)}, u32[]{:S(2)}) async-start(bf16[32,160,128]{2,1,0:T(8,128)(2,1)} %grow_columns.1), calls=%async_computation.1 | async-start | bytes 2621440 | tf_op jit(solution)/shard_map/all_to_all | solution.py:416
  47.6 1.7 stack_tokens.2.refs_0_
  49.3 2.6 %collective-permute-start.6 = (bf16[2,4,16,1280]{3,2,1,0:T(8,128)(2,1)}, bf16[2,4,16,1280]{3,2,1,0:T(8,128)(2,1)S(1)}, u32[]{:S(2)}, u32[]{:S(2)}) collective-permute-start(bf16[2,4,16,1280]{3,2,1,0:T(8,128)(2,1)} %stack_tokens.2.refs_0_), channel_id=1, source_target_pairs={{0,24},{1,25},{2,26},{3,27},{4,28},{5,29},{6,30},{7,31},{8,0},{9,1... | collective-permute-start | bytes 983048 | tf_op jit(solution)/shard_map/ppermute | solution.py:438
  54.4 11.5 %collective-permute-done.6.refs_3_ = bf16[2,4,16,1280]{3,2,1,0:T(8,128)(2,1)S(1)} collective-permute-done((bf16[2,4,16,1280]{3,2,1,0:T(8,128)(2,1)}, bf16[2,4,16,1280]{3,2,1,0:T(8,128)(2,1)S(1)}, u32[]{:S(2)}, u32[]{:S(2)}) %collective-permute-start.6) | collective-permute-done | bytes 327712 | tf_op jit(solution)/shard_map/ppermute | solution.py:438
  65.9 5.2 %collective-permute-done.5.refs_2_ = bf16[2,4,16,1280]{3,2,1,0:T(8,128)(2,1)S(1)} collective-permute-done((bf16[2,4,16,1280]{3,2,1,0:T(8,128)(2,1)}, bf16[2,4,16,1280]{3,2,1,0:T(8,128)(2,1)S(1)}, u32[]{:S(2)}, u32[]{:S(2)}) %collective-permute-start.5) | collective-permute-done | bytes 327712 | tf_op jit(solution)/shard_map/ppermute | solution.py:438
  71.2 9.1 %collective-permute-done.4.refs_1_ = bf16[2,4,16,1280]{3,2,1,0:T(8,128)(2,1)S(1)} collective-permute-done((bf16[2,4,16,1280]{3,2,1,0:T(8,128)(2,1)}, bf16[2,4,16,1280]{3,2,1,0:T(8,128)(2,1)S(1)}, u32[]{:S(2)}, u32[]{:S(2)}) %collective-permute-start.4) | collective-permute-done | bytes 327712 | tf_op jit(solution)/shard_map/ppermute | solution.py:438
  80.3 7.6 %grow_rows.1 = bf16[10240,128]{1,0:T(8,128)(2,1)} custom-call(s32[5120]{0:T(1024)S(1)} %copy-done.1, bf16[5120,128]{1,0:T(8,128)(2,1)S(1)} %bitcast.47), custom_call_target="tpu_custom_call" | custom-call | flops 1000 | bytes 1000 | tf_op jit(solution)/shard_map/grow_rows/pallas_call | solution.py:162
  87.9 5.5 %all-to-all-start.2 = ((bf16[8,1280,128]{2,1,0:T(8,128)(2,1)}), bf16[8,1280,128]{2,1,0:T(8,128)(2,1)S(1)}, u32[]{:S(2)}, u32[]{:S(2)}) async-start(bf16[8,1280,128]{2,1,0:T(8,128)(2,1)} %bitcast.14), calls=%async_computation.2 | async-start | bytes 5242880 | tf_op jit(solution)/shard_map/all_to_all | solution.py:416
  93.4 1.7 stack_tokens.3.refs_4_
  98.2 5.6 %collective-permute-done.9.refs_7_ = bf16[2,4,16,1280]{3,2,1,0:T(8,128)(2,1)S(1)} collective-permute-done((bf16[2,4,16,1280]{3,2,1,0:T(8,128)(2,1)}, bf16[2,4,16,1280]{3,2,1,0:T(8,128)(2,1)S(1)}, u32[]{:S(2)}, u32[]{:S(2)}) %collective-permute-start.9) | collective-permute-done | bytes 327712 | tf_op jit(solution)/shard_map/ppermute | solution.py:438
  103.7 3.1 %collective-permute-start.17 = (bf16[2,4,16,1280]{3,2,1,0:T(8,128)(2,1)S(1)}, bf16[2,4,16,1280]{3,2,1,0:T(8,128)(2,1)S(1)}, u32[]{:S(2)}, u32[]{:S(2)}) collective-permute-start(bf16[2,4,16,1280]{3,2,1,0:T(8,128)(2,1)S(1)} %collective-permute-done.9.refs_7_), channel_id=1, source_target_pairs={{0,1},{1,0},{2,3},{3,2},{4,5},{5,4},{6,7},{7,6},{8,9},{9,8},{10,11... | collective-permute-start | bytes 983048 | tf_op jit(solution)/shard_map/ppermute | solution.py:446
  106.9 2.4 %collective-permute-start.16 = (bf16[2,4,16,1280]{3,2,1,0:T(8,128)(2,1)S(1)}, bf16[2,4,16,1280]{3,2,1,0:T(8,128)(2,1)S(1)}, u32[]{:S(2)}, u32[]{:S(2)}) collective-permute-start(bf16[2,4,16,1280]{3,2,1,0:T(8,128)(2,1)S(1)} %collective-permute-done.8.refs_6_), channel_id=1, source_target_pairs={{0,1},{1,0},{2,3},{3,2},{4,5},{5,4},{6,7},{7,6},{8,9},{9,8},{10,11... | collective-permute-start | bytes 983048 | tf_op jit(solution)/shard_map/ppermute | solution.py:446
  109.3 4.9 %collective-permute-done.7.refs_5_ = bf16[2,4,16,1280]{3,2,1,0:T(8,128)(2,1)} collective-permute-done((bf16[2,4,16,1280]{3,2,1,0:T(8,128)(2,1)}, bf16[2,4,16,1280]{3,2,1,0:T(8,128)(2,1)}, u32[]{:S(2)}, u32[]{:S(2)}) %collective-permute-start.7) | collective-permute-done | bytes 327712 | tf_op jit(solution)/shard_map/ppermute | solution.py:438
  118.5 6.7 %all-to-all-done.2.refs_16_.blocks_ref = bf16[8,1280,128]{2,1,0:T(8,128)(2,1)S(1)} async-done(((bf16[8,1280,128]{2,1,0:T(8,128)(2,1)}), bf16[8,1280,128]{2,1,0:T(8,128)(2,1)S(1)}, u32[]{:S(2)}, u32[]{:S(2)}) %all-to-all-start.2) | async-done | bytes 2621472 | tf_op jit(solution)/shard_map/all_to_all | solution.py:416
  125.1 1.5 copy-done.2
  126.6 7.4 %forward_terms.1 = (bf16[320,1280]{1,0:T(8,128)(2,1)}, bf16[8,320,256]{2,1,0:T(8,128)(2,1)}) custom-call(s32[2]{0:T(128)} %pad_add_fusion.place_ref, bf16[2,4,16,1280]{3,2,1,0:T(8,128)(2,1)} %stack_tokens.2.refs_0_, bf16[2,4,16,1280]{3,2,1,0:T(8,128)(2,1)} %copy-done.6, bf16[2,4,16,1280]{3,2,1,0:T(8,128)(2,1)} %copy-done.5, ...), custom_call_target="tpu_custom_call" | custom-call | flops 1000 | bytes 1000 | tf_op jit(solution)/shard_map/forward_terms/pallas_call | solution.py:243
  134.0 3.7 %all-to-all-start.3 = ((bf16[8,320,256]{2,1,0:T(8,128)(2,1)}), bf16[8,320,256]{2,1,0:T(8,128)(2,1)S(1)}, u32[]{:S(2)}, u32[]{:S(2)}) async-start(bf16[8,320,256]{2,1,0:T(8,128)(2,1)} %get-tuple-element.86), calls=%async_computation.3 | async-start | bytes 2621440 | tf_op jit(solution)/shard_map/all_to_all | solution.py:416
  137.7 4.6 %grown_block_2.1 = (bf16[320,1280]{1,0:T(8,128)(2,1)}, bf16[320,1280]{1,0:T(8,128)(2,1)}) custom-call(bf16[8,1280,128]{2,1,0:T(8,128)(2,1)} %copy-done.2), custom_call_target="tpu_custom_call" | custom-call | flops 1000 | bytes 1000 | tf_op jit(solution)/shard_map/grown_block_2/pallas_call | solution.py:196
  142.3 13.2 %all-to-all-done.3 = bf16[8,320,256]{2,1,0:T(8,128)(2,1)S(1)} async-done(((bf16[8,320,256]{2,1,0:T(8,128)(2,1)}), bf16[8,320,256]{2,1,0:T(8,128)(2,1)S(1)}, u32[]{:S(2)}, u32[]{:S(2)}) %all-to-all-start.3) | async-done | bytes 1310752 | tf_op jit(solution)/shard_map/all_to_all | solution.py:416
  156.1 2.5 %collective-permute-start.24 = (bf16[320,256]{1,0:T(8,128)(2,1)S(1)}, bf16[320,256]{1,0:T(8,128)(2,1)S(1)}, u32[]{:S(2)}, u32[]{:S(2)}) collective-permute-start(bf16[320,256]{1,0:T(8,128)(2,1)S(1)} %fusion.6.refs_16_), channel_id=1, source_target_pairs={{0,224},{32,192},{64,160},{96,128},{128,96},{160,64},{192,32},{224... | collective-permute-start | bytes 491528 | tf_op jit(solution)/shard_map/ppermute | solution.py:392
  158.8 2.4 %collective-permute-start.22 = (bf16[320,256]{1,0:T(8,128)(2,1)S(1)}, bf16[320,256]{1,0:T(8,128)(2,1)S(1)}, u32[]{:S(2)}, u32[]{:S(2)}) collective-permute-start(bf16[320,256]{1,0:T(8,128)(2,1)S(1)} %fusion.6.refs_16_), channel_id=1, source_target_pairs={{0,160},{32,128},{64,224},{96,192},{128,32},{160,0},{192,96},{224,... | collective-permute-start | bytes 491528 | tf_op jit(solution)/shard_map/ppermute | solution.py:392
  163.9 2.9 %collective-permute-done.23.refs_22_ = bf16[320,256]{1,0:T(8,128)(2,1)S(1)} collective-permute-done((bf16[320,256]{1,0:T(8,128)(2,1)S(1)}, bf16[320,256]{1,0:T(8,128)(2,1)S(1)}, u32[]{:S(2)}, u32[]{:S(2)}) %collective-permute-start.23) | collective-permute-done | bytes 163872 | tf_op jit(solution)/shard_map/ppermute | solution.py:392
  168.9 3.9 %collective-permute-done.21.refs_20_ = bf16[320,256]{1,0:T(8,128)(2,1)S(1)} collective-permute-done((bf16[320,256]{1,0:T(8,128)(2,1)S(1)}, bf16[320,256]{1,0:T(8,128)(2,1)S(1)}, u32[]{:S(2)}, u32[]{:S(2)}) %collective-permute-start.21) | collective-permute-done | bytes 163872 | tf_op jit(solution)/shard_map/ppermute | solution.py:392
  172.8 1.6 collective-permute-done.20.refs_19_
  174.3 2.3 %collective-permute-done.18.refs_17_ = bf16[320,256]{1,0:T(8,128)(2,1)S(1)} collective-permute-done((bf16[320,256]{1,0:T(8,128)(2,1)S(1)}, bf16[320,256]{1,0:T(8,128)(2,1)S(1)}, u32[]{:S(2)}, u32[]{:S(2)}) %collective-permute-start.18) | collective-permute-done | bytes 163872 | tf_op jit(solution)/shard_map/ppermute | solution.py:392
  177.3 8.7 %gradient_adam.1 = (bf16[320,1280]{1,0:T(8,128)(2,1)}, f32[320,1280]{1,0:T(8,128)}, f32[320,1280]{1,0:T(8,128)}) custom-call(s32[2]{0:T(128)} %pad_add_fusion.place_ref, bf16[2,4,16,1280]{3,2,1,0:T(8,128)(2,1)} %stack_tokens.2.refs_0_, bf16[2,4,16,1280]{3,2,1,0:T(8,128)(2,1)} %copy-done.6, bf16[2,4,16,1280]{3,2,1,0:T(8,128)(2,1)} %copy-done.5, ...), custom_call_target="tpu_custom_call" | custom-call | flops 1000 | bytes 1000 | tf_op jit(solution)/shard_map/gradient_adam/pallas_call | solution.py:326
  (115 shorter events, 22.0 us)
Async XLA Ops:
  0.6 155.0 %copy-start = (bf16[256,320]{0,1:T(8,128)(2,1)S(1)}, bf16[256,320]{0,1:T(8,128)(2,1)}, u32[]{:S(2)}) copy-start(bf16[256,320]{0,1:T(8,128)(2,1)} %param.10) | copy-start | bytes 491524
  0.6 12.2 %all-to-all-start = ((bf16[8,8,1280]{2,0,1:T(8,128)(2,1)}), bf16[8,8,1280]{2,0,1:T(8,128)(2,1)S(1)}, u32[]{:S(2)}, u32[]{:S(2)}) async-start(bf16[8,8,1280]{2,0,1:T(8,128)(2,1)} %bitcast.50), calls=%async_computation | async-start | bytes 327680 | tf_op jit(solution)/shard_map/all_to_all | solution.py:427
  12.8 3.0 %collective-permute-start = (bf16[4,8,1280]{2,1,0:T(8,128)(2,1)S(1)}, bf16[4,8,1280]{2,1,0:T(8,128)(2,1)S(1)}, u32[]{:S(2)}, u32[]{:S(2)}) collective-permute-start(bf16[4,8,1280]{2,1,0:T(8,128)(2,1)S(1)} %constant_dynamic-slice_fusion), channel_id=1, source_target_pairs={{0,1},{1,0},{2,3},{3,2},{4,5},{5,4},{6,7},{7,6},{8,9},{9,8},{10,11... | collective-permute-start | bytes 245768 | tf_op jit(solution)/shard_map/ppermute | solution.py:385
  15.9 19.8 %collective-permute-start.3 = (bf16[1,4,16,1280]{3,2,1,0:T(8,128)(2,1)S(1)}, bf16[1,4,16,1280]{3,2,1,0:T(8,128)(2,1)S(1)}, u32[]{:S(2)}, u32[]{:S(2)}) collective-permute-start(bf16[1,4,16,1280]{3,2,1,0:T(8,128)(2,1)S(1)} %maximum_bitcast_fusion.refs_0_), channel_id=1, source_target_pairs={{0,6},{1,7},{2,0},{3,1},{4,2},{5,3},{6,4},{7,5},{8,14},{9,15},{10,... | collective-permute-start | bytes 491528 | tf_op jit(solution)/shard_map/ppermute | solution.py:432
  21.1 14.6 %collective-permute-start.2 = (bf16[1,4,16,1280]{3,2,1,0:T(8,128)(2,1)S(1)}, bf16[1,4,16,1280]{3,2,1,0:T(8,128)(2,1)S(1)}, u32[]{:S(2)}, u32[]{:S(2)}) collective-permute-start(bf16[1,4,16,1280]{3,2,1,0:T(8,128)(2,1)S(1)} %maximum_bitcast_fusion.refs_0_), channel_id=1, source_target_pairs={{0,4},{1,5},{2,6},{3,7},{4,0},{5,1},{6,2},{7,3},{8,12},{9,13},{10,... | collective-permute-start | bytes 491528 | tf_op jit(solution)/shard_map/ppermute | solution.py:432
  22.2 14.1 %collective-permute-start.1 = (bf16[1,4,16,1280]{3,2,1,0:T(8,128)(2,1)S(1)}, bf16[1,4,16,1280]{3,2,1,0:T(8,128)(2,1)S(1)}, u32[]{:S(2)}, u32[]{:S(2)}) collective-permute-start(bf16[1,4,16,1280]{3,2,1,0:T(8,128)(2,1)S(1)} %maximum_bitcast_fusion.refs_0_), channel_id=1, source_target_pairs={{0,2},{1,3},{2,4},{3,5},{4,6},{5,7},{6,0},{7,1},{8,10},{9,11},{10,... | collective-permute-start | bytes 491528 | tf_op jit(solution)/shard_map/ppermute | solution.py:432
  35.6 44.7 %copy-start.1 = (s32[5120]{0:T(1024)S(1)}, s32[5120]{0:T(1024)}, u32[]{:S(2)}) copy-start(s32[5120]{0:T(1024)} %index_ref.1) | copy-start | bytes 61444
  36.4 43.9 %all-to-all-start.1 = ((bf16[32,160,128]{2,1,0:T(8,128)(2,1)}), bf16[32,160,128]{2,1,0:T(8,128)(2,1)S(1)}, u32[]{:S(2)}, u32[]{:S(2)}) async-start(bf16[32,160,128]{2,1,0:T(8,128)(2,1)} %grow_columns.1), calls=%async_computation.1 | async-start | bytes 2621440 | tf_op jit(solution)/shard_map/all_to_all | solution.py:416
  49.3 16.6 %collective-permute-start.6 = (bf16[2,4,16,1280]{3,2,1,0:T(8,128)(2,1)}, bf16[2,4,16,1280]{3,2,1,0:T(8,128)(2,1)S(1)}, u32[]{:S(2)}, u32[]{:S(2)}) collective-permute-start(bf16[2,4,16,1280]{3,2,1,0:T(8,128)(2,1)} %stack_tokens.2.refs_0_), channel_id=1, source_target_pairs={{0,24},{1,25},{2,26},{3,27},{4,28},{5,29},{6,30},{7,31},{8,0},{9,1... | collective-permute-start | bytes 983048 | tf_op jit(solution)/shard_map/ppermute | solution.py:438
  52.0 19.2 %collective-permute-start.5 = (bf16[2,4,16,1280]{3,2,1,0:T(8,128)(2,1)}, bf16[2,4,16,1280]{3,2,1,0:T(8,128)(2,1)S(1)}, u32[]{:S(2)}, u32[]{:S(2)}) collective-permute-start(bf16[2,4,16,1280]{3,2,1,0:T(8,128)(2,1)} %stack_tokens.2.refs_0_), channel_id=1, source_target_pairs={{0,16},{1,17},{2,18},{3,19},{4,20},{5,21},{6,22},{7,23},{8,24},{9,... | collective-permute-start | bytes 983048 | tf_op jit(solution)/shard_map/ppermute | solution.py:438
  52.5 27.8 %collective-permute-start.4 = (bf16[2,4,16,1280]{3,2,1,0:T(8,128)(2,1)}, bf16[2,4,16,1280]{3,2,1,0:T(8,128)(2,1)S(1)}, u32[]{:S(2)}, u32[]{:S(2)}) collective-permute-start(bf16[2,4,16,1280]{3,2,1,0:T(8,128)(2,1)} %stack_tokens.2.refs_0_), channel_id=1, source_target_pairs={{0,8},{1,9},{2,10},{3,11},{4,12},{5,13},{6,14},{7,15},{8,16},{9,17... | collective-permute-start | bytes 983048 | tf_op jit(solution)/shard_map/ppermute | solution.py:438
  65.9 49.4 %copy-start.4 = (bf16[2,4,16,1280]{3,2,1,0:T(8,128)(2,1)}, bf16[2,4,16,1280]{3,2,1,0:T(8,128)(2,1)S(1)}, u32[]{:S(2)}) copy-start(bf16[2,4,16,1280]{3,2,1,0:T(8,128)(2,1)S(1)} %collective-permute-done.6.refs_3_) | copy-start | bytes 983044
  87.9 37.2 %all-to-all-start.2 = ((bf16[8,1280,128]{2,1,0:T(8,128)(2,1)}), bf16[8,1280,128]{2,1,0:T(8,128)(2,1)S(1)}, u32[]{:S(2)}, u32[]{:S(2)}) async-start(bf16[8,1280,128]{2,1,0:T(8,128)(2,1)} %bitcast.14), calls=%async_computation.2 | async-start | bytes 5242880 | tf_op jit(solution)/shard_map/all_to_all | solution.py:416
  95.1 8.6 %collective-permute-start.9 = (bf16[2,4,16,1280]{3,2,1,0:T(8,128)(2,1)}, bf16[2,4,16,1280]{3,2,1,0:T(8,128)(2,1)S(1)}, u32[]{:S(2)}, u32[]{:S(2)}) collective-permute-start(bf16[2,4,16,1280]{3,2,1,0:T(8,128)(2,1)} %stack_tokens.3.refs_4_), channel_id=1, source_target_pairs={{0,24},{1,25},{2,26},{3,27},{4,28},{5,29},{6,30},{7,31},{8,0},{9,1... | collective-permute-start | bytes 983048 | tf_op jit(solution)/shard_map/ppermute | solution.py:438
  95.7 11.1 %collective-permute-start.8 = (bf16[2,4,16,1280]{3,2,1,0:T(8,128)(2,1)}, bf16[2,4,16,1280]{3,2,1,0:T(8,128)(2,1)S(1)}, u32[]{:S(2)}, u32[]{:S(2)}) collective-permute-start(bf16[2,4,16,1280]{3,2,1,0:T(8,128)(2,1)} %stack_tokens.3.refs_4_), channel_id=1, source_target_pairs={{0,16},{1,17},{2,18},{3,19},{4,20},{5,21},{6,22},{7,23},{8,24},{9,... | collective-permute-start | bytes 983048 | tf_op jit(solution)/shard_map/ppermute | solution.py:438
  97.0 17.2 %collective-permute-start.7 = (bf16[2,4,16,1280]{3,2,1,0:T(8,128)(2,1)}, bf16[2,4,16,1280]{3,2,1,0:T(8,128)(2,1)}, u32[]{:S(2)}, u32[]{:S(2)}) collective-permute-start(bf16[2,4,16,1280]{3,2,1,0:T(8,128)(2,1)} %stack_tokens.3.refs_4_), channel_id=1, source_target_pairs={{0,8},{1,9},{2,10},{3,11},{4,12},{5,13},{6,14},{7,15},{8,16},{9,17... | collective-permute-start | bytes 983048 | tf_op jit(solution)/shard_map/ppermute | solution.py:438
  97.2 17.6 %collective-permute-start.14 = (bf16[2,4,16,1280]{3,2,1,0:T(8,128)(2,1)}, bf16[2,4,16,1280]{3,2,1,0:T(8,128)(2,1)S(1)}, u32[]{:S(2)}, u32[]{:S(2)}) collective-permute-start(bf16[2,4,16,1280]{3,2,1,0:T(8,128)(2,1)} %stack_tokens.3.refs_4_), channel_id=1, source_target_pairs={{0,1},{1,0},{2,3},{3,2},{4,5},{5,4},{6,7},{7,6},{8,9},{9,8},{10,11... | collective-permute-start | bytes 983048 | tf_op jit(solution)/shard_map/ppermute | solution.py:446
  103.7 11.5 %collective-permute-start.17 = (bf16[2,4,16,1280]{3,2,1,0:T(8,128)(2,1)S(1)}, bf16[2,4,16,1280]{3,2,1,0:T(8,128)(2,1)S(1)}, u32[]{:S(2)}, u32[]{:S(2)}) collective-permute-start(bf16[2,4,16,1280]{3,2,1,0:T(8,128)(2,1)S(1)} %collective-permute-done.9.refs_7_), channel_id=1, source_target_pairs={{0,1},{1,0},{2,3},{3,2},{4,5},{5,4},{6,7},{7,6},{8,9},{9,8},{10,11... | collective-permute-start | bytes 983048 | tf_op jit(solution)/shard_map/ppermute | solution.py:446
  106.9 8.5 %collective-permute-start.16 = (bf16[2,4,16,1280]{3,2,1,0:T(8,128)(2,1)S(1)}, bf16[2,4,16,1280]{3,2,1,0:T(8,128)(2,1)S(1)}, u32[]{:S(2)}, u32[]{:S(2)}) collective-permute-start(bf16[2,4,16,1280]{3,2,1,0:T(8,128)(2,1)S(1)} %collective-permute-done.8.refs_6_), channel_id=1, source_target_pairs={{0,1},{1,0},{2,3},{3,2},{4,5},{5,4},{6,7},{7,6},{8,9},{9,8},{10,11... | collective-permute-start | bytes 983048 | tf_op jit(solution)/shard_map/ppermute | solution.py:446
  114.2 3.4 %collective-permute-start.15 = (bf16[2,4,16,1280]{3,2,1,0:T(8,128)(2,1)}, bf16[2,4,16,1280]{3,2,1,0:T(8,128)(2,1)}, u32[]{:S(2)}, u32[]{:S(2)}) collective-permute-start(bf16[2,4,16,1280]{3,2,1,0:T(8,128)(2,1)} %collective-permute-done.7.refs_5_), channel_id=1, source_target_pairs={{0,1},{1,0},{2,3},{3,2},{4,5},{5,4},{6,7},{7,6},{8,9},{9,8},{10,11... | collective-permute-start | bytes 983048 | tf_op jit(solution)/shard_map/ppermute | solution.py:446
  114.7 2.9 %collective-permute-start.10 = (bf16[2,4,16,1280]{3,2,1,0:T(8,128)(2,1)S(1)}, bf16[2,4,16,1280]{3,2,1,0:T(8,128)(2,1)}, u32[]{:S(2)}, u32[]{:S(2)}) collective-permute-start(bf16[2,4,16,1280]{3,2,1,0:T(8,128)(2,1)S(1)} %copy-done.3), channel_id=1, source_target_pairs={{0,1},{1,0},{2,3},{3,2},{4,5},{5,4},{6,7},{7,6},{8,9},{9,8},{10,11... | collective-permute-start | bytes 983048 | tf_op jit(solution)/shard_map/ppermute | solution.py:446
  114.7 2.9 %collective-permute-start.11 = (bf16[2,4,16,1280]{3,2,1,0:T(8,128)(2,1)}, bf16[2,4,16,1280]{3,2,1,0:T(8,128)(2,1)}, u32[]{:S(2)}, u32[]{:S(2)}) collective-permute-start(bf16[2,4,16,1280]{3,2,1,0:T(8,128)(2,1)} %copy-done.6), channel_id=1, source_target_pairs={{0,1},{1,0},{2,3},{3,2},{4,5},{5,4},{6,7},{7,6},{8,9},{9,8},{10,11... | collective-permute-start | bytes 983048 | tf_op jit(solution)/shard_map/ppermute | solution.py:446
  115.2 2.5 %collective-permute-start.12 = (bf16[2,4,16,1280]{3,2,1,0:T(8,128)(2,1)}, bf16[2,4,16,1280]{3,2,1,0:T(8,128)(2,1)}, u32[]{:S(2)}, u32[]{:S(2)}) collective-permute-start(bf16[2,4,16,1280]{3,2,1,0:T(8,128)(2,1)} %copy-done.5), channel_id=1, source_target_pairs={{0,1},{1,0},{2,3},{3,2},{4,5},{5,4},{6,7},{7,6},{8,9},{9,8},{10,11... | collective-permute-start | bytes 983048 | tf_op jit(solution)/shard_map/ppermute | solution.py:446
  116.7 1.8 collective-permute-start.13
  134.0 21.5 %all-to-all-start.3 = ((bf16[8,320,256]{2,1,0:T(8,128)(2,1)}), bf16[8,320,256]{2,1,0:T(8,128)(2,1)S(1)}, u32[]{:S(2)}, u32[]{:S(2)}) async-start(bf16[8,320,256]{2,1,0:T(8,128)(2,1)} %get-tuple-element.86), calls=%async_computation.3 | async-start | bytes 2621440 | tf_op jit(solution)/shard_map/all_to_all | solution.py:416
  156.1 7.1 %collective-permute-start.24 = (bf16[320,256]{1,0:T(8,128)(2,1)S(1)}, bf16[320,256]{1,0:T(8,128)(2,1)S(1)}, u32[]{:S(2)}, u32[]{:S(2)}) collective-permute-start(bf16[320,256]{1,0:T(8,128)(2,1)S(1)} %fusion.6.refs_16_), channel_id=1, source_target_pairs={{0,224},{32,192},{64,160},{96,128},{128,96},{160,64},{192,32},{224... | collective-permute-start | bytes 491528 | tf_op jit(solution)/shard_map/ppermute | solution.py:392
  158.6 8.3 %collective-permute-start.23 = (bf16[320,256]{1,0:T(8,128)(2,1)S(1)}, bf16[320,256]{1,0:T(8,128)(2,1)S(1)}, u32[]{:S(2)}, u32[]{:S(2)}) collective-permute-start(bf16[320,256]{1,0:T(8,128)(2,1)S(1)} %fusion.6.refs_16_), channel_id=1, source_target_pairs={{0,192},{32,224},{64,128},{96,160},{128,64},{160,96},{192,0},{224,... | collective-permute-start | bytes 491528 | tf_op jit(solution)/shard_map/ppermute | solution.py:392
  158.8 10.1 %collective-permute-start.22 = (bf16[320,256]{1,0:T(8,128)(2,1)S(1)}, bf16[320,256]{1,0:T(8,128)(2,1)S(1)}, u32[]{:S(2)}, u32[]{:S(2)}) collective-permute-start(bf16[320,256]{1,0:T(8,128)(2,1)S(1)} %fusion.6.refs_16_), channel_id=1, source_target_pairs={{0,160},{32,128},{64,224},{96,192},{128,32},{160,0},{192,96},{224,... | collective-permute-start | bytes 491528 | tf_op jit(solution)/shard_map/ppermute | solution.py:392
  161.2 11.5 %collective-permute-start.21 = (bf16[320,256]{1,0:T(8,128)(2,1)S(1)}, bf16[320,256]{1,0:T(8,128)(2,1)S(1)}, u32[]{:S(2)}, u32[]{:S(2)}) collective-permute-start(bf16[320,256]{1,0:T(8,128)(2,1)S(1)} %fusion.6.refs_16_), channel_id=1, source_target_pairs={{0,128},{32,160},{64,192},{96,224},{128,0},{160,32},{192,64},{224,... | collective-permute-start | bytes 491528 | tf_op jit(solution)/shard_map/ppermute | solution.py:392
  161.5 12.8 %collective-permute-start.20 = (bf16[320,256]{1,0:T(8,128)(2,1)S(1)}, bf16[320,256]{1,0:T(8,128)(2,1)S(1)}, u32[]{:S(2)}, u32[]{:S(2)}) collective-permute-start(bf16[320,256]{1,0:T(8,128)(2,1)S(1)} %fusion.6.refs_16_), channel_id=1, source_target_pairs={{0,96},{32,64},{64,32},{96,0},{128,224},{160,192},{192,160},{224,1... | collective-permute-start | bytes 491528 | tf_op jit(solution)/shard_map/ppermute | solution.py:392
  163.2 11.2 %collective-permute-start.19 = (bf16[320,256]{1,0:T(8,128)(2,1)S(1)}, bf16[320,256]{1,0:T(8,128)(2,1)S(1)}, u32[]{:S(2)}, u32[]{:S(2)}) collective-permute-start(bf16[320,256]{1,0:T(8,128)(2,1)S(1)} %fusion.6.refs_16_), channel_id=1, source_target_pairs={{0,64},{32,96},{64,0},{96,32},{128,192},{160,224},{192,128},{224,1... | collective-permute-start | bytes 491528 | tf_op jit(solution)/shard_map/ppermute | solution.py:392
  166.8 9.8 %collective-permute-start.18 = (bf16[320,256]{1,0:T(8,128)(2,1)S(1)}, bf16[320,256]{1,0:T(8,128)(2,1)S(1)}, u32[]{:S(2)}, u32[]{:S(2)}) collective-permute-start(bf16[320,256]{1,0:T(8,128)(2,1)S(1)} %fusion.6.refs_16_), channel_id=1, source_target_pairs={{0,32},{32,0},{64,96},{96,64},{128,160},{160,128},{192,224},{224,1... | collective-permute-start | bytes 491528 | tf_op jit(solution)/shard_map/ppermute | solution.py:392
  (23 other events, 203.3 us)
